TPU v7x, 32 devices: a whole 2x2x4 slice. The times are simulated.
32 devices in a mesh: batch: 4 (over y, x), seq: 8 (over z, core).
Axes of the slice: x: 2, y: 2, z: 4, core: 2. Of those that a mesh axis runs over, the one named last changes fastest.
Arguments:
- tokens: bfloat16 [4, 2048, 2048], P('batch', 'seq'), may hold values from -6 to 6
- segments: int32 [4, 2048], P('batch', 'seq'), may hold values from 0 to 10, as said below
- cotangent: bfloat16 [4, 2048, 2048], P('batch', 'seq'), may hold values from -6 to 6
- norm_gain: bfloat16 [2048], P(('batch', 'seq')), may hold values from 0.099609375 to 1.8984375
- gating_weight: bfloat16 [2048, 3072], P(('batch', 'seq')), may hold values from -0.125 to 0.125
- input_weight: bfloat16 [2048, 3072], P(('batch', 'seq')), may hold values from -0.125 to 0.125
- state_weight: bfloat16 [2048, 512], P(('batch', 'seq')), may hold values from -0.125 to 0.125
- step_weight: bfloat16 [2048, 48], P(('batch', 'seq')), may hold values from -0.125 to 0.125
- conv_weight: bfloat16 [4, 3584], P(None, ('batch', 'seq')), may hold values from -3 to 3
- conv_bias: bfloat16 [3584], P(('batch', 'seq')), may hold values from -3 to 3
- step_bias: bfloat16 [48], replicated, may hold values from -7 to -2.296875
- decay_log: bfloat16 [48], replicated, may hold values from 0 to 2.765625
- skip_gain: bfloat16 [48], replicated, may hold values from 0.5 to 1.5
- ssm_gain: bfloat16 [3072], P(('batch', 'seq')), may hold values from 0.099609375 to 1.8984375
- out_weight: bfloat16 [3072, 2048], P(('batch', 'seq')), may hold values from -0.109375 to 0.109375
- query_weight: bfloat16 [2048, 1024], P(('batch', 'seq')), may hold values from -0.125 to 0.125
- keyval_weight: bfloat16 [2048, 512], P(('batch', 'seq')), may hold values from -0.125 to 0.125
- context_weight: bfloat16 [1024, 2048], P(('batch', 'seq')), may hold values from -3 to 3
- mlp_gain: bfloat16 [2048], P(('batch', 'seq')), may hold values from 0.099609375 to 1.8984375
- gate_weight: bfloat16 [2048, 4096], P(('batch', 'seq')), may hold values from -0.125 to 0.125
- up_weight: bfloat16 [2048, 4096], P(('batch', 'seq')), may hold values from -0.125 to 0.125
- down_weight: bfloat16 [4096, 2048], P(('batch', 'seq')), may hold values from -0.09375 to 0.09375
Outputs:
- layer_out: bfloat16 [4, 2048, 2048], P('batch', 'seq')
- grad_tokens: bfloat16 [4, 2048, 2048], P('batch', 'seq')
- grad_norm_gain: float32 [2048], P(('batch', 'seq'))
- grad_gating_weight: float32 [2048, 3072], P(('batch', 'seq'))
- grad_input_weight: float32 [2048, 3072], P(('batch', 'seq'))
- grad_state_weight: float32 [2048, 512], P(('batch', 'seq'))
- grad_step_weight: float32 [2048, 48], P(('batch', 'seq'))
- grad_conv_weight: float32 [4, 3584], P(None, ('batch', 'seq'))
- grad_conv_bias: float32 [3584], P(('batch', 'seq'))
- grad_step_bias: float32 [48], replicated
- grad_decay_log: float32 [48], replicated
- grad_skip_gain: float32 [48], replicated
- grad_ssm_gain: float32 [3072], P(('batch', 'seq'))
- grad_out_weight: float32 [3072, 2048], P(('batch', 'seq'))
- grad_query_weight: float32 [2048, 1024], P(('batch', 'seq'))
- grad_keyval_weight: float32 [2048, 512], P(('batch', 'seq'))
- grad_context_weight: float32 [1024, 2048], P(('batch', 'seq'))
- grad_mlp_gain: float32 [2048], P(('batch', 'seq'))
- grad_gate_weight: float32 [2048, 4096], P(('batch', 'seq'))
- grad_up_weight: float32 [2048, 4096], P(('batch', 'seq'))
- grad_down_weight: float32 [4096, 2048], P(('batch', 'seq'))
Inputs may be any that keep to these rules, and one draw needn't show every extreme that they name: `segments`: along each sequence the segment numbers start at 0 and rise by one where a new document begins; every document has at most 2000 tokens, and every one but the last of its sequence at least 200. In one sequence every document but the last has exactly 200 tokens.
All inputs are finite; a program needn't handle non-finite values.
Results may differ from a plain program's by a relative error of at most 0.03.
Values may be sent and summed in bfloat16 or wider, within the bound.
No kernel may reach another device: no remote copies, remote signals or barrier semaphores. Data moves between devices by JAX's collectives and lax.ppermute only.
A program may use at most 448 MiB of HBM per device.

v0:
```python
import math

import jax
import jax.numpy as jnp
from jax import lax
from jax.sharding import PartitionSpec as P

HEADS = 48
SSM_HEAD = 64
STATE = 256
CONV = 4
QHEADS = 8
KVHEADS = 2
ATT_HEAD = 128


HIGH = lax.Precision.HIGHEST
EPSILON = 1e-05
ROPE_BASE = 10000.0
NEG_BIG = -1e30


def passed_along(block, axis, distance):
    devices = range(lax.axis_size(axis))
    route = [(i - distance, i) for i in devices if i - distance in devices]
    return lax.ppermute(block, axis, route)


def carried_in(x, axis, combine, identity, reverse):
    length, mine = (lax.axis_size(axis), lax.axis_index(axis))
    everything = jax.tree.map(
        lambda part, kind: lax.all_gather(part.astype(kind), axis), x, (jnp.bfloat16, jnp.bfloat16)
    )
    start = jax.tree.map(
        lambda part, zero: jnp.broadcast_to(jnp.asarray(zero, part.dtype), part.shape), x, identity
    )

    def lap(k, before):
        at = length - 1 - k if reverse else k
        reached = at > mine if reverse else at < mine
        new = combine(
            before, jax.tree.map(lambda part, own: part[at].astype(own.dtype), everything, x)
        )
        return jax.tree.map(lambda a, b: jnp.where(reached, a, b), new, before)

    return lax.fori_loop(0, length, lap, start)


def rms_scale(values):
    return lax.rsqrt(jnp.mean(values * values, axis=-1, keepdims=True) + EPSILON)


def matmul(left, right):
    return jnp.dot(left, right, preferred_element_type=jnp.float32)


def matmul_high(left, right):
    return jnp.dot(left, right, precision=HIGH, preferred_element_type=jnp.float32)


def inner_rows(left, right):
    return lax.dot_general(
        left, right, (((0,), (0,)), ((), ())), preferred_element_type=jnp.float32
    )


def inner_high(left, right):
    return lax.dot_general(
        left, right, (((0,), (0,)), ((), ())), precision=HIGH, preferred_element_type=jnp.float32
    )


def times_trans(left, right):
    return lax.dot_general(
        left, right, (((1,), (1,)), ((), ())), preferred_element_type=jnp.float32
    )


def times_high(left, right):
    return lax.dot_general(
        left, right, (((1,), (1,)), ((), ())), precision=HIGH, preferred_element_type=jnp.float32
    )


def silu_slope(values):
    sigmoid_val = jax.nn.sigmoid(values)
    return sigmoid_val * (1.0 + values * (1.0 - sigmoid_val))


def rotate(values, places, direction):
    full_width = values.shape[-1]
    half_width = full_width // 2
    frequency = jnp.exp(
        jnp.arange(half_width, dtype=jnp.float32) * (-2.0 * math.log(ROPE_BASE) / full_width)
    )
    angles = places.astype(jnp.float32)[:, None] * frequency[None, :]
    cosine = jnp.cos(angles)[:, None, :]
    sine_part = direction * jnp.sin(angles)[:, None, :]
    first_half = values[..., :half_width]
    second_half = values[..., half_width:]
    return jnp.concatenate(
        [
            first_half * cosine - second_half * sine_part,
            second_half * cosine + first_half * sine_part,
        ],
        axis=-1,
    )


def chain_join(earlier, later):
    return (earlier[0] * later[0], later[0][:, None, None] * earlier[1] + later[1])


def score_block(queries, query_seg, query_pos, key_rows, key_seg, key_pos, score_scale):
    raw_scores = (
        jnp.einsum("tkgd,skd->kgts", queries, key_rows, preferred_element_type=jnp.float32)
        * score_scale
    )
    allowed = (
        (query_seg[:, None] == key_seg[None, :])
        & (query_pos[:, None] >= key_pos[None, :])
        & (key_pos[None, :] >= 0)
    )
    return (raw_scores, allowed[None, None])


def absorb(
    running, queries, query_seg, query_pos, key_rows, value_rows, key_seg, key_pos, score_scale
):
    best_prev, total_prev, context_prev = running
    raw_scores, allowed = score_block(
        queries, query_seg, query_pos, key_rows, key_seg, key_pos, score_scale
    )
    masked = jnp.where(allowed, raw_scores, NEG_BIG)
    best_new = jnp.maximum(best_prev, jnp.max(masked, axis=-1))
    shrink = jnp.exp(best_prev - best_new)
    weights_new = jnp.where(allowed, jnp.exp(masked - best_new[..., None]), 0.0)
    total_new = total_prev * shrink + jnp.sum(weights_new, axis=-1)
    context_new = context_prev * shrink[..., None] + jnp.einsum(
        "kgts,skd->kgtd",
        weights_new.astype(jnp.bfloat16),
        value_rows,
        preferred_element_type=jnp.float32,
    )
    return (best_new, total_new, context_new)


def back_block(
    queries,
    query_seg,
    query_pos,
    grad_ctx,
    logsum,
    row_delta,
    key_rows,
    value_rows,
    key_seg,
    key_pos,
    score_scale,
):
    raw_scores, allowed = score_block(
        queries, query_seg, query_pos, key_rows, key_seg, key_pos, score_scale
    )
    probability = jnp.where(
        allowed, jnp.exp(jnp.where(allowed, raw_scores - logsum[..., None], NEG_BIG)), 0.0
    )
    probs_low = probability.astype(jnp.bfloat16)
    grad_values = jnp.einsum(
        "kgts,tkgd->skd", probs_low, grad_ctx, preferred_element_type=jnp.float32
    )
    grad_probs = jnp.einsum(
        "tkgd,skd->kgts", grad_ctx, value_rows, preferred_element_type=jnp.float32
    )
    grad_scores = (probability * (grad_probs - row_delta[..., None])).astype(jnp.bfloat16)
    grad_query = (
        jnp.einsum("kgts,skd->tkgd", grad_scores, key_rows, preferred_element_type=jnp.float32)
        * score_scale
    )
    grad_keys = (
        jnp.einsum("kgts,tkgd->skd", grad_scores, queries, preferred_element_type=jnp.float32)
        * score_scale
    )
    return (grad_query, grad_keys, grad_values)


def per_device(
    tokens,
    segments,
    cotangent,
    norm_gain,
    gating_weight,
    input_weight,
    state_weight,
    step_weight,
    conv_weight,
    conv_bias,
    step_bias,
    decay_log,
    skip_gain,
    ssm_gain,
    out_weight,
    query_weight,
    keyval_weight,
    context_weight,
    mlp_gain,
    gate_weight,
    up_weight,
    down_weight,
):
    bfloat = jnp.bfloat16
    single = jnp.float32
    tok_rows = tokens.shape[1]
    ssm_width = HEADS * SSM_HEAD
    kv_width = KVHEADS * ATT_HEAD
    groups = QHEADS // KVHEADS
    score_scale = 1.0 / math.sqrt(ATT_HEAD)
    places = lax.axis_index("seq") * tok_rows + jnp.arange(tok_rows, dtype=jnp.int32)
    inputs = tokens[0].astype(single)
    seg_ids = segments[0]
    own_segs = seg_ids.astype(single)
    grad_top = cotangent[0]
    index_col = jnp.arange(tok_rows)
    is_last = (index_col == tok_rows - 1).astype(single)[:, None]
    mixer_full = (
        lax.all_gather(norm_gain, ("batch", "seq"), axis=0, tiled=True),
        lax.all_gather(gating_weight, ("batch", "seq"), axis=0, tiled=True),
        lax.all_gather(input_weight, ("batch", "seq"), axis=0, tiled=True),
        lax.all_gather(state_weight, ("batch", "seq"), axis=0, tiled=True),
        lax.all_gather(step_weight, ("batch", "seq"), axis=0, tiled=True),
        lax.all_gather(conv_weight, ("batch", "seq"), axis=1, tiled=True),
        lax.all_gather(conv_bias, ("batch", "seq"), axis=0, tiled=True),
        lax.all_gather(ssm_gain, ("batch", "seq"), axis=0, tiled=True),
        lax.all_gather(out_weight, ("batch", "seq"), axis=0, tiled=True),
        lax.all_gather(query_weight, ("batch", "seq"), axis=0, tiled=True),
        lax.all_gather(keyval_weight, ("batch", "seq"), axis=0, tiled=True),
        lax.all_gather(context_weight, ("batch", "seq"), axis=0, tiled=True),
    )
    (
        gain_one,
        gating_full,
        input_full,
        state_full,
        step_full,
        conv_full,
        convbias_full,
        ssmgain_full,
        outw_full,
        query_full,
        keyval_full,
        context_full,
    ) = mixer_full
    scale_one = rms_scale(inputs)
    unit_one = inputs * scale_one
    normed = (unit_one * gain_one.astype(single)).astype(bfloat)
    gating = matmul(normed, gating_full)
    mixed_in = jnp.concatenate(
        [matmul(normed, input_full), matmul(normed, state_full)], axis=1
    ).astype(bfloat)
    step_raw = matmul(normed, step_full)
    prev_vals, prev_segs = passed_along(
        (mixed_in[tok_rows - CONV + 1 :], seg_ids[tok_rows - CONV + 1 :].astype(bfloat)), "seq", 1
    )
    extended = jnp.concatenate([prev_vals, mixed_in], axis=0).astype(single)
    ext_segs = jnp.concatenate([prev_segs.astype(single), own_segs])
    conv_pre = convbias_full.astype(single)[None, :]
    tap_masks = []
    for offset in range(CONV):
        matches = (ext_segs[offset : offset + tok_rows] == own_segs).astype(single)[:, None]
        tap_masks.append(matches)
        conv_pre = (
            conv_pre
            + conv_full[offset].astype(single)[None, :]
            * extended[offset : offset + tok_rows]
            * matches
        )
    activated = jax.nn.silu(conv_pre).astype(bfloat)
    ssm_in = activated[:, :ssm_width].reshape(tok_rows, HEADS, SSM_HEAD)
    ssm_in_f = ssm_in.astype(single)
    b_mat = activated[:, ssm_width : ssm_width + STATE]
    c_mat = activated[:, ssm_width + STATE :]
    stepbias_f = step_bias.astype(single)
    step_size = jax.nn.softplus(step_raw + stepbias_f[None, :])
    decay_rate = -jnp.exp(decay_log.astype(single))
    cumulative = jnp.cumsum(step_size * decay_rate[None, :], axis=0)
    allowed = (seg_ids[:, None] == seg_ids[None, :]) & (index_col[:, None] >= index_col[None, :])
    spread = jnp.where(allowed[None], cumulative.T[:, :, None] - cumulative.T[:, None, :], 0.0)
    decays = jnp.where(allowed[None], jnp.exp(spread), 0.0)
    inner_prod = matmul(c_mat, b_mat.T)
    step_cols = step_size.T[:, None, :]
    mix_weights = (inner_prod[None] * decays * step_cols).astype(bfloat)
    within = jnp.einsum("hts,shp->thp", mix_weights, ssm_in, preferred_element_type=single)
    prev_last = prev_segs[CONV - 2].astype(single)
    carried = (own_segs == prev_last).astype(single)
    entry_decay = jnp.exp(cumulative) * carried[:, None]
    ending = (seg_ids == seg_ids[tok_rows - 1]).astype(single)
    tail_decay = jnp.exp(cumulative[tok_rows - 1][None, :] - cumulative) * ending[:, None]
    tail_weight = tail_decay * step_size
    weighted = (ssm_in_f * tail_weight[:, :, None]).astype(bfloat)
    local_state = jnp.einsum("shp,sn->hpn", weighted, b_mat, preferred_element_type=single)
    passing = jnp.exp(cumulative[tok_rows - 1]) * carried[tok_rows - 1]
    _, state_in = carried_in(
        (passing, local_state),
        "seq",
        chain_join,
        (jnp.ones_like(passing), jnp.zeros_like(local_state)),
        False,
    )
    state_low = state_in.astype(bfloat)
    inter_raw = jnp.einsum("tn,hpn->thp", c_mat, state_low, preferred_element_type=single)
    skip_f = skip_gain.astype(single)
    ssm_out = (
        within + inter_raw * entry_decay[:, :, None] + skip_f[None, :, None] * ssm_in_f
    ).reshape(tok_rows, ssm_width)
    gate_act = jax.nn.silu(gating)
    gated = ssm_out * gate_act
    scale_ssm = rms_scale(gated)
    unit_ssm = gated * scale_ssm
    mamba_in = (unit_ssm * ssmgain_full.astype(single)).astype(bfloat)
    mamba_out = matmul(mamba_in, outw_full)
    query_proj = matmul(normed, query_full).reshape(tok_rows, QHEADS, ATT_HEAD)
    keyval_proj = matmul(normed, keyval_full)
    query_grp = (
        rotate(query_proj, places, 1.0).astype(bfloat).reshape(tok_rows, KVHEADS, groups, ATT_HEAD)
    )
    key_rot = (
        rotate(keyval_proj[:, :kv_width].reshape(tok_rows, KVHEADS, ATT_HEAD), places, 1.0)
        .astype(bfloat)
        .reshape(tok_rows, kv_width)
    )
    value_low = keyval_proj[:, kv_width:].astype(bfloat)
    key_segs = seg_ids.astype(bfloat)
    running = (
        jnp.full((KVHEADS, groups, tok_rows), NEG_BIG, single),
        jnp.zeros((KVHEADS, groups, tok_rows), single),
        jnp.zeros((KVHEADS, groups, tok_rows, ATT_HEAD), single),
    )
    run_state = running
    key_flat = lax.all_gather(key_rot, "seq", axis=0, tiled=True)
    value_flat = lax.all_gather(value_low, "seq", axis=0, tiled=True)
    key_seg_in = lax.all_gather(key_segs, "seq", axis=0, tiled=True)
    piece_rows = key_flat.shape[0]
    fold_block_rows = min(piece_rows, 512)

    def one_block(inner_run, block_index):
        offset = block_index * fold_block_rows
        key_part = lax.dynamic_slice_in_dim(key_flat, offset, fold_block_rows, 0).reshape(
            fold_block_rows, KVHEADS, ATT_HEAD
        )
        value_part = lax.dynamic_slice_in_dim(value_flat, offset, fold_block_rows, 0).reshape(
            fold_block_rows, KVHEADS, ATT_HEAD
        )
        seg_part = lax.dynamic_slice_in_dim(key_seg_in, offset, fold_block_rows, 0).astype(single)
        pos_part = offset + jnp.arange(fold_block_rows, dtype=jnp.int32)
        return (
            absorb(
                inner_run,
                query_grp,
                own_segs,
                places,
                key_part,
                value_part,
                seg_part,
                pos_part,
                score_scale,
            ),
            None,
        )

    run_state, _ = lax.scan(
        one_block, run_state, jnp.arange(piece_rows // fold_block_rows, dtype=jnp.int32)
    )
    running = run_state
    best_run, total_run, context_run = running
    context = context_run / total_run[..., None]
    logsum = best_run + jnp.log(total_run)
    context_low = (
        jnp.transpose(context, (2, 0, 1, 3)).reshape(tok_rows, QHEADS * ATT_HEAD).astype(bfloat)
    )
    attn_out = matmul(context_low, context_full)
    hidden = inputs + (mamba_out + attn_out)
    ffn_full = (
        lax.all_gather(mlp_gain, ("batch", "seq"), axis=0, tiled=True),
        lax.all_gather(gate_weight, ("batch", "seq"), axis=0, tiled=True),
        lax.all_gather(up_weight, ("batch", "seq"), axis=0, tiled=True),
        lax.all_gather(down_weight, ("batch", "seq"), axis=0, tiled=True),
    )
    scale_two = rms_scale(hidden)
    unit_two = hidden * scale_two
    normed_two = (unit_two * ffn_full[0].astype(single)).astype(bfloat)
    gate_pre = matmul(normed_two, ffn_full[1])
    up_pre = matmul(normed_two, ffn_full[2])
    gate_silu = jax.nn.silu(gate_pre)
    activation = (gate_silu * up_pre).astype(bfloat)
    result = (hidden + matmul(activation, ffn_full[3])).astype(bfloat)
    ffn_back = (
        lax.all_gather(mlp_gain, ("batch", "seq"), axis=0, tiled=True),
        lax.all_gather(gate_weight, ("batch", "seq"), axis=0, tiled=True),
        lax.all_gather(up_weight, ("batch", "seq"), axis=0, tiled=True),
        lax.all_gather(down_weight, ("batch", "seq"), axis=0, tiled=True),
    )
    gain_back, gatew_back, upw_back, downw_back = ffn_back
    grad_down = inner_rows(activation, grad_top)
    grad_act = times_trans(grad_top, downw_back)
    grad_gate_pre = (grad_act * up_pre * silu_slope(gate_pre)).astype(bfloat)
    grad_up_pre = (grad_act * gate_silu).astype(bfloat)
    grad_gatew = inner_rows(normed_two, grad_gate_pre)
    grad_upw = inner_rows(normed_two, grad_up_pre)
    grad_normed_two = times_trans(grad_gate_pre, gatew_back) + times_trans(grad_up_pre, upw_back)
    grad_gain_two = jnp.sum(grad_normed_two * unit_two, axis=0)
    grad_unit_two = grad_normed_two * gain_back.astype(single)
    grad_hidden = grad_top.astype(single) + scale_two * (
        grad_unit_two - unit_two * jnp.mean(grad_unit_two * unit_two, axis=-1, keepdims=True)
    )
    ffn_grads = (
        lax.psum_scatter(grad_gain_two, ("batch", "seq"), scatter_dimension=0, tiled=True),
        lax.psum_scatter(grad_gatew, ("batch", "seq"), scatter_dimension=0, tiled=True),
        lax.psum_scatter(grad_upw, ("batch", "seq"), scatter_dimension=0, tiled=True),
        lax.psum_scatter(grad_down, ("batch", "seq"), scatter_dimension=0, tiled=True),
    )
    mixer_back = (
        lax.all_gather(norm_gain, ("batch", "seq"), axis=0, tiled=True),
        lax.all_gather(gating_weight, ("batch", "seq"), axis=0, tiled=True),
        lax.all_gather(input_weight, ("batch", "seq"), axis=0, tiled=True),
        lax.all_gather(state_weight, ("batch", "seq"), axis=0, tiled=True),
        lax.all_gather(step_weight, ("batch", "seq"), axis=0, tiled=True),
        lax.all_gather(conv_weight, ("batch", "seq"), axis=1, tiled=True),
        lax.all_gather(conv_bias, ("batch", "seq"), axis=0, tiled=True),
        lax.all_gather(ssm_gain, ("batch", "seq"), axis=0, tiled=True),
        lax.all_gather(out_weight, ("batch", "seq"), axis=0, tiled=True),
        lax.all_gather(query_weight, ("batch", "seq"), axis=0, tiled=True),
        lax.all_gather(keyval_weight, ("batch", "seq"), axis=0, tiled=True),
        lax.all_gather(context_weight, ("batch", "seq"), axis=0, tiled=True),
    )
    (
        gainone_back,
        gating_back,
        input_back,
        state_back,
        step_back,
        conv_back,
        convbias_back,
        ssmgain_back,
        outw_back,
        query_back,
        keyval_back,
        context_back,
    ) = mixer_back
    grad_mix = grad_hidden.astype(bfloat)
    grad_outw = inner_rows(mamba_in, grad_mix)
    grad_ctxw = inner_rows(context_low, grad_mix)
    grad_context = times_trans(grad_mix, context_back).astype(bfloat)
    grad_mamba_in = times_trans(grad_mix, outw_back)
    grad_ssm_gain = jnp.sum(grad_mamba_in * unit_ssm, axis=0)
    grad_unit_ssm = grad_mamba_in * ssmgain_back.astype(single)
    grad_gated = scale_ssm * (
        grad_unit_ssm - unit_ssm * jnp.mean(grad_unit_ssm * unit_ssm, axis=-1, keepdims=True)
    )
    grad_y = (grad_gated * gate_act).astype(bfloat).reshape(tok_rows, HEADS, SSM_HEAD)
    grad_gating = (grad_gated * ssm_out * silu_slope(gating)).astype(bfloat)
    grad_ctx_grp = grad_context.reshape(tok_rows, KVHEADS, groups, ATT_HEAD)
    row_delta = jnp.sum(jnp.transpose(grad_ctx_grp.astype(single), (1, 2, 0, 3)) * context, axis=-1)
    zero_query = jnp.zeros((tok_rows, KVHEADS, groups, ATT_HEAD), single)
    keys_all, values_all, segs_all = (
        lax.all_gather(key_rot, "seq", axis=0, tiled=True),
        lax.all_gather(value_low, "seq", axis=0, tiled=True),
        lax.all_gather(key_segs, "seq", axis=0, tiled=True),
    )
    total_rows = keys_all.shape[0]
    block_rows = min(total_rows, 512)

    def back_step(acc_query, block_index):
        offset = block_index * block_rows
        key_part = lax.dynamic_slice_in_dim(keys_all, offset, block_rows, 0).reshape(
            block_rows, KVHEADS, ATT_HEAD
        )
        value_part = lax.dynamic_slice_in_dim(values_all, offset, block_rows, 0).reshape(
            block_rows, KVHEADS, ATT_HEAD
        )
        seg_part = lax.dynamic_slice_in_dim(segs_all, offset, block_rows, 0).astype(single)
        pos_part = offset + jnp.arange(block_rows, dtype=jnp.int32)
        part_query, part_keys, part_values = back_block(
            query_grp,
            own_segs,
            places,
            grad_ctx_grp,
            logsum,
            row_delta,
            key_part,
            value_part,
            seg_part,
            pos_part,
            score_scale,
        )
        return (
            acc_query + part_query,
            jnp.concatenate(
                [
                    part_keys.reshape(block_rows, kv_width),
                    part_values.reshape(block_rows, kv_width),
                ],
                axis=1,
            ),
        )

    grad_query, grad_parts = lax.scan(
        back_step, zero_query, jnp.arange(total_rows // block_rows, dtype=jnp.int32)
    )
    grad_keyval = lax.psum_scatter(
        grad_parts.reshape(total_rows, 2 * kv_width).astype(jnp.bfloat16),
        "seq",
        scatter_dimension=0,
        tiled=True,
    ).astype(jnp.float32)
    grad_query_proj = (
        rotate(grad_query.reshape(tok_rows, QHEADS, ATT_HEAD), places, -1.0)
        .reshape(tok_rows, QHEADS * ATT_HEAD)
        .astype(bfloat)
    )
    grad_key_proj = rotate(
        grad_keyval[:, :kv_width].reshape(tok_rows, KVHEADS, ATT_HEAD), places, -1.0
    ).reshape(tok_rows, kv_width)
    grad_keyval_proj = jnp.concatenate([grad_key_proj, grad_keyval[:, kv_width:]], axis=1).astype(
        bfloat
    )
    grad_y_f = grad_y.astype(single)
    grad_skip = jnp.sum(grad_y_f * ssm_in_f, axis=(0, 2))
    grad_mixw = jnp.einsum("thp,shp->hts", grad_y, ssm_in, preferred_element_type=single)
    grad_ssm_in = skip_f[None, :, None] * grad_y_f + jnp.einsum(
        "hts,thp->shp", mix_weights, grad_y, preferred_element_type=single
    )
    product = grad_mixw * decays
    grad_inner = jnp.sum(product * step_cols, axis=0).astype(bfloat)
    decay_flow = product * inner_prod[None] * step_cols
    grad_step = jnp.sum(product * inner_prod[None], axis=1).T
    grad_cumul = jnp.sum(decay_flow, axis=2).T - jnp.sum(decay_flow, axis=1).T
    grad_c = matmul(grad_inner, b_mat)
    grad_b = inner_rows(grad_inner, c_mat)
    grad_across = (grad_y_f * entry_decay[:, :, None]).reshape(tok_rows, ssm_width)
    grad_c = grad_c + matmul_high(grad_across, state_low.astype(single).reshape(ssm_width, STATE))
    grad_state_here = inner_high(grad_across, c_mat.astype(single)).reshape(HEADS, SSM_HEAD, STATE)
    grad_entry = jnp.sum(grad_y_f * inter_raw, axis=2)
    grad_cumul = grad_cumul + grad_entry * entry_decay
    _, grad_state_out = carried_in(
        (passing, grad_state_here),
        "seq",
        chain_join,
        (jnp.ones_like(passing), jnp.zeros_like(grad_state_here)),
        True,
    )
    grad_passing = jnp.sum(grad_state_out * state_in, axis=(1, 2))
    grad_out_flat = grad_state_out.reshape(ssm_width, STATE)
    grad_weighted = times_high(b_mat.astype(single), grad_out_flat).reshape(
        tok_rows, HEADS, SSM_HEAD
    )
    grad_b = grad_b + matmul_high(
        weighted.astype(single).reshape(tok_rows, ssm_width), grad_out_flat
    )
    grad_ssm_in = grad_ssm_in + grad_weighted * tail_weight[:, :, None]
    grad_tail = jnp.sum(grad_weighted * ssm_in_f, axis=2)
    tail_flow = grad_tail * tail_weight
    grad_step = grad_step + grad_tail * tail_decay
    grad_cumul = (
        grad_cumul
        - tail_flow
        + is_last * (grad_passing * passing + jnp.sum(tail_flow, axis=0))[None, :]
    )
    grad_rate_term = lax.cumsum(grad_cumul, axis=0, reverse=True)
    grad_step = grad_step + grad_rate_term * decay_rate[None, :]
    grad_decay = jnp.sum(grad_rate_term * step_size, axis=0) * decay_rate
    grad_step_raw = grad_step * jax.nn.sigmoid(step_raw + stepbias_f[None, :])
    grad_step_bias = jnp.sum(grad_step_raw, axis=0)
    grad_step_low = grad_step_raw.astype(bfloat)
    grad_act_in = jnp.concatenate(
        [grad_ssm_in.reshape(tok_rows, ssm_width), grad_b, grad_c], axis=1
    )
    grad_pre = grad_act_in * silu_slope(conv_pre)
    grad_conv_bias = jnp.sum(grad_pre, axis=0)
    conv_rows = []
    grad_ext = jnp.zeros((tok_rows + CONV - 1, grad_pre.shape[1]), single)
    for offset in range(CONV):
        masked_grad = grad_pre * tap_masks[offset]
        conv_rows.append(jnp.sum(masked_grad * extended[offset : offset + tok_rows], axis=0))
        grad_ext = grad_ext + jnp.pad(
            masked_grad * conv_back[offset].astype(single)[None, :],
            ((offset, CONV - 1 - offset), (0, 0)),
        )
    grad_conv = jnp.stack(conv_rows, axis=0)
    returned = passed_along(grad_ext[: CONV - 1].astype(jnp.bfloat16), "seq", -1).astype(
        jnp.float32
    )
    grad_mixed = (
        grad_ext[CONV - 1 :] + jnp.pad(returned, ((tok_rows - CONV + 1, 0), (0, 0)))
    ).astype(bfloat)
    grad_inputw = inner_rows(normed, grad_mixed[:, :ssm_width])
    grad_statew = inner_rows(normed, grad_mixed[:, ssm_width:])
    grad_gatingw = inner_rows(normed, grad_gating)
    grad_stepw = inner_rows(normed, grad_step_low)
    grad_queryw = inner_rows(normed, grad_query_proj)
    grad_keyvalw = inner_rows(normed, grad_keyval_proj)
    grad_normed = (
        times_trans(grad_mixed[:, :ssm_width], input_back)
        + times_trans(grad_mixed[:, ssm_width:], state_back)
        + times_trans(grad_gating, gating_back)
        + times_trans(grad_step_low, step_back)
        + times_trans(grad_query_proj, query_back)
        + times_trans(grad_keyval_proj, keyval_back)
    )
    grad_gain_one = jnp.sum(grad_normed * unit_one, axis=0)
    grad_unit_one = grad_normed * gainone_back.astype(single)
    grad_inputs = grad_hidden + scale_one * (
        grad_unit_one - unit_one * jnp.mean(grad_unit_one * unit_one, axis=-1, keepdims=True)
    )
    mixer_grads = (
        lax.psum_scatter(grad_gain_one, ("batch", "seq"), scatter_dimension=0, tiled=True),
        lax.psum_scatter(grad_gatingw, ("batch", "seq"), scatter_dimension=0, tiled=True),
        lax.psum_scatter(grad_inputw, ("batch", "seq"), scatter_dimension=0, tiled=True),
        lax.psum_scatter(grad_statew, ("batch", "seq"), scatter_dimension=0, tiled=True),
        lax.psum_scatter(grad_stepw, ("batch", "seq"), scatter_dimension=0, tiled=True),
        lax.psum_scatter(grad_conv, ("batch", "seq"), scatter_dimension=1, tiled=True),
        lax.psum_scatter(grad_conv_bias, ("batch", "seq"), scatter_dimension=0, tiled=True),
        lax.psum_scatter(grad_ssm_gain, ("batch", "seq"), scatter_dimension=0, tiled=True),
        lax.psum_scatter(grad_outw, ("batch", "seq"), scatter_dimension=0, tiled=True),
        lax.psum_scatter(grad_queryw, ("batch", "seq"), scatter_dimension=0, tiled=True),
        lax.psum_scatter(grad_keyvalw, ("batch", "seq"), scatter_dimension=0, tiled=True),
        lax.psum_scatter(grad_ctxw, ("batch", "seq"), scatter_dimension=0, tiled=True),
    )
    head_sums = lax.psum((grad_step_bias, grad_decay, grad_skip), ("batch", "seq"))
    return (
        result[None],
        grad_inputs.astype(bfloat)[None],
        mixer_grads[0],
        mixer_grads[1],
        mixer_grads[2],
        mixer_grads[3],
        mixer_grads[4],
        mixer_grads[5],
        mixer_grads[6],
        head_sums[0],
        head_sums[1],
        head_sums[2],
        mixer_grads[7],
        mixer_grads[8],
        mixer_grads[9],
        mixer_grads[10],
        mixer_grads[11],
        ffn_grads[0],
        ffn_grads[1],
        ffn_grads[2],
        ffn_grads[3],
    )


def solution(mesh):
    return jax.shard_map(
        per_device,
        mesh=mesh,
        in_specs=(
            P("batch", "seq", None),
            P("batch", "seq"),
            P("batch", "seq", None),
            P(("batch", "seq")),
            P(("batch", "seq"), None),
            P(("batch", "seq"), None),
            P(("batch", "seq"), None),
            P(("batch", "seq"), None),
            P(None, ("batch", "seq")),
            P(("batch", "seq")),
            P(),
            P(),
            P(),
            P(("batch", "seq")),
            P(("batch", "seq"), None),
            P(("batch", "seq"), None),
            P(("batch", "seq"), None),
            P(("batch", "seq"), None),
            P(("batch", "seq")),
            P(("batch", "seq"), None),
            P(("batch", "seq"), None),
            P(("batch", "seq"), None),
        ),
        out_specs=(
            P("batch", "seq", None),
            P("batch", "seq", None),
            P(("batch", "seq")),
            P(("batch", "seq"), None),
            P(("batch", "seq"), None),
            P(("batch", "seq"), None),
            P(("batch", "seq"), None),
            P(None, ("batch", "seq")),
            P(("batch", "seq")),
            P(),
            P(),
            P(),
            P(("batch", "seq")),
            P(("batch", "seq"), None),
            P(("batch", "seq"), None),
            P(("batch", "seq"), None),
            P(("batch", "seq"), None),
            P(("batch", "seq")),
            P(("batch", "seq"), None),
            P(("batch", "seq"), None),
            P(("batch", "seq"), None),
        ),
        check_vma=False,
    )
```

profile of v0, /device:TPU:0, one launch (start us, length us, event | category | flops | bytes accessed | tf_op | source)
XLA Modules:
  0.0 4035.3 jit_solution(15488468895492674639)
XLA Ops:
  12.9 42.7 %all-reduce.14 = (bf16[2048]{0:T(1024)(128)(2,1)S(1)}, bf16[3584]{0:T(1024)(128)(2,1)S(1)}, bf16[3072]{0:T(1024)(128)(2,1)}, bf16[2048]{0:T(1024)(128)(2,1)}) all-reduce(bf16[2048]{0:T(1024)(128)(2,1)S(1)} %dynamic-update-slice.1, bf16[3584]{0:T(1024)(128)(2,1)S(1)} %dynamic-update-slice, ...), channel_id=1, replica_groups=mesh['batch'=4,'seq'=8] {'batch','seq'}, use_global_device_ids=true, to_apply=%add.6 | all-reduce | flops 10752 | bytes 43008
  78.8 41.3 %all-gather.3 = bf16[32,64,48]{1,2,0:T(8,128)(2,1)S(1)} all-gather(bf16[1,64,48]{1,2,0:T(8,128)(2,1)S(1)} %bitcast.495), channel_id=1, replica_groups=mesh['batch'=4,'seq'=8] {'batch','seq'}, dimensions={0}, use_global_device_ids=true | all-gather | bytes 202752 | tf_op jit(solution)/shard_map/all_gather | solution.py:229
  123.6 36.7 all-gather.2
  170.7 56.5 %all-gather.21.cloned.1.call-done = bf16[2048,3072]{1,0:T(8,128)(2,1)} async-done(((bf16[64,3072]{1,0:T(8,128)(2,1)}), bf16[2048,3072]{1,0:T(8,128)(2,1)}) %all-gather.21.cloned.1.call-update) | async-done | bytes 12582928 | tf_op jit(solution)/shard_map/all_gather | solution.py:227
  294.6 19.8 all-gather.33.cloned.1.call-done
  339.5 72.1 %while.59 = (s32[]{:T(128)}, f32[2,4,256]{2,1,0:T(4,128)S(1)}, f32[2,4,256]{2,1,0:T(4,128)}, f32[2,4,256,128]{3,2,1,0:T(8,128)}, f32[256]{0:T(256)}, /*index=5*/...) while((s32[]{:T(128)}, f32[2,4,256]{2,1,0:T(4,128)S(1)}, ...), condition=%wide.region_9.10_spmd.clone, body=%wide.region_6.9_spmd.clone.sunk | while | flops 551825664 | bytes 34288952 | solution.py:369
  417.4 38.6 all-gather.45.cloned.1.call-done
  456.0 29.8 while.58
  506.3 47.1 %all-gather.25.cloned.1.call-done = bf16[2048,3072]{1,0:T(8,128)(2,1)} async-done(((bf16[64,3072]{1,0:T(8,128)(2,1)}), bf16[2048,3072]{1,0:T(8,128)(2,1)}) %all-gather.25.cloned.1.call-update) | async-done | bytes 12582928 | tf_op jit(solution)/shard_map/all_gather | solution.py:226
  565.6 85.0 %all-gather.27.cloned.1.call-done = bf16[3072,2048]{1,0:T(8,128)(2,1)} async-done(((bf16[96,2048]{1,0:T(8,128)(2,1)}), bf16[3072,2048]{1,0:T(8,128)(2,1)}) %all-gather.27.cloned.1.call-update) | async-done | bytes 12582928 | tf_op jit(solution)/shard_map/all_gather | solution.py:233
  661.0 52.9 %all-gather.37.cloned.1.call-done = bf16[1024,2048]{1,0:T(8,128)(2,1)} async-done(((bf16[32,2048]{1,0:T(8,128)(2,1)}), bf16[1024,2048]{1,0:T(8,128)(2,1)}) %all-gather.37.cloned.1.call-update) | async-done | bytes 4194320 | tf_op jit(solution)/shard_map/all_gather | solution.py:236
  721.1 109.3 %all-gather.39.cloned.1.call-done = bf16[2048,4096]{1,0:T(8,128)(2,1)} async-done(((bf16[64,4096]{1,0:T(8,128)(2,1)}), bf16[2048,4096]{1,0:T(8,128)(2,1)}) %all-gather.39.cloned.1.call-update) | async-done | bytes 16777232 | tf_op jit(solution)/shard_map/all_gather | solution.py:383
  843.0 103.4 %all-gather.41.cloned.1.call-done = bf16[2048,4096]{1,0:T(8,128)(2,1)} async-done(((bf16[64,4096]{1,0:T(8,128)(2,1)}), bf16[2048,4096]{1,0:T(8,128)(2,1)}) %all-gather.41.cloned.1.call-update) | async-done | bytes 16777232 | tf_op jit(solution)/shard_map/all_gather | solution.py:384
  959.5 103.0 %all-gather.43.cloned.1.call-done = bf16[4096,2048]{1,0:T(8,128)(2,1)} async-done(((bf16[128,2048]{1,0:T(8,128)(2,1)}), bf16[4096,2048]{1,0:T(8,128)(2,1)}) %all-gather.43.cloned.1.call-update) | async-done | bytes 16777232 | tf_op jit(solution)/shard_map/all_gather | solution.py:385
  1171.4 50.3 %while.61 = (s32[]{:T(128)}, f32[256,2,4,128]{0,3,2,1:T(8,128)}, bf16[4,512,512]{2,1,0:T(8,128)(2,1)}, s32[4]{0:T(128)S(1)}, bf16[2048,256]{0,1:T(8,128)(2,1)}, ...) while((s32[]{:T(128)}, f32[256,2,4,128]{0,3,2,1:T(8,128)}, ...), condition=%wide.region_27.28_spmd.clone, body=%wide.region_26.27_spmd.clone.sunk | while | flops 1357383936 | bytes 33199916 | solution.py:505
  1223.1 27.5 all-gather.47.cloned.1.call-done
  1250.6 43.5 %while.60 = (s32[]{:T(128)}, f32[48,64,256]{2,1,0:T(8,128)}, s32[]{:T(128)}, bf16[8,48]{1,0:T(8,128)(2,1)}, bf16[8,48,64,256]{3,2,1,0:T(8,128)(2,1)}, /*index=5*/s32[]{:T(128)}, s32[]{:T(128)}, s32[]{:T(128)}, s32[]{:T(128)}) while((s32[]{:T(128)}, f32[48,64,256]{2,1,0:T(8,128)}, s32[]{:T(128)}, bf16[8,48]{1,0:T(8,128)(2,1)}, ...), condition=%wide.region_14.15_spmd.clone, body=%wide.region_13.14_spmd.clone.sunk | while | flops 3932216 | bytes 7864967 | solution.py:46
  1405.1 14.8 fusion.172
  1419.9 14.8 fusion.173
  1436.0 14.9 fusion.83
  1493.3 42.5 %all-reduce.13 = (f32[2048]{0:T(1024)S(1)}, f32[3584]{0:T(1024)S(1)}, f32[48]{0:T(128)}, f32[48]{0:T(128)}, f32[48]{0:T(128)}, /*index=5*/f32[3072]{0:T(1024)S(1)}, f32[2048]{0:T(1024)S(1)}) all-reduce(f32[2048]{0:T(1024)S(1)} %get-tuple-element.658, ...), channel_id=5, replica_groups=mesh['batch'=4,'seq'=8] {'batch','seq'}, use_global_device_ids=true, to_apply=%region_31.32.clone | all-reduce | flops 10896 | bytes 87168
  1544.2 54.5 %reduce-scatter.40.cloned.1.call-done = f32[64,48]{1,0:T(8,128)} async-done(((f32[2048,48]{1,0:T(8,128)}), f32[64,48]{1,0:T(8,128)}) %reduce-scatter.40.cloned.1.call-update) | async-done | bytes 12304
  1600.1 140.2 %reduce-scatter.30.cloned.1.call-done = f32[64,512]{1,0:T(8,128)} async-done(((f32[2048,512]{1,0:T(8,128)}), f32[64,512]{1,0:T(8,128)}) %reduce-scatter.30.cloned.1.call-update) | async-done | bytes 131088 | tf_op jit(solution)/shard_map/reduce_scatter | solution.py:624
  1740.4 151.7 %reduce-scatter.32.cloned.1.call-done = f32[32,2048]{1,0:T(8,128)} async-done(((f32[1024,2048]{1,0:T(8,128)}), f32[32,2048]{1,0:T(8,128)}) %reduce-scatter.32.cloned.1.call-update) | async-done | bytes 262160 | tf_op jit(solution)/shard_map/reduce_scatter | solution.py:625
  1892.1 152.4 %reduce-scatter.28.cloned.1.call-done = f32[64,1024]{1,0:T(8,128)} async-done(((f32[2048,1024]{1,0:T(8,128)}), f32[64,1024]{1,0:T(8,128)}) %reduce-scatter.28.cloned.1.call-update) | async-done | bytes 262160 | tf_op jit(solution)/shard_map/reduce_scatter | solution.py:623
  2044.5 143.7 %reduce-scatter.24.cloned.1.call-done = f32[64,512]{1,0:T(8,128)} async-done(((f32[2048,512]{1,0:T(8,128)}), f32[64,512]{1,0:T(8,128)}) %reduce-scatter.24.cloned.1.call-update) | async-done | bytes 131088 | tf_op jit(solution)/shard_map/reduce_scatter | solution.py:617
  2188.2 250.0 %reduce-scatter.26.cloned.1.call-done = f32[96,2048]{1,0:T(8,128)} async-done(((f32[3072,2048]{1,0:T(8,128)}), f32[96,2048]{1,0:T(8,128)}) %reduce-scatter.26.cloned.1.call-update) | async-done | bytes 786448 | tf_op jit(solution)/shard_map/reduce_scatter | solution.py:622
  2438.2 253.2 %reduce-scatter.20.cloned.1.call-done = f32[64,3072]{1,0:T(8,128)} async-done(((f32[2048,3072]{1,0:T(8,128)}), f32[64,3072]{1,0:T(8,128)}) %reduce-scatter.20.cloned.1.call-update) | async-done | bytes 786448 | tf_op jit(solution)/shard_map/reduce_scatter | solution.py:615
  2691.4 251.9 %reduce-scatter.22.cloned.1.call-done = f32[64,3072]{1,0:T(8,128)} async-done(((f32[2048,3072]{1,0:T(8,128)}), f32[64,3072]{1,0:T(8,128)}) %reduce-scatter.22.cloned.1.call-update) | async-done | bytes 786448 | tf_op jit(solution)/shard_map/reduce_scatter | solution.py:616
  2943.3 363.7 %reduce-scatter.34.cloned.1.call-done = f32[64,4096]{1,0:T(8,128)} async-done(((f32[2048,4096]{1,0:T(8,128)}), f32[64,4096]{1,0:T(8,128)}) %reduce-scatter.34.cloned.1.call-update) | async-done | bytes 1048592 | tf_op jit(solution)/shard_map/reduce_scatter | solution.py:416
  3307.0 360.5 %reduce-scatter.36.cloned.1.call-done = f32[64,4096]{1,0:T(8,128)} async-done(((f32[2048,4096]{1,0:T(8,128)}), f32[64,4096]{1,0:T(8,128)}) %reduce-scatter.36.cloned.1.call-update) | async-done | bytes 1048592 | tf_op jit(solution)/shard_map/reduce_scatter | solution.py:417
  3667.5 360.5 %reduce-scatter.38.cloned.1.call-done = f32[128,2048]{1,0:T(8,128)} async-done(((f32[4096,2048]{1,0:T(8,128)}), f32[128,2048]{1,0:T(8,128)}) %reduce-scatter.38.cloned.1.call-update) | async-done | bytes 1048592 | tf_op jit(solution)/shard_map/reduce_scatter | solution.py:418
  (722 shorter events, 678.4 us)
Async XLA Ops:
  7.2 63.2 %all-gather.29.cloned.1.call-start = ((), (), s32[]{:S(2)}) async-start(), calls=%async_computation.17 | async-start | bytes 2162688 | tf_op jit(solution)/shard_map/all_gather | solution.py:235
  7.9 160.4 %all-gather.23.cloned.1.call-start = ((), (), s32[]{:S(2)}) async-start(), calls=%async_computation.14 | async-start | bytes 2162688 | tf_op jit(solution)/shard_map/all_gather | solution.py:228
  8.7 218.5 %all-gather.21.cloned.1.call-start = ((), (), s32[]{:S(2)}) async-start(), calls=%async_computation.13 | async-start | bytes 12976128 | tf_op jit(solution)/shard_map/all_gather | solution.py:227
  9.4 282.9 %all-gather.35.cloned.1.call-start = ((), (), s32[]{:S(2)}) async-start(), calls=%async_computation.20 | async-start | bytes 1179648 | tf_op jit(solution)/shard_map/all_gather | solution.py:339
  73.7 240.7 %all-gather.33.cloned.1.call-start = ((), (), s32[]{:S(2)}) async-start(), calls=%async_computation.19 | async-start | bytes 4325376 | tf_op jit(solution)/shard_map/all_gather | solution.py:234
  74.3 264.7 %all-gather.31.cloned.1.call-start = ((), (), s32[]{:S(2)}) async-start(), calls=%async_computation.18 | async-start | bytes 1179648 | tf_op jit(solution)/shard_map/all_gather | solution.py:338
  74.5 87.3 %collective-permute-start.1 = (bf16[3]{0:T(256)(128)(2,1)S(1)}, bf16[3]{0:T(256)(128)(2,1)S(1)}, u32[]{:S(2)}, u32[]{:S(2)}) collective-permute-start(bf16[3]{0:T(256)(128)(2,1)S(1)} %fusion.138), channel_id=1, source_target_pairs={{0,1},{1,2},{2,3},{3,4},{4,5},{5,6},{6,7},{8,9},{9,10},{10,11},{11... | collective-permute-start | bytes 26 | tf_op jit(solution)/shard_map/ppermute | solution.py:26
  235.4 3.7 collective-permute-start
  238.8 217.2 %all-gather.45.cloned.1.call-start = ((), (), s32[]{:S(2)}) async-start(), calls=%async_computation.36 | async-start | bytes 14155776 | tf_op jit(solution)/shard_map/all_gather | solution.py:32
  250.1 303.2 %all-gather.25.cloned.1.call-start = ((), (), s32[]{:S(2)}) async-start(), calls=%async_computation.15 | async-start | bytes 12976128 | tf_op jit(solution)/shard_map/all_gather | solution.py:226
  250.9 399.8 %all-gather.27.cloned.1.call-start = ((), (), s32[]{:S(2)}) async-start(), calls=%async_computation.16 | async-start | bytes 12976128 | tf_op jit(solution)/shard_map/all_gather | solution.py:233
  251.6 462.3 %all-gather.37.cloned.1.call-start = ((), (), s32[]{:S(2)}) async-start(), calls=%async_computation.21 | async-start | bytes 4325376 | tf_op jit(solution)/shard_map/all_gather | solution.py:236
  252.2 578.2 %all-gather.39.cloned.1.call-start = ((), (), s32[]{:S(2)}) async-start(), calls=%async_computation.22 | async-start | bytes 17301504 | tf_op jit(solution)/shard_map/all_gather | solution.py:383
  252.9 693.4 %all-gather.41.cloned.1.call-start = ((), (), s32[]{:S(2)}) async-start(), calls=%async_computation.23 | async-start | bytes 17301504 | tf_op jit(solution)/shard_map/all_gather | solution.py:384
  253.5 809.0 %all-gather.43.cloned.1.call-start = ((), (), s32[]{:S(2)}) async-start(), calls=%async_computation.24 | async-start | bytes 17301504 | tf_op jit(solution)/shard_map/all_gather | solution.py:385
  254.3 996.3 %all-gather.47.cloned.1.call-start = ((), (), s32[]{:S(2)}) async-start(), calls=%async_computation.37 | async-start | bytes 14155776 | tf_op jit(solution)/shard_map/all_gather | solution.py:32
  417.4 733.2 %copy-start.82 = (f32[256,256]{1,0:T(8,128)}, f32[256,256]{1,0:T(8,128)S(1)}, u32[]{:S(2)}) copy-start(f32[256,256]{1,0:T(8,128)S(1)} %fusion.123) | copy-start | bytes 786436
  485.8 680.8 %copy-start.3 = (f32[48,64,256]{2,1,0:T(8,128)}, f32[48,64,256]{2,1,0:T(8,128)S(1)}, u32[]{:S(2)}) copy-start(f32[48,64,256]{2,1,0:T(8,128)S(1)} %get-tuple-element.374) | copy-start | bytes 9437188
  1135.5 197.4 %reduce-scatter.18.cloned.1.call-start = ((), (), s32[]{:S(2)}) async-start(), calls=%async_computation.25 | async-start | bytes 2359296 | tf_op jit(solution)/shard_map/reduce_scatter | solution.py:508
  1221.7 321.0 %reduce-scatter.42.cloned.1.call-start = ((), (), s32[]{:S(2)}) async-start(), calls=%async_computation.39 | async-start | bytes 1892352
  1330.2 268.5 %reduce-scatter.40.cloned.1.call-start = ((), (), s32[]{:S(2)}) async-start(), calls=%async_computation.38 | async-start | bytes 1081344
  1332.6 407.8 %reduce-scatter.30.cloned.1.call-start = ((), (), s32[]{:S(2)}) async-start(), calls=%async_computation.31 | async-start | bytes 4325376 | tf_op jit(solution)/shard_map/reduce_scatter | solution.py:624
  1338.5 553.7 %reduce-scatter.32.cloned.1.call-start = ((), (), s32[]{:S(2)}) async-start(), calls=%async_computation.32 | async-start | bytes 8650752 | tf_op jit(solution)/shard_map/reduce_scatter | solution.py:625
  1344.4 700.1 %reduce-scatter.28.cloned.1.call-start = ((), (), s32[]{:S(2)}) async-start(), calls=%async_computation.30 | async-start | bytes 8650752 | tf_op jit(solution)/shard_map/reduce_scatter | solution.py:623
  1350.7 837.5 %reduce-scatter.24.cloned.1.call-start = ((), (), s32[]{:S(2)}) async-start(), calls=%async_computation.28 | async-start | bytes 4325376 | tf_op jit(solution)/shard_map/reduce_scatter | solution.py:617
  1359.7 3.1 collective-permute-start.2
  1367.3 1070.9 %reduce-scatter.26.cloned.1.call-start = ((), (), s32[]{:S(2)}) async-start(), calls=%async_computation.29 | async-start | bytes 25952256 | tf_op jit(solution)/shard_map/reduce_scatter | solution.py:622
  1380.2 1311.1 %reduce-scatter.20.cloned.1.call-start = ((), (), s32[]{:S(2)}) async-start(), calls=%async_computation.26 | async-start | bytes 25952256 | tf_op jit(solution)/shard_map/reduce_scatter | solution.py:615
  1391.9 1551.4 %reduce-scatter.22.cloned.1.call-start = ((), (), s32[]{:S(2)}) async-start(), calls=%async_computation.27 | async-start | bytes 25952256 | tf_op jit(solution)/shard_map/reduce_scatter | solution.py:616
  1403.9 1903.1 %reduce-scatter.34.cloned.1.call-start = ((), (), s32[]{:S(2)}) async-start(), calls=%async_computation.33 | async-start | bytes 34603008 | tf_op jit(solution)/shard_map/reduce_scatter | solution.py:416
  1419.9 2247.6 %reduce-scatter.36.cloned.1.call-start = ((), (), s32[]{:S(2)}) async-start(), calls=%async_computation.34 | async-start | bytes 34603008 | tf_op jit(solution)/shard_map/reduce_scatter | solution.py:417
  1434.8 2593.1 %reduce-scatter.38.cloned.1.call-start = ((), (), s32[]{:S(2)}) async-start(), calls=%async_computation.35 | async-start | bytes 34603008 | tf_op jit(solution)/shard_map/reduce_scatter | solution.py:418
  (159 other events, 3409.8 us)
Sparse Core Ops, SparseCore 0:
  11.0 59.2 all-gather.28
  73.3 55.6 all-gather.22
  132.1 95.0 all-gather.20
  229.2 20.4 all-gather.34
  252.6 61.7 all-gather.32
  316.4 22.5 all-gather.30
  340.6 115.3 all-gather.44
  459.0 94.2 all-gather.24
  556.3 94.2 all-gather.26
  653.5 60.3 all-gather.36
  716.9 113.4 all-gather.38
  833.3 113.0 all-gather.40
  949.4 113.0 all-gather.42
  1135.6 114.8 all-gather.46
  1252.7 33.9 reduce-scatter.17
  1330.3 134.7 reduce-scatter.41
  1467.3 131.3 reduce-scatter.39
  1601.4 138.9 reduce-scatter.29
  1743.2 148.8 reduce-scatter.31
  1894.8 149.6 reduce-scatter.27
  2047.4 140.7 reduce-scatter.23
  2195.2 242.9 reduce-scatter.25
  2446.3 245.0 reduce-scatter.19
  2698.2 245.0 reduce-scatter.21
  2946.3 360.6 reduce-scatter.33
  3309.8 357.6 reduce-scatter.35
  3670.3 357.6 reduce-scatter.37
where the time goes:
time: 4050 us; the launch traced here: 4040 us
  waiting for transfers between devices  3160 us (78%)
  matrix products  373 us (9%)
  blocking collectives  185 us (5%)
  other arithmetic  176 us (4%)
  local copies, waits for them, and re-layouts  112 us (3%)
    reduce_scatter x1, waiting for transfers between devices, per_device(): lax.psum_scatter(grad_gatew, ('batch', 'seq'), scatter_dimension=0, tiled...  364 us
    reduce_scatter x1, waiting for transfers between devices, per_device(): lax.psum_scatter(grad_upw, ('batch', 'seq'), scatter_dimension=0, tiled=T...  360 us
    reduce_scatter x1, waiting for transfers between devices, per_device(): lax.psum_scatter(grad_down, ('batch', 'seq'), scatter_dimension=0, tiled=...  360 us
    reduce_scatter x1, waiting for transfers between devices, per_device(): lax.psum_scatter(grad_gatingw, ('batch', 'seq'), scatter_dimension=0, til...  253 us
    reduce_scatter x1, waiting for transfers between devices, per_device(): lax.psum_scatter(grad_inputw, ('batch', 'seq'), scatter_dimension=0, tile...  252 us
    reduce_scatter x1, waiting for transfers between devices, per_device(): lax.psum_scatter(grad_outw, ('batch', 'seq'), scatter_dimension=0, tiled=...  250 us
    reduce_scatter x1, waiting for transfers between devices, per_device(): lax.psum_scatter(grad_queryw, ('batch', 'seq'), scatter_dimension=0, tile...  152 us
    reduce_scatter x1, waiting for transfers between devices, per_device(): lax.psum_scatter(grad_ctxw, ('batch', 'seq'), scatter_dimension=0, tiled=...  152 us
  transfers between devices with their start and end apart: 30, of which 24 were waited for; matrix products, arithmetic and copies ran while one was open for 14% of the time, Pallas kernels for 0%

commit v1 on v0

v1 whole, which is shorter than its diff:
```python
import math

import jax
import jax.numpy as jnp
from jax import lax
from jax.sharding import Mesh
from jax.sharding import PartitionSpec as P

HEADS = 48
SSM_HEAD = 64
STATE = 256
CONV = 4
QHEADS = 8
KVHEADS = 2
ATT_HEAD = 128
EPSILON = 1e-05
ROPE_BASE = 10000.0
NEG_BIG = -1e30
HIGH = lax.Precision.HIGHEST

RANKS = 8
ROWS = 4
OWN_HEADS = HEADS // RANKS
OWN_SSM = OWN_HEADS * SSM_HEAD
OWN_STATE = 2 * STATE // RANKS
OWN_CONV = OWN_SSM + OWN_STATE

bf16 = jnp.bfloat16
f32 = jnp.float32


def dot(left, right, dims=((1,), (0,))):
    return lax.dot_general(left, right, (dims, ((), ())), preferred_element_type=f32)


def dot_rows(left, right):
    return dot(left, right, ((0,), (0,)))


def dot_cols(left, right):
    return dot(left, right, ((1,), (1,)))


def bdot(left, right, lc, rc):
    return lax.dot_general(
        left, right, (((lc,), (rc,)), ((0,), (0,))), preferred_element_type=f32
    )


def hop(values, flip):
    return lax.ppermute(values, "b", [(i, i ^ flip) for i in range(ROWS)])


def twin(values):
    return lax.ppermute(values, "c", [(0, 1), (1, 0)])


def zhop(values, flip):
    return lax.ppermute(values, "z", [(i, i ^ flip) for i in range(lax.axis_size("z"))])


def zshift(values, step):
    size = lax.axis_size("z")
    return lax.ppermute(
        values, "z", [(i, i + step) for i in range(size) if 0 <= i + step < size]
    )


def gather_group(own):
    half = own.shape[0] // 2
    by_x = hop(own, 1)
    by_y = hop(own, 2)
    far = jnp.concatenate([hop(by_x[:half], 2), hop(by_y[half:], 1)], axis=0)
    mine = [own, by_x, by_y, far]
    return jnp.stack(mine + [twin(part) for part in mine]).reshape((2, ROWS) + own.shape)


def scatter_group(terms):
    half = terms.shape[2] // 2
    other = [twin(terms[1, k]) for k in range(ROWS)]
    sums = [terms[0, k].astype(f32) + other[k].astype(f32) for k in range(ROWS)]
    far = sums[3].astype(bf16)
    to_x = hop(far[:half], 2).astype(f32)
    to_y = hop(far[half:], 1).astype(f32)
    by_x = jnp.concatenate([sums[1][:half] + to_x, sums[1][half:]], axis=0).astype(bf16)
    by_y = jnp.concatenate([sums[2][:half], sums[2][half:] + to_y], axis=0).astype(bf16)
    return sums[0] + hop(by_x, 1).astype(f32) + hop(by_y, 2).astype(f32)


def reslot(values, flip, axis):
    order = [k ^ flip for k in range(ROWS)]
    return jnp.concatenate(
        [lax.slice_in_dim(values, k, k + 1, axis=axis) for k in order], axis=axis
    )


def sum_group(values):
    values = values + twin(values)
    values = values + reslot(hop(values, 1), 1, 1)
    return values + reslot(hop(values, 2), 2, 1)


def gather_all(own):
    rows = own[None]
    rows = jnp.concatenate([rows, twin(rows)], axis=0)
    for flip in (1, 2):
        rows = jnp.concatenate([rows, hop(rows, flip)], axis=0)
    flip = 1
    while flip < lax.axis_size("z"):
        rows = jnp.concatenate([rows, zhop(rows, flip)], axis=0)
        flip *= 2
    return rows


def silu_slope(values):
    sigmoid = jax.nn.sigmoid(values)
    return sigmoid * (1.0 + values * (1.0 - sigmoid))


def rms_scale(values):
    return lax.rsqrt(jnp.mean(values * values, axis=-1, keepdims=True) + EPSILON)


def rotate(values, cosine, sine):
    half = values.shape[-1] // 2
    first = values[..., :half]
    second = values[..., half:]
    return jnp.concatenate([first * cosine - second * sine, second * cosine + first * sine], axis=-1)


def per_device(
    tokens,
    segments,
    cotangent,
    norm_gain,
    gating_weight,
    input_weight,
    state_weight,
    step_weight,
    conv_weight,
    conv_bias,
    step_bias,
    decay_log,
    skip_gain,
    ssm_gain,
    out_weight,
    query_weight,
    keyval_weight,
    context_weight,
    mlp_gain,
    gate_weight,
    up_weight,
    down_weight,
):
    zs = lax.axis_size("z")
    b = lax.axis_index("b")
    z = lax.axis_index("z")
    c = lax.axis_index("c")
    rank = 2 * b + c
    rows = tokens.shape[1]
    width = tokens.shape[2]
    share = norm_gain.shape[0]
    ssm_width = HEADS * SSM_HEAD
    score_scale = 1.0 / math.sqrt(ATT_HEAD)

    def to_z(values):
        return (
            values.reshape(rows, ROWS, zs, 2 * share).transpose(0, 2, 1, 3).reshape(rows, width)
        )

    def from_z(values):
        return (
            values.reshape(rows, zs, ROWS, 2 * share).transpose(0, 2, 1, 3).reshape(rows, width)
        )

    def swap(values):
        return jnp.where(c == 0, values, values[::-1])

    def to_ranks(values):
        return lax.all_to_all(values, ("b", "c"), split_axis=0, concat_axis=0, tiled=True)

    def along_z(values):
        return lax.all_gather(values, "z", axis=0, tiled=True)

    def owner_z(values):
        return lax.psum_scatter(values, "z", scatter_dimension=0, tiled=True)

    x = tokens[0].astype(f32)
    cot = cotangent[0]
    gain_col = norm_gain.astype(f32)[:, None]
    gain2_col = mlp_gain.astype(f32)[:, None]
    ssm_gain_col = ssm_gain.astype(f32)[:, None]

    scale_one = rms_scale(x)
    unit_one = x * scale_one
    n1 = gather_group(to_z(unit_one.astype(bf16))).reshape(-1, width)
    g_all = gather_group(cot).reshape(-1, width)

    scaled = lambda w, gain: (w.astype(f32) * gain).astype(bf16)
    by_rank = lambda w: w.reshape(w.shape[0], RANKS, -1).transpose(1, 0, 2)
    group_kv = KVHEADS * ATT_HEAD
    kv_heads = keyval_weight.reshape(share, 2, KVHEADS, ATT_HEAD).transpose(2, 0, 1, 3)
    kv_rank = jnp.repeat(kv_heads.reshape(KVHEADS, share, 2 * ATT_HEAD), RANKS // KVHEADS, axis=0)
    pad_cols = 128 - OWN_STATE - OWN_HEADS
    w_a = jnp.concatenate(
        [
            by_rank(input_weight),
            by_rank(state_weight),
            by_rank(step_weight),
            jnp.zeros((RANKS, share, pad_cols), bf16),
        ],
        axis=2,
    )
    w_b = jnp.concatenate([by_rank(query_weight), kv_rank], axis=2)
    w_c = by_rank(gating_weight)
    cols_a, cols_b, cols_c = w_a.shape[2], w_b.shape[2], w_c.shape[2]
    w_abc = to_ranks(scaled(jnp.concatenate([w_a, w_b, w_c], axis=2), gain_col[None]))
    cut_b, cut_c = cols_a, cols_a + cols_b
    wa = along_z(w_abc[:, :, :cut_b]).reshape(width, cols_a)
    wb = along_z(w_abc[:, :, cut_b:cut_c]).reshape(width, cols_b)
    wc = along_z(w_abc[:, :, cut_c:]).reshape(width, cols_c)

    def ff_ranks(w):
        return (
            w.reshape(w.shape[0], ROWS, zs, 2, -1)
            .transpose(1, 3, 0, 2, 4)
            .reshape(RANKS, w.shape[0], -1)
        )

    w_gu = to_ranks(
        scaled(jnp.concatenate([ff_ranks(gate_weight), ff_ranks(up_weight)], axis=2), gain2_col[None])
    )
    own_ff = w_gu.shape[2] // 2

    row_out = out_weight.shape[0]
    row_ctx = context_weight.shape[0]
    w_oc = along_z(jnp.concatenate([scaled(out_weight, ssm_gain_col), context_weight], axis=0)[None])
    halves = w_oc.reshape(2, zs // 2, row_out + row_ctx, width)
    kept = lax.dynamic_index_in_dim(halves, c, 0, keepdims=False)
    sent = lax.dynamic_index_in_dim(halves, 1 - c, 0, keepdims=False)
    got = twin(sent)
    both = jnp.where(c == 0, jnp.stack([kept, got], 1), jnp.stack([got, kept], 1))
    w_out = both[:, :, :row_out].reshape(-1, width)
    w_ctx = both[:, :, row_out:].reshape(-1, width)

    w_gu_full = along_z(w_gu).reshape(width, 2 * own_ff)
    w_down = along_z(down_weight)

    chan = conv_bias.shape[0]
    small = gather_all(
        jnp.concatenate(
            [segments[0].astype(bf16), conv_weight.reshape(-1), conv_bias.reshape(-1)]
        )
    )
    count = small.shape[0]
    place = jnp.arange(count)
    me = c + 2 * b + 8 * z

    def pick(wanted, table):
        chosen = (wanted[:, None] == place[None, :]).astype(bf16)
        return dot(chosen, table)

    slot_rows = (place // (2 * zs)) * 2 + ((place // 2) % zs ^ z) * 8 + (place % 2 ^ c)
    segs_all = pick(slot_rows, small[:, :rows]).reshape(ROWS, zs * 2 * rows)
    plain_rows = ((place // (2 * zs)) * 2 + ((place // 2) % zs) * 8 + place % 2) ^ me
    conv_all = pick(plain_rows, small[:, rows:]).reshape(count, CONV + 1, chan)
    conv_all = conv_all.transpose(1, 0, 2).reshape(CONV + 1, count * chan)
    conv_own = jnp.concatenate(
        [
            lax.dynamic_slice_in_dim(conv_all, rank * OWN_SSM, OWN_SSM, 1),
            lax.dynamic_slice_in_dim(conv_all, ssm_width + rank * OWN_STATE, OWN_STATE, 1),
        ],
        axis=1,
    )
    conv_w, conv_b = conv_own[:CONV], conv_own[CONV]
    seg_pad = jnp.concatenate([jnp.zeros((ROWS, rows), f32), segs_all], axis=1)
    seg_near = lax.dynamic_slice_in_dim(seg_pad, z * 2 * rows, 3 * rows, 1)
    seg = seg_near[:, rows:].reshape(ROWS, 2, rows).transpose(1, 0, 2)
    seg_before = seg_near[:, : 2 * rows].reshape(ROWS, 2, rows).transpose(1, 0, 2)

    proj_a = swap(dot(n1, wa).reshape(2, ROWS, rows, cols_a))
    proj_b = swap(dot(n1, wb).reshape(2, ROWS, rows, cols_b))
    gating = swap(dot(n1, wc).reshape(2, ROWS, rows, cols_c))

    mixed = proj_a[..., :OWN_CONV].astype(bf16)
    step_raw = proj_a[..., OWN_CONV : OWN_CONV + OWN_HEADS]
    tails = mixed[:, :, rows - CONV + 1 :]
    before = jnp.stack([zshift(tails[1], 1), tails[0]])
    extended = jnp.concatenate([before, mixed], axis=2).astype(f32)
    seg_ext = jnp.concatenate([seg_before[:, :, rows - CONV + 1 :], seg], axis=2)
    tap_masks = [
        (seg_ext[:, :, o : o + rows] == seg).astype(f32)[..., None] for o in range(CONV)
    ]
    conv_pre = conv_b
    for o in range(CONV):
        conv_pre = conv_pre + conv_w[o] * extended[:, :, o : o + rows] * tap_masks[o]
    activated = jax.nn.silu(conv_pre).astype(bf16)
    chunks = 2 * ROWS
    xs = activated[..., :OWN_SSM].reshape(chunks, rows, OWN_SSM)
    bc = gather_group(activated[..., OWN_SSM:].reshape(2 * ROWS * rows, OWN_STATE))
    bc = bc.reshape(2, ROWS, 2, ROWS, rows, OWN_STATE)

    def joined(slots):
        parts = [reslot(bc[r, m], m, 1) for m in slots for r in range(2)]
        return jnp.concatenate(parts, axis=-1).reshape(chunks, rows, STATE)

    low_half, high_half = joined((0, 1)), joined((2, 3))
    b_mat = jnp.where(b < 2, low_half, high_half)
    c_mat = jnp.where(b < 2, high_half, low_half)

    own_slice = lambda v: lax.dynamic_slice_in_dim(v.astype(f32), rank * OWN_HEADS, OWN_HEADS, 0)
    step_b = own_slice(step_bias)
    rate = -jnp.exp(own_slice(decay_log))
    skip = own_slice(skip_gain)
    skip_wide = jnp.repeat(skip, SSM_HEAD)
    step_in = (step_raw + step_b).reshape(chunks, rows, OWN_HEADS)
    step = jax.nn.softplus(step_in)
    index = jnp.arange(rows)
    lower = (index[:, None] >= index[None, :])
    lower_f = lower.astype(f32)
    cumulative = jnp.einsum("ts,qsh->qth", lower_f, step * rate, precision=HIGH)
    seg_q = seg.reshape(chunks, rows)
    allowed = (seg_q[:, :, None] == seg_q[:, None, :]) & lower[None]
    cum_h = cumulative.transpose(0, 2, 1)
    decays = jnp.where(
        allowed[:, None],
        jnp.exp(jnp.where(allowed[:, None], cum_h[..., None] - cum_h[:, :, None, :], 0.0)),
        0.0,
    )
    inner = bdot(c_mat, b_mat, 2, 2)
    step_h = step.transpose(0, 2, 1)[:, :, None, :]
    mix = (inner[:, None] * decays * step_h).astype(bf16)
    xs_h = xs.reshape(chunks, rows, OWN_HEADS, SSM_HEAD)
    within = jnp.einsum("qhts,qshp->qthp", mix, xs_h, preferred_element_type=f32)
    within = within.reshape(chunks, rows, OWN_SSM)
    wide = lambda v: jnp.repeat(v, SSM_HEAD, axis=-1)
    per_head = lambda v: v.reshape(v.shape[:-1] + (OWN_HEADS, SSM_HEAD)).sum(-1)
    last_before = seg_before[:, :, rows - 1].reshape(chunks, 1)
    carried = (seg_q == last_before).astype(f32)
    entry = jnp.exp(cumulative) * carried[..., None]
    ending = (seg_q == seg_q[:, rows - 1 :]).astype(f32)
    cum_last = cumulative[:, rows - 1 :]
    tail_decay = jnp.exp(cum_last - cumulative) * ending[..., None]
    tail = tail_decay * step
    xs_f = xs.astype(f32)
    weighted = (xs_f * wide(tail)).astype(bf16)
    local = bdot(weighted, b_mat, 1, 1).reshape(2, ROWS, OWN_SSM, STATE)
    passing = (jnp.exp(cum_last[:, 0]) * carried[:, rows - 1 :]).reshape(2, ROWS, OWN_HEADS)
    pass_wide = wide(passing)[..., None]
    pass_both = pass_wide[0] * pass_wide[1]
    local_both = pass_wide[1] * local[0] + local[1]
    state = jnp.zeros_like(local[0])
    for s in range(zs - 1):
        message = (pass_both * state + local_both).astype(bf16)
        state = state + lax.ppermute(message, "z", [(s, s + 1)]).astype(f32)
    state_in = jnp.stack([state, pass_wide[0] * state + local[0]]).reshape(chunks, OWN_SSM, STATE)
    state_low = state_in.astype(bf16)
    inter = bdot(c_mat, state_low, 2, 2)
    entry_wide = wide(entry)
    ssm_out = within + inter * entry_wide + skip_wide * xs_f
    gating_q = gating.reshape(chunks, rows, OWN_SSM)
    gate_act = jax.nn.silu(gating_q)
    gated = ssm_out * gate_act

    squares = sum_group(jnp.sum(gated * gated, axis=-1).reshape(2, ROWS, rows))
    scale_ssm = lax.rsqrt(squares * (1.0 / ssm_width) + EPSILON).reshape(chunks, rows, 1)
    unit_ssm = gated * scale_ssm
    unit_low = unit_ssm.astype(bf16)

    places = (z * 2 * rows + jnp.arange(2 * rows, dtype=jnp.int32)).astype(f32)
    half_head = ATT_HEAD // 2
    frequency = jnp.exp(jnp.arange(half_head, dtype=f32) * (-2.0 * math.log(ROPE_BASE) / ATT_HEAD))
    angles = (places[:, None] * frequency[None, :]).reshape(2, 1, rows, half_head)
    cosine, sine = jnp.cos(angles), jnp.sin(angles)
    by_seq = lambda v: v.transpose(1, 0, 2, 3).reshape(ROWS, 2 * rows, v.shape[-1])
    from_seq = lambda v: v.reshape(ROWS, 2, rows, v.shape[-1]).transpose(1, 0, 2, 3)
    query = by_seq(rotate(proj_b[..., :ATT_HEAD], cosine, sine).astype(bf16))
    key = rotate(proj_b[..., ATT_HEAD : 2 * ATT_HEAD], cosine, sine).astype(bf16)
    keyval = by_seq(jnp.concatenate([key, proj_b[..., 2 * ATT_HEAD :].astype(bf16)], axis=-1))
    own_kv = lax.dynamic_slice_in_dim(keyval, 2 * c, 2, 0)
    kv_parts = [own_kv] + [zhop(own_kv, m) for m in range(1, zs)]
    kv_own = jnp.stack(kv_parts, axis=1)
    kv_other = twin(kv_own)
    kv_all = jnp.where(
        c == 0,
        jnp.concatenate([kv_own, kv_other], axis=0),
        jnp.concatenate([kv_other, kv_own], axis=0),
    ).reshape(ROWS, zs * 2 * rows, 2 * ATT_HEAD)
    key_all, val_all = kv_all[..., :ATT_HEAD], kv_all[..., ATT_HEAD:]
    key_place = ((jnp.arange(zs) ^ z)[:, None] * 2 * rows + jnp.arange(2 * rows)[None, :]).reshape(-1)
    seg_keys = jnp.concatenate(
        [lax.dynamic_slice_in_dim(segs_all, (m ^ z) * 2 * rows, 2 * rows, 1) for m in range(zs)],
        axis=1,
    )
    seg_query = seg_near[:, rows:]
    seen = (seg_query[:, :, None] == seg_keys[:, None, :]) & (
        places.astype(jnp.int32)[None, :, None] >= key_place[None, None, :]
    )
    scores = jnp.where(seen, bdot(query, key_all, 2, 2) * score_scale, NEG_BIG)
    highest = jnp.max(scores, axis=-1, keepdims=True)
    exponent = jnp.where(seen, jnp.exp(scores - highest), 0.0)
    total = jnp.sum(exponent, axis=-1, keepdims=True)
    context = bdot(exponent.astype(bf16), val_all, 2, 1) / total
    logsum = highest + jnp.log(total)
    context_low = context.astype(bf16)

    mixer_in = jnp.concatenate(
        [unit_low.reshape(2, ROWS, rows, OWN_SSM), from_seq(context_low)], axis=-1
    )
    mixer_in = swap(mixer_in).reshape(-1, OWN_SSM + ATT_HEAD)
    w_mix = jnp.concatenate([w_out, w_ctx], axis=0)
    terms = dot(mixer_in, w_mix).astype(bf16)
    hidden = x + scatter_group(terms.reshape(2, ROWS, rows, width))

    scale_two = rms_scale(hidden)
    unit_two = hidden * scale_two
    n2 = gather_group(to_z(unit_two.astype(bf16))).reshape(-1, width)
    gate_up = dot(n2, w_gu_full)
    gate_pre, up_pre = gate_up[:, :own_ff], gate_up[:, own_ff:]
    gate_silu = jax.nn.silu(gate_pre)
    activation = (gate_silu * up_pre).astype(bf16)
    down_terms = dot(activation, w_down).astype(bf16)
    result = (hidden + scatter_group(down_terms.reshape(2, ROWS, rows, width))).astype(bf16)

    grad_down = owner_z(dot_rows(activation, g_all).astype(bf16))
    grad_act = dot_cols(g_all, w_down)
    grad_gate = (grad_act * up_pre * silu_slope(gate_pre)).astype(bf16)
    grad_up = (grad_act * gate_silu).astype(bf16)
    grad_gu = jnp.concatenate([grad_gate, grad_up], axis=1)
    grad_gu_w = owner_z(dot_rows(n2, grad_gu).astype(bf16)).reshape(RANKS, share, 2 * own_ff)
    e2_terms = dot_cols(grad_gu, w_gu_full).astype(bf16)
    e2 = from_z(scatter_group(e2_terms.reshape(2, ROWS, rows, width)))
    grad_hidden = cot.astype(f32) + scale_two * (
        e2 - unit_two * jnp.mean(e2 * unit_two, axis=-1, keepdims=True)
    )
    grad_mix = gather_group(grad_hidden.astype(bf16)).reshape(-1, width)

    grad_oc_w = dot_rows(mixer_in, grad_mix).astype(bf16)
    grad_out_rows = grad_oc_w[:OWN_SSM].reshape(zs // 2, 2, row_out, width)
    grad_ctx_rows = grad_oc_w[OWN_SSM:].reshape(zs // 2, 2, row_ctx, width)
    grad_oc = jnp.concatenate([grad_out_rows, grad_ctx_rows], axis=2)
    oc_kept = lax.dynamic_index_in_dim(grad_oc, c, 1, keepdims=False)
    oc_got = twin(lax.dynamic_index_in_dim(grad_oc, 1 - c, 1, keepdims=False))
    oc_all = jnp.where(
        c == 0,
        jnp.concatenate([oc_kept, oc_got], axis=0),
        jnp.concatenate([oc_got, oc_kept], axis=0),
    )
    grad_oc_own = owner_z(oc_all)[0].astype(f32)
    grad_mixer = swap(dot_cols(grad_mix, w_mix).reshape(2, ROWS, rows, OWN_SSM + ATT_HEAD))
    es = grad_mixer[..., :OWN_SSM].reshape(chunks, rows, OWN_SSM)
    grad_context = by_seq(grad_mixer[..., OWN_SSM:].astype(bf16))

    es_sum = sum_group(jnp.sum(es * unit_ssm, axis=-1).reshape(2, ROWS, rows))
    es_mean = (es_sum * (1.0 / ssm_width)).reshape(chunks, rows, 1)
    grad_gated = scale_ssm * (es - unit_ssm * es_mean)
    gy = (grad_gated * gate_act).astype(bf16)
    grad_gating = (grad_gated * ssm_out * silu_slope(gating_q)).astype(bf16)
    to_rel = lambda v: swap(v.reshape(2, ROWS, rows, v.shape[-1])).reshape(-1, v.shape[-1])
    grad_c_low = to_rel(grad_gating)
    grad_wc = owner_z(dot_rows(n1, grad_c_low).astype(bf16)).reshape(RANKS, share, cols_c)

    delta = jnp.sum(grad_context.astype(f32) * context, axis=-1, keepdims=True)
    prob = jnp.where(seen, jnp.exp(jnp.where(seen, scores - logsum, NEG_BIG)), 0.0)
    grad_prob = bdot(grad_context, val_all, 2, 2)
    grad_scores = (prob * (grad_prob - delta)).astype(bf16)
    grad_query = bdot(grad_scores, key_all, 2, 1) * score_scale
    grad_key = bdot(grad_scores, query, 1, 1) * score_scale
    grad_val = bdot(prob.astype(bf16), grad_context, 1, 1)
    grad_kv = jnp.concatenate([grad_key, grad_val], axis=-1).astype(bf16)
    grad_kv = grad_kv.reshape(2, 2, zs, 2 * rows, 2 * ATT_HEAD)
    kv_kept = lax.dynamic_index_in_dim(grad_kv, c, 0, keepdims=False).astype(f32)
    kv_got = twin(lax.dynamic_index_in_dim(grad_kv, 1 - c, 0, keepdims=False)).astype(f32)
    kv_sum = kv_kept + kv_got
    kv_low = kv_sum.astype(bf16)
    kv_grad = kv_sum[:, 0]
    for m in range(1, zs):
        kv_grad = kv_grad + zhop(kv_low[:, m], m).astype(f32)
    zero_kv = jnp.zeros_like(kv_grad)
    kv_grad = jnp.where(
        c == 0,
        jnp.concatenate([kv_grad, zero_kv], axis=0),
        jnp.concatenate([zero_kv, kv_grad], axis=0),
    )
    kv_grad = from_seq(kv_grad)
    grad_b_low = jnp.concatenate(
        [
            rotate(from_seq(grad_query), cosine, -sine),
            rotate(kv_grad[..., :ATT_HEAD], cosine, -sine),
            kv_grad[..., ATT_HEAD:],
        ],
        axis=-1,
    ).astype(bf16)
    grad_b_low = to_rel(grad_b_low)
    grad_wb = owner_z(dot_rows(n1, grad_b_low).astype(bf16)).reshape(RANKS, share, cols_b)

    gy_f = gy.astype(f32)
    gy_h = gy.reshape(chunks, rows, OWN_HEADS, SSM_HEAD)
    grad_skip = per_head(jnp.sum(gy_f * xs_f, axis=(0, 1)))
    grad_mixw = jnp.einsum("qthp,qshp->qhts", gy_h, xs_h, preferred_element_type=f32)
    grad_xs = skip_wide * gy_f + jnp.einsum(
        "qhts,qthp->qshp", mix, gy_h, preferred_element_type=f32
    ).reshape(chunks, rows, OWN_SSM)
    product = grad_mixw * decays
    grad_inner = jnp.sum(product * step_h, axis=1).astype(bf16)
    flow = product * inner[:, None]
    step_grad = jnp.sum(flow, axis=2).transpose(0, 2, 1)
    flow = flow * step_h
    grad_cum = (jnp.sum(flow, axis=3) - jnp.sum(flow, axis=2)).transpose(0, 2, 1)
    grad_c = bdot(grad_inner, b_mat, 2, 1)
    grad_b = bdot(grad_inner, c_mat, 1, 1)
    across = (gy_f * entry_wide).astype(bf16)
    grad_c = grad_c + bdot(across, state_low, 2, 1)
    grad_local = bdot(across, c_mat, 1, 1).reshape(2, ROWS, OWN_SSM, STATE)
    grad_cum = grad_cum + per_head(gy_f * inter) * entry
    back_both = pass_wide[0] * grad_local[1] + grad_local[0]
    flowing = jnp.zeros_like(back_both)
    for s in range(zs - 1, 0, -1):
        message = (pass_both * flowing + back_both).astype(bf16)
        flowing = flowing + lax.ppermute(message, "z", [(s, s - 1)]).astype(f32)
    outgoing = jnp.stack([pass_wide[1] * flowing + grad_local[1], flowing])
    outgoing = outgoing.reshape(chunks, OWN_SSM, STATE)
    out_low = outgoing.astype(bf16)
    grad_pass = jnp.sum((outgoing * state_in).reshape(chunks, OWN_HEADS, -1), axis=-1)
    grad_weighted = bdot(b_mat, out_low, 2, 2)
    grad_b = grad_b + bdot(weighted, out_low, 2, 1)
    grad_xs = grad_xs + grad_weighted * wide(tail)
    grad_tail = per_head(grad_weighted * xs_f)
    tail_flow = grad_tail * tail
    step_grad = step_grad + grad_tail * tail_decay
    is_last = (index == rows - 1).astype(f32)[None, :, None]
    end_term = grad_pass * passing.reshape(chunks, OWN_HEADS) + jnp.sum(tail_flow, axis=1)
    grad_cum = grad_cum - tail_flow + is_last * end_term[:, None]
    grad_rate = jnp.einsum("st,qsh->qth", lower_f, grad_cum, precision=HIGH)
    step_grad = step_grad + grad_rate * rate
    grad_decay = jnp.sum(grad_rate * step, axis=(0, 1)) * rate
    grad_step_raw = step_grad * jax.nn.sigmoid(step_in)
    grad_step_bias = jnp.sum(grad_step_raw, axis=(0, 1))

    low_grad = jnp.where(b < 2, grad_b, grad_c).reshape(2, ROWS, rows, 4, OWN_STATE)
    high_grad = jnp.where(b < 2, grad_c, grad_b).reshape(2, ROWS, rows, 4, OWN_STATE)
    bc_terms = [[None] * ROWS, [None] * ROWS]
    for m in range(ROWS):
        source = low_grad if m < 2 else high_grad
        for r in range(2):
            piece = reslot(source[..., 2 * (m % 2) + r, :], m, 1)
            bc_terms[r][m] = piece.reshape(-1, OWN_STATE).astype(bf16)
    grad_bc = scatter_group(jnp.stack([jnp.stack(bc_terms[0]), jnp.stack(bc_terms[1])]))
    grad_act_in = jnp.concatenate(
        [grad_xs.reshape(2, ROWS, rows, OWN_SSM), grad_bc.reshape(2, ROWS, rows, OWN_STATE)],
        axis=-1,
    )

    grad_pre = grad_act_in * silu_slope(conv_pre)
    conv_sums = []
    grad_ext = jnp.zeros((2, ROWS, rows + CONV - 1, OWN_CONV), f32)
    for o in range(CONV):
        masked = grad_pre * tap_masks[o]
        conv_sums.append(jnp.sum(masked * extended[:, :, o : o + rows], axis=(0, 1, 2)))
        grad_ext = grad_ext + jnp.pad(
            masked * conv_w[o], ((0, 0), (0, 0), (o, CONV - 1 - o), (0, 0))
        )
    conv_sums.append(jnp.sum(grad_pre, axis=(0, 1, 2)))
    head_sums = jnp.concatenate([grad_step_bias, grad_decay, grad_skip])
    conv_sums.append(jnp.pad(head_sums, (0, OWN_CONV - head_sums.shape[0])))
    first = grad_ext[:, :, : CONV - 1]
    returned = jnp.stack([first[1], zshift(first[0].astype(bf16), -1).astype(f32)])
    grad_mixed = grad_ext[:, :, CONV - 1 :] + jnp.pad(
        returned, ((0, 0), (0, 0), (rows - CONV + 1, 0), (0, 0))
    )
    grad_a_low = jnp.concatenate(
        [
            grad_mixed.astype(bf16),
            grad_step_raw.reshape(2, ROWS, rows, OWN_HEADS).astype(bf16),
            jnp.zeros((2, ROWS, rows, pad_cols), bf16),
        ],
        axis=-1,
    )
    grad_a_low = to_rel(grad_a_low)
    grad_wa = owner_z(dot_rows(n1, grad_a_low).astype(bf16)).reshape(RANKS, share, cols_a)

    e1_terms = (
        dot_cols(grad_c_low, wc) + dot_cols(grad_b_low, wb) + dot_cols(grad_a_low, wa)
    ).astype(bf16)
    e1 = from_z(scatter_group(e1_terms.reshape(2, ROWS, rows, width)))
    grad_x = grad_hidden + scale_one * (
        e1 - unit_one * jnp.mean(e1 * unit_one, axis=-1, keepdims=True)
    )

    def from_ranks(values):
        return to_ranks(values).astype(f32)

    def unrank(values):
        return values.transpose(1, 0, 2).reshape(share, -1)

    got_a = from_ranks(grad_wa)
    got_b = from_ranks(grad_wb)
    got_c = from_ranks(grad_wc)
    got_gu = from_ranks(grad_gu_w)
    d_input = unrank(got_a[..., :OWN_SSM])
    d_state = unrank(got_a[..., OWN_SSM:OWN_CONV])
    d_step = unrank(got_a[..., OWN_CONV : OWN_CONV + OWN_HEADS])
    d_query = unrank(got_b[..., :ATT_HEAD])
    d_kv = got_b[..., ATT_HEAD:].reshape(KVHEADS, RANKS // KVHEADS, share, 2, ATT_HEAD).sum(1)
    d_kv = d_kv.transpose(1, 2, 0, 3).reshape(share, 2 * group_kv)
    d_gating = unrank(got_c)

    def ff_unrank(values):
        return (
            values.reshape(ROWS, 2, share, zs, own_ff // zs)
            .transpose(2, 0, 3, 1, 4)
            .reshape(share, -1)
        )

    d_gate, d_up = ff_unrank(got_gu[..., :own_ff]), ff_unrank(got_gu[..., own_ff:])

    def gain_grad(pairs):
        return sum(jnp.sum(w.astype(f32) * d, axis=1) for w, d in pairs)

    d_norm_gain = gain_grad(
        (
            (gating_weight, d_gating),
            (input_weight, d_input),
            (state_weight, d_state),
            (step_weight, d_step),
            (query_weight, d_query),
            (keyval_weight, d_kv),
        )
    )
    d_mlp_gain = gain_grad(((gate_weight, d_gate), (up_weight, d_up)))
    d_out = grad_oc_own[:row_out]
    d_ctx = grad_oc_own[row_out:]
    d_ssm_gain = gain_grad(((out_weight, d_out),))

    sums = jnp.stack(conv_sums)
    flip = 1
    while flip < zs:
        sums = sums + zhop(sums, flip)
        flip *= 2
    table = sums[None]
    table = jnp.concatenate([table, twin(table)], axis=0)
    for flip in (1, 2):
        table = jnp.concatenate([table, hop(table, flip)], axis=0)
    place = jnp.arange(RANKS)
    chosen = ((place ^ rank)[:, None] == place[None, :]).astype(f32)
    table = jnp.einsum("rs,sof->rof", chosen, table, precision=HIGH)
    conv_ssm = table[:, : CONV + 1, :OWN_SSM].transpose(1, 0, 2).reshape(CONV + 1, -1)
    conv_state = table[:, : CONV + 1, OWN_SSM:].transpose(1, 0, 2).reshape(CONV + 1, -1)
    conv_full = jnp.concatenate([conv_ssm, conv_state], axis=1)
    conv_mine = lax.dynamic_slice_in_dim(conv_full, (rank // 2 * zs * 2 + z * 2 + c) * chan, chan, 1)
    heads = table[:, CONV + 1, : 3 * OWN_HEADS].reshape(RANKS, 3, OWN_HEADS)
    heads = heads.transpose(1, 0, 2).reshape(3, HEADS)

    return (
        result[None],
        grad_x.astype(bf16)[None],
        d_norm_gain,
        d_gating * gain_col,
        d_input * gain_col,
        d_state * gain_col,
        d_step * gain_col,
        conv_mine[:CONV],
        conv_mine[CONV],
        heads[0],
        heads[1],
        heads[2],
        d_ssm_gain,
        d_out * ssm_gain_col,
        d_query * gain_col,
        d_kv * gain_col,
        d_ctx,
        d_mlp_gain,
        d_gate * gain2_col,
        d_up * gain2_col,
        grad_down.astype(f32),
    )


def solution(mesh):
    places = mesh.devices.reshape(ROWS, mesh.shape["seq"] // 2, 2)
    split = Mesh(places, ("b", "z", "c"))
    everywhere = ("b", "z", "c")
    row = P(everywhere, None)
    vector = P(everywhere)
    token = P("b", ("z", "c"), None)
    return jax.shard_map(
        per_device,
        mesh=split,
        in_specs=(
            token,
            P("b", ("z", "c")),
            token,
            vector,
            row,
            row,
            row,
            row,
            P(None, everywhere),
            vector,
            P(),
            P(),
            P(),
            vector,
            row,
            row,
            row,
            row,
            vector,
            row,
            row,
            row,
        ),
        out_specs=(
            token,
            token,
            vector,
            row,
            row,
            row,
            row,
            P(None, everywhere),
            vector,
            P(),
            P(),
            P(),
            vector,
            row,
            row,
            row,
            row,
            vector,
            row,
            row,
            row,
        ),
        check_vma=False,
    )
```

time: 4050 us -> 1290 us (0.32)
  waiting for transfers between devices: 3160 us -> 300 us
  local copies, waits for them, and re-layouts: 112 us -> 318 us
  blocking collectives: 185 us -> 41.7 us
  starting transfers between devices: 7.6 us -> 142 us
  matrix products: 373 us -> 272 us
    reduce_scatter x11 -> x6, waiting for transfers between devices: 2430 us -> 0.03 us  [owner_z(): return lax.psum_scatter(values, 'z', scatter_dimension=0, tiled=True)]
    all_gather x14 -> x6, waiting for transfers between devices: 667 us -> 0.05 us  [along_z(): return lax.all_gather(values, 'z', axis=0, tiled=True)]
    ppermute x3 -> x114, waiting for transfers between devices: 1.8 us -> 285 us  [the longest x48 211 us: hop(): return lax.ppermute(values, 'b', [(i, i ^ flip) for i in range(ROWS)])]
    ppermute x3 -> x114, starting transfers between devices: 5.63 us -> 126 us  [the longest x48 49.6 us: hop(): return lax.ppermute(values, 'b', [(i, i ^ flip) for i in range(ROWS)])]
    all_gather x4 -> x0, blocking collectives: 100 us -> none  [the longest x1 41.3 us: per_device(): lax.all_gather(step_weight, ('batch', 'seq'), axis=0, tiled=True)]
    dot_general x72 -> x41, matrix products: 372 us -> 272 us  [the longest x20 176 us: dot(): lax.dot_general(left, right, (dims, ((), ())), preferred_element_type=f32)]
    unnamed x306 -> x515, local copies, waits for them, and re-layouts: 36.3 us -> 128 us
    unnamed x2 -> x0, blocking collectives: 85.1 us -> none
  transfers between devices with their start and end apart: 30 -> 130, of which waited for: 24 -> 44; matrix products, arithmetic and copies ran while one was open for 14% -> 54% of each run, Pallas kernels for 0% -> 0%
where the time goes in v1:
time: 1290 us; the launch traced here: 1280 us
  local copies, waits for them, and re-layouts  318 us (25%)
  waiting for transfers between devices  300 us (23%)
  matrix products  272 us (21%)
  other arithmetic  185 us (14%)
  starting transfers between devices  142 us (11%)
  blocking collectives  41.7 us (3%)
  between operations  18.7 us (1%)
    ppermute x48, waiting for transfers between devices, hop(): return lax.ppermute(values, 'b', [(i, i ^ flip) for i in range(ROWS)])  211 us
    dot_general x20, matrix products, dot(): lax.dot_general(left, right, (dims, ((), ())), preferred_element_type=f32)  176 us
    unnamed x515, local copies, waits for them, and re-layouts  128 us
    dot_general x15, matrix products, bdot(): lax.dot_general(left, right, (((lc,), (rc,)), ((0,), (0,))), preferred_el...  74.8 us
    ppermute x48, starting transfers between devices, hop(): return lax.ppermute(values, 'b', [(i, i ^ flip) for i in range(ROWS)])  49.6 us
    all_to_all x2, blocking collectives, to_ranks(): lax.all_to_all(values, ('b', 'c'), split_axis=0, concat_axis=0, tiled=True)  41.7 us
    another operation x9, local copies, waits for them, and re-layouts, gather_group(): jnp.stack(mine + [twin(part) for part in mine])  41.7 us
    ppermute x10, starting transfers between devices, zhop(): lax.ppermute(values, 'z', [(i, i ^ flip) for i in range(lax.axis_size('z'...  37.9 us
  transfers between devices with their start and end apart: 130, of which 44 were waited for; matrix products, arithmetic and copies ran while one was open for 54% of the time, Pallas kernels for 0%

profile of v1, /device:TPU:0, one launch (start us, length us, event | category | flops | bytes accessed | tf_op | source)
XLA Modules:
  0.0 1278.2 jit_solution(11465868187421429728)
XLA Ops:
  17.3 23.3 %all_to_all.30 = bf16[8,64,1280]{2,1,0:T(8,128)(2,1)S(1)} all-to-all(bf16[8,64,1280]{2,1,0:T(8,128)(2,1)S(1)} %copy.785), channel_id=1, replica_groups=mesh['b'=4,'z'=4,'c'=2] {'b','c'}, dimensions={0} | all-to-all | bytes 2621440 | tf_op jit(solution)/shard_map/all_to_all | solution.py:180
  45.0 18.5 %all_to_all.31 = bf16[8,64,1024]{2,1,0:T(8,128)(2,1)} all-to-all(bf16[8,64,1024]{2,1,0:T(8,128)(2,1)S(1)} %multiply_convert_fusion.12), channel_id=1, replica_groups=mesh['b'=4,'z'=4,'c'=2] {'b','c'}, dimensions={0} | all-to-all | bytes 2097152 | tf_op jit(solution)/shard_map/all_to_all | solution.py:180
  91.4 20.6 %collective-permute-done.2 = bf16[4,816]{1,0:T(4,128)(2,1)S(1)} collective-permute-done((bf16[4,816]{1,0:T(4,128)(2,1)S(1)}, bf16[4,816]{1,0:T(4,128)(2,1)S(1)}, u32[]{:S(2)}, u32[]{:S(2)}) %collective-permute-start.2) | collective-permute-done | bytes 6560 | tf_op jit(solution)/shard_map/ppermute | solution.py:51
  130.8 18.7 %collective-permute-done.5 = bf16[256,2048]{1,0:T(8,128)(2,1)S(1)} collective-permute-done((bf16[256,2048]{1,0:T(8,128)(2,1)}, bf16[256,2048]{1,0:T(8,128)(2,1)S(1)}, u32[]{:S(2)}, u32[]{:S(2)}) %collective-permute-start.5) | collective-permute-done | bytes 1048608 | tf_op jit(solution)/shard_map/ppermute | solution.py:51
  202.5 17.7 %collective-permute-done.13 = bf16[4,3,448]{2,1,0:T(4,128)(2,1)S(1)} collective-permute-done((bf16[4,3,448]{2,1,0:T(4,128)(2,1)S(1)}, bf16[4,3,448]{2,1,0:T(4,128)(2,1)S(1)}, u32[]{:S(2)}, u32[]{:S(2)}) %collective-permute-start.13) | collective-permute-done | bytes 10784 | tf_op jit(solution)/shard_map/ppermute | solution.py:64
  279.5 17.4 %collective-permute-start.22 = (bf16[4,384,256]{1,2,0:T(8,128)(2,1)}, bf16[4,384,256]{1,2,0:T(8,128)(2,1)S(1)}, u32[]{:S(2)}, u32[]{:S(2)}) collective-permute-start(bf16[4,384,256]{1,2,0:T(8,128)(2,1)} %get-tuple-element.171), channel_id=1, source_target_pairs={{0,2},{1,3},{8,10},{9,11},{16,18},{17,19},{24,26},{25,27}} | collective-permute-start | bytes 2359304 | tf_op jit(solution)/shard_map/ppermute | solution.py:355
  309.0 13.5 %collective-permute-done.22 = bf16[4,384,256]{1,2,0:T(8,128)(2,1)S(1)} collective-permute-done((bf16[4,384,256]{1,2,0:T(8,128)(2,1)}, bf16[4,384,256]{1,2,0:T(8,128)(2,1)S(1)}, u32[]{:S(2)}, u32[]{:S(2)}) %collective-permute-start.22) | collective-permute-done | bytes 786464 | tf_op jit(solution)/shard_map/ppermute | solution.py:355
  441.7 10.4 collective-permute-done.39
  465.8 11.7 collective-permute-done.40
  490.1 11.4 copy.845
  527.8 11.5 copy.832
  539.3 14.8 %fusion.224 = f32[2048,1024]{0,1:T(8,128)} fusion(bf16[2048,2048]{1,0:T(8,128)(2,1)} %bitcast.702, bf16[2048,1024]{1,0:T(8,128)(2,1)} %bitcast.854), kind=kOutput, calls=%fused_computation.623 | convolution fusion | flops 8589934592 | bytes 20971520 | tf_op jit(solution)/shard_map/dot_general | solution.py:33
  554.1 14.4 %multiply_convert_fusion.6 = (bf16[2048,512]{0,1:T(8,128)(2,1)S(1)}, bf16[2048,512]{0,1:T(8,128)(2,1)}, bf16[2048,512]{0,1:T(8,128)(2,1)}) fusion(f32[2048,1024]{0,1:T(8,128)} %fusion.224, bf16[2048,2048]{1,0:T(8,128)(2,1)} %bitcast.704, bf16[512,2048]{1,0:T(8,128)(2,1)} %all-gather.16.cloned.1.call-done), kind=kOutput, calls=%fused_computation.55 | convolution fusion | flops 4310695936 | bytes 25165824 | tf_op jit(solution)/shard_map/dot_general | solution.py:33
  568.5 11.4 convolution_convert_fusion
  589.8 12.2 collective-permute-done.71
  604.7 22.2 %collective-permute-done.72 = bf16[256,2048]{1,0:T(8,128)(2,1)S(1)} collective-permute-done((bf16[256,2048]{1,0:T(8,128)(2,1)S(1)}, bf16[256,2048]{1,0:T(8,128)(2,1)S(1)}, u32[]{:S(2)}, u32[]{:S(2)}) %collective-permute-start.72) | collective-permute-done | bytes 1048608 | tf_op jit(solution)/shard_map/ppermute | solution.py:51
  652.6 12.8 %collective-permute-done.74 = bf16[256,2048]{0,1:T(8,128)(2,1)S(1)} collective-permute-done((bf16[256,2048]{0,1:T(8,128)(2,1)S(1)}, bf16[256,2048]{0,1:T(8,128)(2,1)S(1)}, u32[]{:S(2)}, u32[]{:S(2)}) %collective-permute-start.74) | collective-permute-done | bytes 1048608 | tf_op jit(solution)/shard_map/ppermute | solution.py:51
  734.3 13.9 %convolution_convert_fusion.3 = bf16[2048,1024]{1,0:T(8,128)(2,1)} fusion(bf16[2048,2048]{1,0:T(8,128)(2,1)} %bitcast.703, bf16[2048,512]{0,1:T(8,128)(2,1)} %get-tuple-element.182, bf16[2048,512]{0,1:T(8,128)(2,1)} %copy-done.215), kind=kOutput, calls=%fused_computation.66 | convolution fusion | flops 8600420352 | bytes 16777216 | tf_op jit(solution)/shard_map/dot_general | solution.py:33
  764.1 11.8 collective-permute-done.55
  782.0 12.4 copy.847
  806.2 12.8 multiply_convert_fusion
  832.2 11.6 fusion.30
  859.6 10.2 multiply_reduce_fusion.2
  883.7 12.3 fusion.225
  909.2 24.5 %collective-permute-start.85 = (bf16[2,512,256]{2,1,0:T(8,128)(2,1)}, bf16[2,512,256]{2,1,0:T(8,128)(2,1)}, u32[]{:S(2)}, u32[]{:S(2)}) collective-permute-start(bf16[2,512,256]{2,1,0:T(8,128)(2,1)} %get-tuple-element.247), channel_id=1, source_target_pairs={{0,2},{2,0},{4,6},{6,4},{1,3},{3,1},{5,7},{7,5},{8,10},{10,8},{12,... | collective-permute-start | bytes 1572872 | tf_op jit(solution)/shard_map/ppermute | solution.py:59
  935.6 23.3 %collective-permute-done.90 = bf16[4,384,256]{1,2,0:T(8,128)(2,1)} collective-permute-done((bf16[4,384,256]{1,2,0:T(8,128)(2,1)}, bf16[4,384,256]{1,2,0:T(8,128)(2,1)}, u32[]{:S(2)}, u32[]{:S(2)}) %collective-permute-start.90) | collective-permute-done | bytes 786464 | tf_op jit(solution)/shard_map/ppermute | solution.py:520
  981.1 9.3 fusion.16
  1072.7 9.5 convolution_convert_fusion.7
  1101.7 16.6 %add_convert_fusion = bf16[2048,2048]{1,0:T(8,128)(2,1)} fusion(f32[2048,2048]{1,0:T(8,128)} %fusion.227, f32[2048,2048]{1,0:T(8,128)} %fusion.225, bf16[2048,384]{1,0:T(8,128)(2,1)S(1)} %bitcast.716, bf16[2048,384]{1,0:T(8,128)(2,1)S(1)} %bitcast.768), kind=kOutput, calls=%fused_computation | convolution fusion | flops 3233808384 | bytes 45088768 | tf_op jit(solution)/shard_map/dot_general | solution.py:33
  1118.9 9.8 convolution_convert_fusion.6
  1187.9 10.4 collective-permute-done.103
  1206.5 10.0 collective-permute-done.107
  (1189 shorter events, 798.3 us)
Async XLA Ops:
  7.2 158.3 %all-gather.18.cloned.1.call-start = ((), (), s32[]{:S(2)}) async-start(), calls=%async_computation.23 | async-start | bytes 2621440 | tf_op jit(solution)/shard_map/all_gather | solution.py:183
  11.4 157.7 %all-gather.12.cloned.1.call-start = ((), (), s32[]{:S(2)}) async-start(), calls=%async_computation.14 | async-start | bytes 1966080 | tf_op jit(solution)/shard_map/all_gather | solution.py:183
  41.6 144.1 %all-gather.8.cloned.1.call-start = ((), (), s32[]{:S(2)}) async-start(), calls=%async_computation.12 | async-start | bytes 2621440 | tf_op jit(solution)/shard_map/all_gather | solution.py:183
  42.5 254.4 %all-gather.10.cloned.1.call-start = ((), (), s32[]{:S(2)}) async-start(), calls=%async_computation.13 | async-start | bytes 1966080 | tf_op jit(solution)/shard_map/all_gather | solution.py:183
  43.1 496.2 %all-gather.14.cloned.1.call-start = ((), (), s32[]{:S(2)}) async-start(), calls=%async_computation.15 | async-start | bytes 5242880 | tf_op jit(solution)/shard_map/all_gather | solution.py:183
  63.5 490.6 %all-gather.16.cloned.1.call-start = ((), (), s32[]{:S(2)}) async-start(), calls=%async_computation.16 | async-start | bytes 2621440 | tf_op jit(solution)/shard_map/all_gather | solution.py:183
  64.9 87.3 %collective-permute-start.58 = (bf16[256,2048]{0,1:T(8,128)(2,1)}, bf16[256,2048]{0,1:T(8,128)(2,1)}, u32[]{:S(2)}, u32[]{:S(2)}) collective-permute-start(bf16[256,2048]{0,1:T(8,128)(2,1)} %bitcast.134), channel_id=1, source_target_pairs={{0,16},{8,24},{16,0},{24,8},{1,17},{9,25},{17,1},{25,9},{2,18},{10... | collective-permute-start | bytes 3145736 | tf_op jit(solution)/shard_map/ppermute | solution.py:51
  65.5 88.6 %collective-permute-start.57 = (bf16[256,2048]{0,1:T(8,128)(2,1)}, bf16[256,2048]{0,1:T(8,128)(2,1)}, u32[]{:S(2)}, u32[]{:S(2)}) collective-permute-start(bf16[256,2048]{0,1:T(8,128)(2,1)} %bitcast.134), channel_id=1, source_target_pairs={{0,8},{8,0},{16,24},{24,16},{1,9},{9,1},{17,25},{25,17},{2,10},{10... | collective-permute-start | bytes 3145736 | tf_op jit(solution)/shard_map/ppermute | solution.py:51
  72.3 87.6 %collective-permute-start.9 = (bf16[256,2048]{1,0:T(8,128)(2,1)}, bf16[256,2048]{1,0:T(8,128)(2,1)}, u32[]{:S(2)}, u32[]{:S(2)}) collective-permute-start(bf16[256,2048]{1,0:T(8,128)(2,1)} %reshape.857), channel_id=1, source_target_pairs={{0,1},{1,0},{2,3},{3,2},{4,5},{5,4},{6,7},{7,6},{8,9},{9,8},{10,11... | collective-permute-start | bytes 3145736 | tf_op jit(solution)/shard_map/ppermute | solution.py:55
  72.3 57.8 %collective-permute-start.6 = (bf16[256,2048]{1,0:T(8,128)(2,1)}, bf16[256,2048]{1,0:T(8,128)(2,1)S(1)}, u32[]{:S(2)}, u32[]{:S(2)}) collective-permute-start(bf16[256,2048]{1,0:T(8,128)(2,1)} %reshape.857), channel_id=1, source_target_pairs={{0,16},{8,24},{16,0},{24,8},{1,17},{9,25},{17,1},{25,9},{2,18},{10... | collective-permute-start | bytes 3145736 | tf_op jit(solution)/shard_map/ppermute | solution.py:51
  74.3 704.3 %reduce-scatter.17.cloned.1.call-start = ((), (), s32[]{:S(2)}) async-start(), calls=%async_computation.22 | async-start | bytes 2621440 | tf_op jit(solution)/shard_map/reduce_scatter | solution.py:186
  168.6 162.9 %collective-permute-start.32 = (bf16[2,128,2048]{2,1,0:T(8,128)(2,1)}, bf16[2,128,2048]{2,1,0:T(8,128)(2,1)}, u32[]{:S(2)}, u32[]{:S(2)}) collective-permute-start(bf16[2,128,2048]{2,1,0:T(8,128)(2,1)} %get-tuple-element.260), channel_id=1, source_target_pairs={{0,1},{1,0},{2,3},{3,2},{4,5},{5,4},{6,7},{7,6},{8,9},{9,8},{10,11... | collective-permute-start | bytes 3145736 | tf_op jit(solution)/shard_map/ppermute | solution.py:55
  181.6 122.9 %collective-permute-start.29 = (bf16[2,512,256]{2,1,0:T(8,128)(2,1)}, bf16[2,512,256]{2,1,0:T(8,128)(2,1)}, u32[]{:S(2)}, u32[]{:S(2)}) collective-permute-start(bf16[2,512,256]{2,1,0:T(8,128)(2,1)} %constant_dynamic-slice_fusion), channel_id=1, source_target_pairs={{0,4},{2,6},{4,0},{6,2},{1,5},{3,7},{5,1},{7,3},{8,12},{10,14},{12... | collective-permute-start | bytes 1572872 | tf_op jit(solution)/shard_map/ppermute | solution.py:59
  182.9 121.7 %collective-permute-start.28 = (bf16[2,512,256]{2,1,0:T(8,128)(2,1)}, bf16[2,512,256]{2,1,0:T(8,128)(2,1)}, u32[]{:S(2)}, u32[]{:S(2)}) collective-permute-start(bf16[2,512,256]{2,1,0:T(8,128)(2,1)} %constant_dynamic-slice_fusion), channel_id=1, source_target_pairs={{0,2},{2,0},{4,6},{6,4},{1,3},{3,1},{5,7},{7,5},{8,10},{10,8},{12,... | collective-permute-start | bytes 1572872 | tf_op jit(solution)/shard_map/ppermute | solution.py:59
  247.3 58.3 %collective-permute-start.30 = (bf16[2,512,256]{2,1,0:T(8,128)(2,1)}, bf16[2,512,256]{2,1,0:T(8,128)(2,1)}, u32[]{:S(2)}, u32[]{:S(2)}) collective-permute-start(bf16[2,512,256]{2,1,0:T(8,128)(2,1)} %constant_dynamic-slice_fusion), channel_id=1, source_target_pairs={{0,6},{2,4},{4,2},{6,0},{1,7},{3,5},{5,3},{7,1},{8,14},{10,12},{12... | collective-permute-start | bytes 1572872 | tf_op jit(solution)/shard_map/ppermute | solution.py:59
  304.5 155.0 %collective-permute-start.61 = (bf16[256,2048]{0,1:T(8,128)(2,1)}, bf16[256,2048]{0,1:T(8,128)(2,1)}, u32[]{:S(2)}, u32[]{:S(2)}) collective-permute-start(bf16[256,2048]{0,1:T(8,128)(2,1)} %bitcast.134), channel_id=1, source_target_pairs={{0,1},{1,0},{2,3},{3,2},{4,5},{5,4},{6,7},{7,6},{8,9},{9,8},{10,11... | collective-permute-start | bytes 3145736 | tf_op jit(solution)/shard_map/ppermute | solution.py:55
  304.6 117.5 %collective-permute-start.60 = (bf16[128,2048]{0,1:T(8,128)(2,1)}, bf16[128,2048]{0,1:T(8,128)(2,1)}, u32[]{:S(2)}, u32[]{:S(2)}) collective-permute-start(bf16[128,2048]{0,1:T(8,128)(2,1)} %slice.1169), channel_id=1, source_target_pairs={{0,8},{8,0},{16,24},{24,16},{1,9},{9,1},{17,25},{25,17},{2,10},{10... | collective-permute-start | bytes 1572872 | tf_op jit(solution)/shard_map/ppermute | solution.py:51
  308.8 51.8 %collective-permute-start.31 = (bf16[2,4,512,256]{3,2,0,1:T(8,128)(2,1)}, bf16[2,4,512,256]{3,2,0,1:T(8,128)(2,1)}, u32[]{:S(2)}, u32[]{:S(2)}) collective-permute-start(bf16[2,4,512,256]{3,2,0,1:T(8,128)(2,1)} %pad_maximum_fusion.5), channel_id=1, source_target_pairs={{0,1},{1,0},{2,3},{3,2},{4,5},{5,4},{6,7},{7,6},{8,9},{9,8},{10,11... | collective-permute-start | bytes 6291464 | tf_op jit(solution)/shard_map/ppermute | solution.py:55
  331.5 88.4 %collective-permute-start.59 = (bf16[128,2048]{0,1:T(8,128)(2,1)}, bf16[128,2048]{0,1:T(8,128)(2,1)}, u32[]{:S(2)}, u32[]{:S(2)}) collective-permute-start(bf16[128,2048]{0,1:T(8,128)(2,1)} %slice.1168), channel_id=1, source_target_pairs={{0,16},{8,24},{16,0},{24,8},{1,17},{9,25},{17,1},{25,9},{2,18},{10... | collective-permute-start | bytes 1572872 | tf_op jit(solution)/shard_map/ppermute | solution.py:51
  652.4 484.0 %reduce-scatter.7.cloned.1.call-start = ((), (), s32[]{:S(2)}) async-start(), calls=%async_computation.17 | async-start | bytes 1966080 | tf_op jit(solution)/shard_map/reduce_scatter | solution.py:186
  720.2 427.5 %reduce-scatter.15.cloned.1.call-start = ((), (), s32[]{:S(2)}) async-start(), calls=%async_computation.21 | async-start | bytes 5242880 | tf_op jit(solution)/shard_map/reduce_scatter | solution.py:186
  758.2 492.7 %collective-permute-start.49 = (bf16[256,2048]{0,1:T(8,128)(2,1)}, bf16[256,2048]{0,1:T(8,128)(2,1)}, u32[]{:S(2)}, u32[]{:S(2)}) collective-permute-start(bf16[256,2048]{0,1:T(8,128)(2,1)} %bitcast.791), channel_id=1, source_target_pairs={{0,1},{1,0},{2,3},{3,2},{4,5},{5,4},{6,7},{7,6},{8,9},{9,8},{10,11... | collective-permute-start | bytes 3145736 | tf_op jit(solution)/shard_map/ppermute | solution.py:55
  758.8 442.3 %reduce-scatter.13.cloned.1.call-start = ((), (), s32[]{:S(2)}) async-start(), calls=%async_computation.20 | async-start | bytes 2621440 | tf_op jit(solution)/shard_map/reduce_scatter | solution.py:186
  777.2 473.8 %collective-permute-start.56 = (bf16[256,2048]{0,1:T(8,128)(2,1)}, bf16[256,2048]{0,1:T(8,128)(2,1)}, u32[]{:S(2)}, u32[]{:S(2)}) collective-permute-start(bf16[256,2048]{0,1:T(8,128)(2,1)} %pad_maximum_fusion.14), channel_id=1, source_target_pairs={{0,16},{8,24},{16,0},{24,8},{1,17},{9,25},{17,1},{25,9},{2,18},{10... | collective-permute-start | bytes 3145736 | tf_op jit(solution)/shard_map/ppermute | solution.py:51
  847.2 55.9 %collective-permute-start.84 = (bf16[2,4,512,256]{3,2,0,1:T(8,128)(2,1)}, bf16[2,4,512,256]{3,2,0,1:T(8,128)(2,1)}, u32[]{:S(2)}, u32[]{:S(2)}) collective-permute-start(bf16[2,4,512,256]{3,2,0,1:T(8,128)(2,1)} %bitcast.672), channel_id=1, source_target_pairs={{0,1},{1,0},{2,3},{3,2},{4,5},{5,4},{6,7},{7,6},{8,9},{9,8},{10,11... | collective-permute-start | bytes 6291464 | tf_op jit(solution)/shard_map/ppermute | solution.py:55
  898.5 60.4 %collective-permute-start.90 = (bf16[4,384,256]{1,2,0:T(8,128)(2,1)}, bf16[4,384,256]{1,2,0:T(8,128)(2,1)}, u32[]{:S(2)}, u32[]{:S(2)}) collective-permute-start(bf16[4,384,256]{1,2,0:T(8,128)(2,1)} %add_convert_fusion.1), channel_id=1, source_target_pairs={{2,0},{3,1},{10,8},{11,9},{18,16},{19,17},{26,24},{27,25}} | collective-permute-start | bytes 2359304 | tf_op jit(solution)/shard_map/ppermute | solution.py:520
  903.1 329.6 %reduce-scatter.11.cloned.1.call-start = ((), (), s32[]{:S(2)}) async-start(), calls=%async_computation.19 | async-start | bytes 1966080 | tf_op jit(solution)/shard_map/reduce_scatter | solution.py:186
  909.2 101.4 %collective-permute-start.85 = (bf16[2,512,256]{2,1,0:T(8,128)(2,1)}, bf16[2,512,256]{2,1,0:T(8,128)(2,1)}, u32[]{:S(2)}, u32[]{:S(2)}) collective-permute-start(bf16[2,512,256]{2,1,0:T(8,128)(2,1)} %get-tuple-element.247), channel_id=1, source_target_pairs={{0,2},{2,0},{4,6},{6,4},{1,3},{3,1},{5,7},{7,5},{8,10},{10,8},{12,... | collective-permute-start | bytes 1572872 | tf_op jit(solution)/shard_map/ppermute | solution.py:59
  933.7 76.9 %collective-permute-start.87 = (bf16[2,512,256]{2,1,0:T(8,128)(2,1)}, bf16[2,512,256]{2,1,0:T(8,128)(2,1)}, u32[]{:S(2)}, u32[]{:S(2)}) collective-permute-start(bf16[2,512,256]{2,1,0:T(8,128)(2,1)} %get-tuple-element.248), channel_id=1, source_target_pairs={{0,6},{2,4},{4,2},{6,0},{1,7},{3,5},{5,3},{7,1},{8,14},{10,12},{12... | collective-permute-start | bytes 1572872 | tf_op jit(solution)/shard_map/ppermute | solution.py:59
  958.9 53.3 %collective-permute-start.86 = (bf16[2,512,256]{2,1,0:T(8,128)(2,1)}, bf16[2,512,256]{2,1,0:T(8,128)(2,1)}, u32[]{:S(2)}, u32[]{:S(2)}) collective-permute-start(bf16[2,512,256]{2,1,0:T(8,128)(2,1)} %get-tuple-element.249), channel_id=1, source_target_pairs={{0,4},{2,6},{4,0},{6,2},{1,5},{3,7},{5,1},{7,3},{8,12},{10,14},{12... | collective-permute-start | bytes 1572872 | tf_op jit(solution)/shard_map/ppermute | solution.py:59
  1082.2 164.3 %reduce-scatter.9.cloned.1.call-start = ((), (), s32[]{:S(2)}) async-start(), calls=%async_computation.18 | async-start | bytes 2621440 | tf_op jit(solution)/shard_map/reduce_scatter | solution.py:186
  1147.2 57.3 %collective-permute-start.100 = (bf16[256,2048]{1,0:T(8,128)(2,1)}, bf16[256,2048]{1,0:T(8,128)(2,1)}, u32[]{:S(2)}, u32[]{:S(2)}) collective-permute-start(bf16[256,2048]{1,0:T(8,128)(2,1)} %get-tuple-element.184), channel_id=1, source_target_pairs={{0,1},{1,0},{2,3},{3,2},{4,5},{5,4},{6,7},{7,6},{8,9},{9,8},{10,11... | collective-permute-start | bytes 3145736 | tf_op jit(solution)/shard_map/ppermute | solution.py:55
  (320 other events, 4537.9 us)
Sparse Core Ops, SparseCore 0:
  11.6 48.6 all-gather.17
  62.4 35.7 all-gather.11
  100.4 45.9 all-gather.7
  147.8 35.8 all-gather.9
  185.0 112.1 all-gather.13
  298.6 49.6 all-gather.15
  652.6 62.7 reduce-scatter.16
  720.3 53.4 reduce-scatter.6
  776.2 77.6 reduce-scatter.14
  903.2 95.4 reduce-scatter.12
  1082.4 36.0 reduce-scatter.10
  1134.9 41.9 reduce-scatter.8

commit v2 on v1

v2 whole, which is shorter than its diff:
```python
import math

import jax
import jax.numpy as jnp
from jax import lax
from jax.experimental import pallas as pl
from jax.experimental.pallas import tpu as pltpu
from jax.sharding import Mesh
from jax.sharding import PartitionSpec as P

HEADS = 48
SSM_HEAD = 64
STATE = 256
CONV = 4
QHEADS = 8
KVHEADS = 2
ATT_HEAD = 128
EPSILON = 1e-05
ROPE_BASE = 10000.0
NEG_BIG = -1e30
HIGH = lax.Precision.HIGHEST

RANKS = 8
ROWS = 4
OWN_HEADS = HEADS // RANKS
OWN_SSM = OWN_HEADS * SSM_HEAD
OWN_STATE = 2 * STATE // RANKS
OWN_CONV = OWN_SSM + OWN_STATE

bf16 = jnp.bfloat16
f32 = jnp.float32


ANY = pl.BlockSpec(memory_space=pl.ANY)
IN_VMEM = pl.BlockSpec(memory_space=pltpu.VMEM)
CHUNK = 256
LANES_A = 512
STEP_AT = OWN_CONV
PIECE = OWN_STATE
HALF = 2 * CHUNK


def dot(left, right, dims=((1,), (0,))):
    return lax.dot_general(left, right, (dims, ((), ())), preferred_element_type=f32)


def dot_rows(left, right):
    return dot(left, right, ((0,), (0,)))


def dot_cols(left, right):
    return dot(left, right, ((1,), (1,)))


def bdot(left, right, lc, rc):
    return lax.dot_general(
        left, right, (((lc,), (rc,)), ((0,), (0,))), preferred_element_type=f32
    )


def hop(values, flip):
    return lax.ppermute(values, "b", [(i, i ^ flip) for i in range(ROWS)])


def twin(values):
    return lax.ppermute(values, "c", [(0, 1), (1, 0)])


def zhop(values, flip):
    return lax.ppermute(values, "z", [(i, i ^ flip) for i in range(lax.axis_size("z"))])


def zshift(values, step):
    size = lax.axis_size("z")
    return lax.ppermute(
        values, "z", [(i, i + step) for i in range(size) if 0 <= i + step < size]
    )


def after(values, *earlier):
    return lax.optimization_barrier((values,) + earlier)[0]


def gather_group(own, meanwhile=None):
    half = own.shape[0] // 2
    by_x = hop(own, 1)
    by_y = hop(own, 2)
    if meanwhile is not None:
        by_x, by_y, meanwhile = lax.optimization_barrier((by_x, by_y, meanwhile))
    mine = [own, by_x, by_y, hop(by_x[:half], 2), hop(by_y[half:], 1)]
    pieces = mine + [twin(part) for part in mine]
    return pieces if meanwhile is None else (pieces, meanwhile)


def starts_of(pieces):
    starts = [0]
    for piece in pieces:
        starts.append(starts[-1] + piece.shape[0])
    return starts


def reslot(values, flip, axis):
    order = [k ^ flip for k in range(ROWS)]
    return jnp.concatenate(
        [lax.slice_in_dim(values, k, k + 1, axis=axis) for k in order], axis=axis
    )


def sum_group(values):
    values = values + twin(values)[::-1]
    total = values
    for flip in range(1, ROWS):
        total = total + reslot(hop(values, flip), flip, 1)
    return total


def silu_slope(values):
    sigmoid = jax.nn.sigmoid(values)
    return sigmoid * (1.0 + values * (1.0 - sigmoid))


def rms_scale(values):
    return lax.rsqrt(jnp.mean(values * values, axis=-1, keepdims=True) + EPSILON)


def rotate(values, cosine, sine):
    half = values.shape[-1] // 2
    first = values[..., :half]
    second = values[..., half:]
    return jnp.concatenate([first * cosine - second * sine, second * cosine + first * sine], axis=-1)


def split(values, count):
    terms = []
    for _ in range(count):
        low = values.astype(bf16)
        terms.append(low)
        values = values - low.astype(f32)
    return terms


def exact(ones, values, dims=((1,), (0,)), count=3):
    return sum(dot(ones.astype(bf16), term, dims) for term in split(values, count))


def head_map(rows, cols, along):
    channel = lax.broadcasted_iota(jnp.int32, (rows, cols), along)
    head = lax.broadcasted_iota(jnp.int32, (rows, cols), 1 - along)
    return (channel // SSM_HEAD == head).astype(bf16)


def widen(values):
    rows = values.shape[0]
    first = lax.broadcasted_iota(jnp.int32, (rows, 2 * SSM_HEAD), 1) < SSM_HEAD
    parts = []
    for h in range(0, OWN_HEADS, 2):
        left = jnp.broadcast_to(values[:, h : h + 1], first.shape)
        right = jnp.broadcast_to(values[:, h + 1 : h + 2], first.shape)
        parts.append(jnp.where(first, left, right))
    return jnp.concatenate(parts, axis=1)


def narrow(values):
    ones = head_map(OWN_SSM, 8, 0)
    return sum(dot(term, ones) for term in split(values, 2))


def row_sums(values):
    ones = jnp.ones((8, values.shape[1]), bf16)
    return exact(ones, values, ((1,), (1,)), 2)


def sigmoid_of(values):
    return 1.0 / (1.0 + jnp.exp(-values))


def tri(lower):
    t = lax.broadcasted_iota(jnp.int32, (CHUNK, CHUNK), 0)
    s = lax.broadcasted_iota(jnp.int32, (CHUNK, CHUNK), 1)
    return (t >= s) if lower else (t <= s)


def conv_kernel(proj, halo, marks, conv, head, xs_out, bc_out, slope_out, meta_out, row_out, ext):
    ext[0:8, :] = halo[0]
    ext[8:, :] = proj[0].astype(bf16).astype(f32)
    pre = conv[4:5, :] + conv[3:4, :] * ext[8 : 8 + CHUNK, :]
    for o in range(CONV - 1):
        pre = pre + conv[o : o + 1, :] * ext[5 + o : 5 + o + CHUNK, :] * marks[0, :, 3 + o : 4 + o]
    sig = sigmoid_of(pre)
    act = (pre * sig).astype(bf16)
    xs_out[0] = act[:, :OWN_SSM]
    for r in range(2):

        @pl.when(pl.program_id(1) == r)
        def _():
            bc_out[0, :, r * PIECE : (r + 1) * PIECE] = act[:, OWN_SSM:OWN_CONV]

    slope_out[0] = sig * (1.0 + pre * (1.0 - sig))
    raw = proj[0][:, STEP_AT : STEP_AT + 8] + head[0:1, 0:8]
    real = lax.broadcasted_iota(jnp.int32, (CHUNK, 8), 1) < OWN_HEADS
    step = jnp.maximum(raw, 0.0) + jnp.log(1.0 + jnp.exp(-jnp.abs(raw)))
    step = jnp.where(real, step, 0.0)
    cum = exact(tri(True), step * head[1:2, 0:8])
    meta = jnp.concatenate(
        [step, cum, sigmoid_of(raw), jnp.zeros((CHUNK, 104), f32)], axis=1
    )
    meta_out[0] = meta[:, :32]
    row_out[0] = meta.T[:16]


def marks_kernel(own, before, out):
    lane = lax.broadcasted_iota(jnp.int32, (1, CHUNK), 1)
    for q in range(own.shape[0]):
        seg, prev = own[q : q + 1, :], before[q : q + 1, :]
        rows = [seg, (seg == prev[:, CHUNK - 1 :]).astype(f32), (seg == seg[:, CHUNK - 1 :]).astype(f32)]
        for o in range(CONV - 1):
            by = CONV - 1 - o
            moved = jnp.where(lane < by, pltpu.roll(prev, by, 1), pltpu.roll(seg, by, 1))
            rows.append((moved == seg).astype(f32))
        rows.append(jnp.zeros((128 - len(rows), CHUNK), f32))
        out[q] = jnp.concatenate(rows, axis=0).T[:, :8]


def marks_of(own, before):
    chunks = own.shape[0]
    return pl.pallas_call(
        marks_kernel,
        in_specs=[IN_VMEM] * 2,
        out_specs=IN_VMEM,
        out_shape=jax.ShapeDtypeStruct((chunks, CHUNK, 8), f32),
        compiler_params=pltpu.CompilerParams(vmem_limit_bytes=VMEM),
        cost_estimate=lasting(3),
        name="marks",
    )(own, before)


def conv_forward(proj, halo, marks, conv, head):
    block = lambda *shape: pl.BlockSpec((1,) + shape, lambda k, r: (r * ROWS + k, 0, 0))
    whole = pl.BlockSpec((8, LANES_A), lambda k, r: (0, 0))
    chunks = proj.shape[0]
    return pl.pallas_call(
        conv_kernel,
        grid=(ROWS, 2),
        in_specs=[
            block(CHUNK, LANES_A),
            block(8, LANES_A),
            block(CHUNK, 8),
            whole,
            pl.BlockSpec((8, 128), lambda k, r: (0, 0)),
        ],
        out_specs=[
            block(CHUNK, OWN_SSM),
            pl.BlockSpec((1, CHUNK, 2 * PIECE), lambda k, r: (k, 0, 0)),
            block(CHUNK, LANES_A),
            block(CHUNK, 32),
            block(16, CHUNK),
        ],
        out_shape=[
            jax.ShapeDtypeStruct((chunks, CHUNK, OWN_SSM), bf16),
            jax.ShapeDtypeStruct((ROWS, CHUNK, 2 * PIECE), bf16),
            jax.ShapeDtypeStruct((chunks, CHUNK, LANES_A), f32),
            jax.ShapeDtypeStruct((chunks, CHUNK, 32), f32),
            jax.ShapeDtypeStruct((chunks, 16, CHUNK), f32),
        ],
        scratch_shapes=[pltpu.VMEM((8 + CHUNK, LANES_A), f32)],
        compiler_params=pltpu.CompilerParams(vmem_limit_bytes=VMEM),
        cost_estimate=lasting(8),
        name="conv_forward",
    )(proj, halo, marks, conv, head)


VMEM = 60 * 1024 * 1024


def lasting(microseconds):
    return pl.CostEstimate(
        flops=0, bytes_accessed=int(microseconds * 1.1e6), transcendentals=0
    )


def time_spec(shape, backward=False):
    def at(k, t, where):
        core = (1 - t if backward else t) ^ where[2]
        return (core * ROWS + k,) + (0,) * len(shape)

    return pl.BlockSpec((1,) + tuple(shape), at)


def slot_spec(shape):
    return pl.BlockSpec((1,) + tuple(shape), lambda k, t, where: (k,) + (0,) * len(shape))


def piece_specs(kind):
    def spec(i):
        def at(k, t, where):
            slot = (i // 2 + 2 * kind) ^ (2 * (where[0] // 2))
            return (i % 2 * ROWS + slot, k ^ slot, 0, 0)

        return pl.BlockSpec((1, 1, CHUNK, 2 * PIECE), at)

    return [spec(i) for i in range(4)]


def core_of(where, backward=False):
    t = pl.program_id(1)
    return (1 - t if backward else t) ^ where[2]


def joined(pieces, core):
    parts = []
    for i, piece in enumerate(pieces):
        both = piece[0, 0]
        parts.append(jnp.where(core ^ (i % 2) == 0, both[:, :PIECE], both[:, PIECE:]))
    return jnp.concatenate(parts, axis=1)


def tails_of(meta, marks):
    step, cum = meta[0, :, 0:8], meta[0, :, 8:16]
    last = cum[CHUNK - 1 : CHUNK]
    decay = jnp.exp(last - cum) * marks[0, :, 2:3]
    return step, cum, decay, decay * step


def local_kernel(where, xs, b0, b1, b2, b3, meta, marks, p1, first_out, both_out):
    _, _, _, tail = tails_of(meta, marks)
    weighted = (xs[0].astype(f32) * widen(tail)).astype(bf16)
    local = dot_rows(weighted, joined((b0, b1, b2, b3), core_of(where)))

    @pl.when(pl.program_id(1) == 0)
    def _():
        first_out[0] = local

    @pl.when(pl.program_id(1) == 1)
    def _():
        both_out[0] = p1[0] * first_out[0] + local


def local_states(where, xs, bc, meta, marks, p1):
    state = jax.ShapeDtypeStruct((ROWS, OWN_SSM, STATE), f32)
    return pl.pallas_call(
        local_kernel,
        grid_spec=pltpu.PrefetchScalarGridSpec(
            num_scalar_prefetch=1,
            grid=(ROWS, 2),
            in_specs=[time_spec((CHUNK, OWN_SSM))]
            + piece_specs(0)
            + [time_spec((CHUNK, 32)), time_spec((CHUNK, 8)), slot_spec((OWN_SSM, 1))],
            out_specs=[slot_spec((OWN_SSM, STATE))] * 2,
        ),
        out_shape=[state, state],
        compiler_params=pltpu.CompilerParams(vmem_limit_bytes=VMEM),
        cost_estimate=lasting(8),
        name="local_states",
    )(where, xs, bc, bc, bc, bc, meta, marks, p1)


def decay_of(meta, row, allowed, h):
    spread = meta[0, :, 8 + h : 9 + h] - row[0, 8 + h : 9 + h, :]
    return jnp.exp(jnp.where(allowed, spread, NEG_BIG))


def ssm_kernel(
    where, xs, b0, b1, b2, b3, c0, c1, c2, c3, meta, row, marks, segs, state, first, p0, gating, skip,
    out, gated_out, square_out, work,
):
    later = pl.program_id(1) == 1
    core = core_of(where)
    b_mat, c_mat = joined((b0, b1, b2, b3), core), joined((c0, c1, c2, c3), core)
    inner = dot_cols(c_mat, b_mat)
    allowed = (marks[0, :, 0:1] == segs[0, 0:1, :]) & tri(True)
    xs_f = xs[0].astype(f32)
    step, cum = meta[0, :, 0:8], meta[0, :, 8:16]
    stepped = (xs_f * widen(step)).astype(bf16)
    entering = jnp.where(later, p0[0] * state[0] + first[0], state[0]).astype(bf16)
    entry = widen(jnp.exp(cum) * marks[0, :, 1:2])
    for h in range(OWN_HEADS):
        at = slice(h * SSM_HEAD, (h + 1) * SSM_HEAD)
        mix = (inner * decay_of(meta, row, allowed, h)).astype(bf16)
        work[:, at] = dot(mix, stepped[:, at])
    total = work[...] + dot_cols(c_mat, entering) * entry + skip[0:1, :] * xs_f
    out[0] = total
    gate = gating[0]
    gated = total * gate * sigmoid_of(gate)
    gated_out[0] = gated.astype(bf16)
    square_out[0] = row_sums(gated * gated)


def ssm_forward(where, xs, bc, meta, row, marks, segs, state, first, p0, gating, skip):
    chunks = xs.shape[0]
    return pl.pallas_call(
        ssm_kernel,
        grid_spec=pltpu.PrefetchScalarGridSpec(
            num_scalar_prefetch=1,
            grid=(ROWS, 2),
            in_specs=[time_spec((CHUNK, OWN_SSM))]
            + piece_specs(0)
            + piece_specs(1)
            + [
                time_spec((CHUNK, 32)),
                time_spec((16, CHUNK)),
                time_spec((CHUNK, 8)),
                time_spec((8, CHUNK)),
                slot_spec((OWN_SSM, STATE)),
                slot_spec((OWN_SSM, STATE)),
                slot_spec((OWN_SSM, 1)),
                time_spec((CHUNK, OWN_SSM)),
                pl.BlockSpec((8, OWN_SSM), lambda k, t, where: (0, 0)),
            ],
            out_specs=[
                time_spec((CHUNK, OWN_SSM)),
                time_spec((CHUNK, OWN_SSM)),
                time_spec((8, CHUNK)),
            ],
            scratch_shapes=[pltpu.VMEM((CHUNK, OWN_SSM), f32)],
        ),
        out_shape=[
            jax.ShapeDtypeStruct((chunks, CHUNK, OWN_SSM), f32),
            jax.ShapeDtypeStruct((chunks, CHUNK, OWN_SSM), bf16),
            jax.ShapeDtypeStruct((chunks, 8, CHUNK), f32),
        ],
        compiler_params=pltpu.CompilerParams(vmem_limit_bytes=VMEM),
        cost_estimate=lasting(16),
        name="ssm_forward",
    )(where, xs, bc, bc, bc, bc, bc, bc, bc, bc, meta, row, marks, segs, state, first, p0, gating, skip)


def attention_mask(where, seg_q, seg_k):
    m = pl.program_id(1)
    same = seg_q[...].reshape(HALF, 8)[:, 0:1] == seg_k[0, 0:1, :]
    row = lax.broadcasted_iota(jnp.int32, (HALF, HALF), 0)
    place = lax.rem(row + where[2] * CHUNK, HALF)
    key = lax.broadcasted_iota(jnp.int32, (HALF, HALF), 1)
    return same & ((place >= key) | (m < where[1]))


def slot_keyval(where, own, other):
    mine = pl.program_id(0) // 2 == where[2]
    return jnp.where(mine, own[0, 0], other[0, 0])


def attend_kernel(where, query, kv_own, kv_other, seg_q, seg_k, out, low_out, sum_out, best, total, acc):
    m = pl.program_id(1)
    scale = 1.0 / math.sqrt(ATT_HEAD)

    @pl.when(m == 0)
    def _():
        best[...] = jnp.full_like(best, NEG_BIG)
        total[...] = jnp.zeros_like(total)
        acc[...] = jnp.zeros_like(acc)

    @pl.when(m <= where[1])
    def _():
        q = query[...].reshape(HALF, ATT_HEAD)
        keyval = slot_keyval(where, kv_own, kv_other)
        keys, vals = keyval[:, :ATT_HEAD], keyval[:, ATT_HEAD:]
        scores = jnp.where(attention_mask(where, seg_q, seg_k), dot_cols(q, keys) * scale, NEG_BIG)
        before = best[:, 0:1]
        now = jnp.maximum(before, jnp.max(scores, axis=1, keepdims=True))
        shrink = jnp.exp(before - now)
        weights = jnp.where(scores > 0.5 * NEG_BIG, jnp.exp(scores - now), 0.0)
        total[...] = total[...] * shrink + jnp.sum(weights, axis=1, keepdims=True)
        acc[...] = acc[...] * shrink + dot(weights.astype(bf16), vals)
        best[...] = jnp.broadcast_to(now, best.shape)

    @pl.when(m == pl.num_programs(1) - 1)
    def _():
        context = (acc[...] / total[...]).reshape(2, 1, CHUNK, ATT_HEAD)
        out[...] = context
        low_out[...] = context.astype(bf16)
        sum_out[0] = (best[...] + jnp.log(total[...]))[:, 0:8]


def pair_spec(width):
    return pl.BlockSpec((2, 1, CHUNK, width), lambda k, m, where: (0, k, 0, 0))


def attend(where, query, kv_own, kv_other, seg_q, seg_k):
    slots = kv_own.shape[0]
    keyval_spec = pl.BlockSpec((1, 1, HALF, 2 * ATT_HEAD), lambda k, m, where: (m, k % 2, 0, 0))
    return pl.pallas_call(
        attend_kernel,
        grid_spec=pltpu.PrefetchScalarGridSpec(
            num_scalar_prefetch=1,
            grid=(ROWS, slots),
            in_specs=[
                pair_spec(ATT_HEAD),
                keyval_spec,
                keyval_spec,
                pair_spec(8),
                pl.BlockSpec((1, 8, HALF), lambda k, m, where: (k * slots + m, 0, 0)),
            ],
            out_specs=[
                pair_spec(ATT_HEAD),
                pair_spec(ATT_HEAD),
                pl.BlockSpec((1, HALF, 8), lambda k, m, where: (k, 0, 0)),
            ],
            scratch_shapes=[pltpu.VMEM((HALF, ATT_HEAD), f32)] * 3,
        ),
        out_shape=[
            jax.ShapeDtypeStruct(query.shape, f32),
            jax.ShapeDtypeStruct(query.shape, bf16),
            jax.ShapeDtypeStruct((ROWS, HALF, 8), f32),
        ],
        compiler_params=pltpu.CompilerParams(vmem_limit_bytes=VMEM),
        cost_estimate=lasting(10),
        name="attend",
    )(where, query, kv_own, kv_other, seg_q, seg_k)


def attend_back_kernel(where, query, kv_own, kv_other, seg_q, seg_k, grad, context, sums, query_out, keyval_out):
    m = pl.program_id(1)
    scale = 1.0 / math.sqrt(ATT_HEAD)
    used = m <= where[1]

    @pl.when(m == 0)
    def _():
        query_out[...] = jnp.zeros_like(query_out)

    @pl.when(jnp.logical_not(used))
    def _():
        keyval_out[...] = jnp.zeros_like(keyval_out)

    @pl.when(used)
    def _():
        q = query[...].reshape(HALF, ATT_HEAD)
        g = grad[...].reshape(HALF, ATT_HEAD)
        keyval = slot_keyval(where, kv_own, kv_other)
        keys, vals = keyval[:, :ATT_HEAD], keyval[:, ATT_HEAD:]
        delta = jnp.sum(
            g.astype(f32) * context[...].reshape(HALF, ATT_HEAD), axis=1, keepdims=True
        )
        spread = dot_cols(q, keys) * scale - sums[0, :, 0:1]
        prob = jnp.exp(jnp.where(attention_mask(where, seg_q, seg_k), spread, NEG_BIG))
        slope = (prob * (dot_cols(g, vals) - delta)).astype(bf16)
        part = (dot(slope, keys) * scale).reshape(2, 1, CHUNK, ATT_HEAD)
        query_out[...] = query_out[...] + part
        keyval_out[0, 0, :, :ATT_HEAD] = (dot_rows(slope, q) * scale).astype(bf16)
        keyval_out[0, 0, :, ATT_HEAD:] = dot_rows(prob.astype(bf16), g).astype(bf16)


def attend_back(where, query, kv_own, kv_other, seg_q, seg_k, grad, context, sums):
    slots = kv_own.shape[0]
    keyval_spec = pl.BlockSpec((1, 1, HALF, 2 * ATT_HEAD), lambda k, m, where: (m, k % 2, 0, 0))
    grad_spec = pl.BlockSpec((1, 1, HALF, 2 * ATT_HEAD), lambda k, m, where: (m, k, 0, 0))
    return pl.pallas_call(
        attend_back_kernel,
        grid_spec=pltpu.PrefetchScalarGridSpec(
            num_scalar_prefetch=1,
            grid=(ROWS, slots),
            in_specs=[
                pair_spec(ATT_HEAD),
                keyval_spec,
                keyval_spec,
                pair_spec(8),
                pl.BlockSpec((1, 8, HALF), lambda k, m, where: (k * slots + m, 0, 0)),
                pair_spec(ATT_HEAD),
                pair_spec(ATT_HEAD),
                pl.BlockSpec((1, HALF, 8), lambda k, m, where: (k, 0, 0)),
            ],
            out_specs=[pair_spec(ATT_HEAD), grad_spec],
        ),
        out_shape=[
            jax.ShapeDtypeStruct(query.shape, f32),
            jax.ShapeDtypeStruct((slots, ROWS, HALF, 2 * ATT_HEAD), bf16),
        ],
        compiler_params=pltpu.CompilerParams(vmem_limit_bytes=VMEM),
        cost_estimate=lasting(14),
        name="attend_back",
    )(where, query, kv_own, kv_other, seg_q, seg_k, grad, context, sums)


def gate_back_kernel(
    where, es, scale, gating, ssm_out, c0, c1, c2, c3, meta, marks, p0,
    gy_out, gating_out, unit_out, later_out, both_out,
):
    gate = gating[0]
    sig = sigmoid_of(gate)
    act = gate * sig
    out = ssm_out[0]
    norm = scale[0, :, 0:1]
    unit = out * act * norm
    unit_out[0] = unit.astype(bf16)
    grad = norm * (es[0] - unit * scale[0, :, 1:2])
    gy = (grad * act).astype(bf16)
    gy_out[0] = gy
    gating_out[0] = (grad * out * (sig * (1.0 + gate * (1.0 - sig)))).astype(bf16)
    entry = widen(jnp.exp(meta[0, :, 8:16]) * marks[0, :, 1:2])
    across = (gy.astype(f32) * entry).astype(bf16)
    local = dot_rows(across, joined((c0, c1, c2, c3), core_of(where, True)))

    @pl.when(pl.program_id(1) == 0)
    def _():
        later_out[0] = local

    @pl.when(pl.program_id(1) == 1)
    def _():
        both_out[0] = p0[0] * later_out[0] + local


def gate_back(where, es, scale, gating, ssm_out, bc, meta, marks, p0):
    chunks = gating.shape[0]
    wide = time_spec((CHUNK, OWN_SSM), True)
    state = jax.ShapeDtypeStruct((ROWS, OWN_SSM, STATE), f32)
    token = jax.ShapeDtypeStruct((chunks, CHUNK, OWN_SSM), bf16)
    return pl.pallas_call(
        gate_back_kernel,
        grid_spec=pltpu.PrefetchScalarGridSpec(
            num_scalar_prefetch=1,
            grid=(ROWS, 2),
            in_specs=[wide, time_spec((CHUNK, 8), True), wide, wide]
            + piece_specs(1)
            + [
                time_spec((CHUNK, 32), True),
                time_spec((CHUNK, 8), True),
                slot_spec((OWN_SSM, 1)),
            ],
            out_specs=[wide, wide, wide, slot_spec((OWN_SSM, STATE)), slot_spec((OWN_SSM, STATE))],
        ),
        out_shape=[token, token, token, state, state],
        compiler_params=pltpu.CompilerParams(vmem_limit_bytes=VMEM),
        cost_estimate=lasting(11),
        name="gate_back",
    )(where, es, scale, gating, ssm_out, bc, bc, bc, bc, meta, marks, p0)


def ssm_back_kernel(
    where, xs, gy, b0, b1, b2, b3, c0, c1, c2, c3, meta, row, marks, segs, state, first, flow, later,
    p0, p1, skip, head,
    xs_out, o00, o01, o02, o03, o10, o11, o12, o13, step_out, sums_out, work,
):
    early = pl.program_id(1) == 1
    core = core_of(where, True)
    b_mat, c_mat = joined((b0, b1, b2, b3), core), joined((c0, c1, c2, c3), core)
    inner = dot_cols(b_mat, c_mat)
    allowed = (marks[0, :, 0:1] == segs[0, 0:1, :]) & tri(False)
    xs_f = xs[0].astype(f32)
    gy_low = gy[0]
    gy_f = gy_low.astype(f32)
    step, cum, tail_decay, tail = tails_of(meta, marks)
    step_wide, tail_wide = widen(step), widen(tail)
    entry = widen(jnp.exp(cum) * marks[0, :, 1:2])
    stepped = (xs_f * step_wide).astype(bf16)
    grad_inner = jnp.zeros((CHUNK, CHUNK), f32)
    read = jnp.zeros((CHUNK, 8), f32)
    reads = jnp.zeros((8, CHUNK), f32)
    lane = lax.broadcasted_iota(jnp.int32, (CHUNK, 8), 1)
    sublane = lax.broadcasted_iota(jnp.int32, (8, CHUNK), 0)
    for h in range(OWN_HEADS):
        at = slice(h * SSM_HEAD, (h + 1) * SSM_HEAD)
        spread = row[0, 8 + h : 9 + h, :] - meta[0, :, 8 + h : 9 + h]
        decay = jnp.exp(jnp.where(allowed, spread, NEG_BIG))
        slope = decay * dot_cols(stepped[:, at], gy_low[:, at])
        grad_inner = grad_inner + slope
        flow_low = (slope * inner).astype(bf16)
        read = read + dot(flow_low, (lane == h).astype(bf16))
        reads = reads + dot((sublane == h).astype(bf16), flow_low)
        work[:, at] = dot((inner * decay).astype(bf16), gy_low[:, at])
    reads = jnp.concatenate([reads, jnp.zeros((120, CHUNK), f32)], axis=0).T
    flows = reads[:, :8] - read
    from_mix = work[...]
    entering = jnp.where(early, state[0], p0[0] * state[0] + first[0])
    leaving = jnp.where(early, p1[0] * flow[0] + later[0], flow[0])
    leaving_low = leaving.astype(bf16)
    inner_low = grad_inner.astype(bf16)
    across = (gy_f * entry).astype(bf16)
    weighted = (xs_f * tail_wide).astype(bf16)
    grad_b = dot(inner_low, c_mat) + dot(weighted, leaving_low)
    grad_c = dot_rows(inner_low, b_mat) + dot(across, entering.astype(bf16))
    from_state = dot_cols(b_mat, leaving_low)
    skip_row = skip[0:1, :]
    xs_out[0] = skip_row * gy_f + step_wide * from_mix + tail_wide * from_state
    low_first = where[0] < 2
    lower = jnp.where(low_first, grad_b, grad_c).astype(bf16)
    upper = jnp.where(low_first, grad_c, grad_b).astype(bf16)
    for ref, value, i in (
        (o00, lower, 0), (o10, lower, 1), (o01, lower, 2), (o11, lower, 3),
        (o02, upper, 0), (o12, upper, 1), (o03, upper, 2), (o13, upper, 3),
    ):
        for half in range(2):

            @pl.when(core ^ (i % 2) == half)
            def _():
                ref[0, :, half * PIECE : (half + 1) * PIECE] = value[:, i * PIECE : (i + 1) * PIECE]

    entering_low = entering.astype(bf16)
    entry_sum = narrow(gy_f * (dot_cols(c_mat, entering_low) * entry))
    step_sum = narrow(xs_f * from_mix)
    tail_sum = narrow(xs_f * from_state)
    skip_sum = narrow(gy_f * xs_f)
    tail_flow = tail_sum * tail
    passed = jnp.sum(leaving * entering, axis=1, keepdims=True)
    passed = jnp.broadcast_to(passed, (OWN_SSM, 8))
    own_head = head_map(OWN_SSM, 8, 0).astype(f32)
    grad_pass = jnp.sum(passed * own_head, axis=0, keepdims=True)
    passing = jnp.exp(cum[CHUNK - 1 : CHUNK]) * marks[0, CHUNK - 1 : CHUNK, 1:2]
    end = grad_pass * passing + jnp.sum(tail_flow, axis=0, keepdims=True)
    last = lax.broadcasted_iota(jnp.int32, (CHUNK, 8), 0) == CHUNK - 1
    grad_cum = flows + entry_sum - tail_flow + jnp.where(last, end, 0.0)
    grad_rate = exact(tri(False), grad_cum)
    grad_step = step_sum + tail_sum * tail_decay + grad_rate * head[1:2, 0:8]
    raw = grad_step * meta[0, :, 16:24]
    step_out[0] = raw
    sums = [raw, grad_rate * step, skip_sum]
    sums_out[0] = jnp.concatenate(
        [jnp.sum(v, axis=0, keepdims=True) for v in sums] + [jnp.zeros((5, 8), f32)], axis=0
    )


def ssm_back(where, xs, gy, bc, meta, row, marks, segs, state, first, flow, later, p0, p1, skip, head):
    chunks = xs.shape[0]
    wide = time_spec((CHUNK, OWN_SSM), True)
    kept = slot_spec((OWN_SSM, STATE))
    column = slot_spec((OWN_SSM, 1))

    def owner(slot):
        return pl.BlockSpec((1, CHUNK, 2 * PIECE), lambda k, t, where: (k ^ slot, 0, 0))

    piece = jax.ShapeDtypeStruct((ROWS, CHUNK, 2 * PIECE), bf16)
    return pl.pallas_call(
        ssm_back_kernel,
        grid_spec=pltpu.PrefetchScalarGridSpec(
            num_scalar_prefetch=1,
            grid=(ROWS, 2),
            in_specs=[wide, wide]
            + piece_specs(0)
            + piece_specs(1)
            + [
                time_spec((CHUNK, 32), True),
                time_spec((16, CHUNK), True),
                time_spec((CHUNK, 8), True),
                time_spec((8, CHUNK), True),
                kept,
                kept,
                kept,
                kept,
                column,
                column,
                pl.BlockSpec((8, OWN_SSM), lambda k, t, where: (0, 0)),
                pl.BlockSpec((8, 128), lambda k, t, where: (0, 0)),
            ],
            out_specs=[wide]
            + [owner(m) for r in range(2) for m in range(ROWS)]
            + [time_spec((CHUNK, 8), True), time_spec((8, 8), True)],
            scratch_shapes=[pltpu.VMEM((CHUNK, OWN_SSM), f32)],
        ),
        out_shape=[jax.ShapeDtypeStruct((chunks, CHUNK, OWN_SSM), f32)]
        + [piece] * 8
        + [
            jax.ShapeDtypeStruct((chunks, CHUNK, 8), f32),
            jax.ShapeDtypeStruct((chunks, 8, 8), f32),
        ],
        compiler_params=pltpu.CompilerParams(vmem_limit_bytes=VMEM),
        cost_estimate=lasting(30),
        name="ssm_back",
    )(
        where, xs, gy, bc, bc, bc, bc, bc, bc, bc, bc, meta, row, marks, segs, state, first, flow,
        later, p0, p1, skip, head,
    )


def conv_back_kernel(grad_xs, grad_bc, step, slope, proj, halo, marks, returned, conv, out, sums_out, ext, back):
    ext[0:8, :] = halo[0]
    ext[8:, :] = proj[0].astype(bf16).astype(f32)
    rest = jnp.zeros((CHUNK, LANES_A - OWN_CONV), f32)
    both = grad_bc[0]
    own_bc = jnp.where(pl.program_id(0) < ROWS, both[:, :PIECE], both[:, PIECE:])
    grad = jnp.concatenate([grad_xs[0], own_bc, rest], axis=1) * slope[0]
    sums = []
    back[...] = jnp.zeros_like(back)
    back[CHUNK : CHUNK + 8, :] = returned[0]
    for o in range(CONV):
        masked = grad if o == CONV - 1 else grad * marks[0, :, 3 + o : 4 + o]
        sums.append(jnp.sum(masked * ext[5 + o : 5 + o + CHUNK, :], axis=0, keepdims=True))
        back[5 + o : 5 + o + CHUNK, :] = (
            back[5 + o : 5 + o + CHUNK, :] + masked * conv[o : o + 1, :]
        )
    sums.append(jnp.sum(grad, axis=0, keepdims=True))
    sums_out[0] = jnp.concatenate(sums + [jnp.zeros((3, LANES_A), f32)], axis=0)
    mixed = back[8 : 8 + CHUNK, :]
    out[0] = mixed.astype(bf16)
    out[0, :, STEP_AT : STEP_AT + 8] = step[0].astype(bf16)


def conv_backward(grad_xs, grad_bc, step, slope, proj, halo, marks, returned, conv):
    chunks = proj.shape[0]
    block = lambda *shape: pl.BlockSpec((1,) + shape, lambda q: (q, 0, 0))
    return pl.pallas_call(
        conv_back_kernel,
        grid=(chunks,),
        in_specs=[
            block(CHUNK, OWN_SSM),
            pl.BlockSpec((1, CHUNK, 2 * PIECE), lambda q: (lax.rem(q, ROWS), 0, 0)),
            block(CHUNK, 8),
            block(CHUNK, LANES_A),
            block(CHUNK, LANES_A),
            block(8, LANES_A),
            block(CHUNK, 8),
            block(8, LANES_A),
            pl.BlockSpec((8, LANES_A), lambda q: (0, 0)),
        ],
        out_specs=[block(CHUNK, LANES_A), block(8, LANES_A)],
        out_shape=[
            jax.ShapeDtypeStruct((chunks, CHUNK, LANES_A), bf16),
            jax.ShapeDtypeStruct((chunks, 8, LANES_A), f32),
        ],
        scratch_shapes=[pltpu.VMEM((8 + CHUNK, LANES_A), f32)] * 2,
        compiler_params=pltpu.CompilerParams(vmem_limit_bytes=VMEM),
        cost_estimate=lasting(6),
        name="conv_backward",
    )(grad_xs, grad_bc, step, slope, proj, halo, marks, returned, conv)


LARGE = VMEM


def fetch(pieces, held, arrived):
    starts = starts_of(pieces)
    copies = []
    for i, piece in enumerate(pieces):
        at = pl.ds(starts[i], piece.shape[0])
        copies.append(pltpu.make_async_copy(piece, held.at[at], arrived.at[i]))
        copies[-1].start()
    return copies, starts


def by_chunk(copies, starts):
    for i in range(8):
        for j, copy in enumerate(copies):
            if i * CHUNK < starts[j + 1] <= (i + 1) * CHUNK:
                copy.wait()
        yield i, slice(i * CHUNK, (i + 1) * CHUNK)


def times_kernel(count, *refs):
    pieces, (weight, out, held, arrived) = refs[:count], refs[count:]
    for i, at in by_chunk(*fetch(pieces, held, arrived)):
        out[i] = dot(held[at, :], weight[...])


def times(pieces, weight):
    width, cols = weight.shape
    count = len(pieces)
    return pl.pallas_call(
        lambda *refs: times_kernel(count, *refs),
        in_specs=[ANY] * count + [IN_VMEM],
        out_specs=IN_VMEM,
        out_shape=jax.ShapeDtypeStruct((8, CHUNK, cols), f32),
        scratch_shapes=[pltpu.VMEM((8 * CHUNK, width), bf16), pltpu.SemaphoreType.DMA((count,))],
        compiler_params=pltpu.CompilerParams(vmem_limit_bytes=LARGE),
        cost_estimate=lasting(5 + cols / 80),
        name="times",
    )(*pieces, weight)


def mixer_back_kernel(count, *refs):
    pieces = refs[:count]
    w_out, w_ctx, ssm_out, gating, es_out, context_out, sum_out, held, arrived = refs[count:]
    for i, at in by_chunk(*fetch(pieces, held, arrived)):
        es = dot_cols(held[at, :], w_out[...])
        es_out[i] = es
        context_out[i] = dot_cols(held[at, :], w_ctx[...]).astype(bf16)
        gate = gating[i]
        sum_out[i] = row_sums(es * ssm_out[i] * gate * sigmoid_of(gate))


def mixer_back(pieces, w_out, w_ctx, ssm_out, gating):
    count, width = len(pieces), w_out.shape[1]
    return pl.pallas_call(
        lambda *refs: mixer_back_kernel(count, *refs),
        in_specs=[ANY] * count + [IN_VMEM] * 4,
        out_specs=[IN_VMEM] * 3,
        out_shape=[
            jax.ShapeDtypeStruct((8, CHUNK, OWN_SSM), f32),
            jax.ShapeDtypeStruct((8, CHUNK, ATT_HEAD), bf16),
            jax.ShapeDtypeStruct((8, 8, CHUNK), f32),
        ],
        scratch_shapes=[pltpu.VMEM((8 * CHUNK, width), bf16), pltpu.SemaphoreType.DMA((count,))],
        compiler_params=pltpu.CompilerParams(vmem_limit_bytes=LARGE),
        cost_estimate=lasting(13),
        name="mixer_back",
    )(*pieces, w_out, w_ctx, ssm_out, gating)


def weight_grad_kernel(*refs):
    left, pieces, out = refs[0], refs[1:-1], refs[-1]
    starts = starts_of(pieces)
    total = dot(left[:, : starts[1]], pieces[0][...])
    for i in range(1, len(pieces)):
        total = total + dot(left[:, starts[i] : starts[i + 1]], pieces[i][...])
    out[...] = total.astype(bf16).reshape(out.shape)


def weight_grad(left, pieces, by_part=0):
    cols, rows = left.shape
    width = pieces[0].shape[1]
    parts = by_part or 4
    part = width // parts
    if by_part:
        out_spec = pl.BlockSpec((1, cols, part), lambda i: (i, 0, 0))
        out_shape = jax.ShapeDtypeStruct((parts, cols, part), bf16)
    else:
        out_spec = pl.BlockSpec((cols, part), lambda i: (0, i))
        out_shape = jax.ShapeDtypeStruct((cols, width), bf16)
    return pl.pallas_call(
        weight_grad_kernel,
        grid=(parts,),
        in_specs=[pl.BlockSpec((cols, rows), lambda i: (0, 0))]
        + [pl.BlockSpec((piece.shape[0], part), lambda i: (0, i)) for piece in pieces],
        out_specs=out_spec,
        out_shape=out_shape,
        compiler_params=pltpu.CompilerParams(vmem_limit_bytes=LARGE),
        cost_estimate=lasting(4 + cols / 100),
        name="weight_grad",
    )(left, *pieces)


def terms_kernel(count, turned, adds, scaled_by, *refs):
    lefts, weights = refs[:count], refs[count : 2 * count]
    rest = refs[2 * count :]
    norm = rest[0] if scaled_by else None
    got = rest[int(scaled_by) : int(scaled_by) + adds]
    outs = rest[int(scaled_by) + adds :]
    rows = outs[0].shape[0]
    half = rows // 2
    for k in range(ROWS):
        at = slice(k * rows, (k + 1) * rows)
        total = None
        for i in range(count):
            product = (dot_cols if turned else dot)(lefts[i][at, :], weights[i][...])
            if i == 0 and scaled_by:
                product = product * norm[at, 0:1]
            total = product if total is None else total + product
        if adds:
            total = total + got[k][...].astype(f32)
        if adds and k == 3:
            outs[3][...] = total[:half].astype(bf16)
            outs[4][...] = total[half:].astype(bf16)
        else:
            outs[k][...] = total.astype(outs[k].dtype)


def group_terms(lefts, weights, turned, core, got=(), norm=None):
    width = weights[0].shape[0 if turned else 1]
    rows = lefts[0].shape[0] // 8
    block = min(width, 512)
    in_specs = [
        pl.BlockSpec((ROWS * rows, left.shape[1]), lambda i, core=core: (core, 0)) for left in lefts
    ]
    for weight in weights:
        if turned:
            in_specs.append(pl.BlockSpec((block, weight.shape[1]), lambda i: (i, 0)))
        else:
            in_specs.append(pl.BlockSpec((weight.shape[0], block), lambda i: (0, i)))
    operands = list(lefts) + list(weights)
    if norm is not None:
        in_specs.append(pl.BlockSpec((ROWS * rows, 8), lambda i, core=core: (core, 0)))
        operands.append(norm)
    piece = pl.BlockSpec((rows, block), lambda i: (0, i))
    in_specs += [piece] * len(got)
    kinds = [(rows, f32)] * 3 + [(rows // 2, bf16)] * 2 if got else [(rows, bf16)] * 4
    depth = sum(left.shape[1] for left in lefts)
    return pl.pallas_call(
        lambda *refs: terms_kernel(len(lefts), turned, len(got), norm is not None, *refs),
        grid=(width // block,),
        in_specs=in_specs,
        out_specs=[pl.BlockSpec((n, block), lambda i: (0, i)) for n, _ in kinds],
        out_shape=[jax.ShapeDtypeStruct((n, width), kind) for n, kind in kinds],
        compiler_params=pltpu.CompilerParams(vmem_limit_bytes=LARGE),
        cost_estimate=lasting(4 + depth / 180),
        name="group_terms",
    )(*operands, *got)


def scatter_product(lefts, weights, turned=False, norm=None, give=False, meanwhile=None):
    other = group_terms(lefts, weights, turned, 1, norm=norm)
    got = [twin(part) for part in other]
    own, for_x, for_y, far_a, far_b = group_terms(lefts, weights, turned, 0, got=got, norm=norm)
    to_x, to_y = hop(far_a, 2), hop(far_b, 1)
    done = None
    if meanwhile is not None:
        done = meanwhile(own)
        to_x, to_y, done = lax.optimization_barrier((to_x, to_y, done))
    by_x, by_y = fold(for_x, for_y, to_x, to_y)
    sums = own, hop(by_x, 1), hop(by_y, 2)
    return (sums, done, own, by_x) if give else sums


def fold_kernel(for_x, for_y, to_x, to_y, by_x, by_y):
    half = to_x.shape[0]
    by_x[:half, :] = (for_x[:half, :] + to_x[...].astype(f32)).astype(bf16)
    by_x[half:, :] = for_x[half:, :].astype(bf16)
    by_y[:half, :] = for_y[:half, :].astype(bf16)
    by_y[half:, :] = (for_y[half:, :] + to_y[...].astype(f32)).astype(bf16)


def fold(for_x, for_y, to_x, to_y):
    rows, width = for_x.shape
    block = min(width, 512)
    spec = lambda n: pl.BlockSpec((n, block), lambda i: (0, i))
    return pl.pallas_call(
        fold_kernel,
        grid=(width // block,),
        in_specs=[spec(rows), spec(rows), spec(rows // 2), spec(rows // 2)],
        out_specs=[spec(rows), spec(rows)],
        out_shape=[jax.ShapeDtypeStruct((rows, width), bf16)] * 2,
        compiler_params=pltpu.CompilerParams(vmem_limit_bytes=VMEM),
        cost_estimate=lasting(2),
        name="fold",
    )(for_x, for_y, to_x, to_y)


def regroup(values, outer, part):
    count = values.shape[1] // part
    if count == 1:
        return values
    inner = count // outer
    order = [o * inner + i for i in range(inner) for o in range(outer)]
    return jnp.concatenate([values[:, k * part : (k + 1) * part] for k in order], axis=1)


def scaled_unit(values):
    scale = lax.rsqrt(jnp.mean(values * values, axis=1, keepdims=True) + EPSILON)
    return values * scale, scale


def norm_in_kernel(part, x, out):
    unit, _ = scaled_unit(x[...].astype(f32))
    out[...] = regroup(unit, ROWS, part).astype(bf16)


def norm_two_kernel(part, x, own, by_x, by_y, hidden_out, out):
    hidden = x[...].astype(f32) + own[...] + by_x[...].astype(f32) + by_y[...].astype(f32)
    hidden_out[...] = hidden
    unit, _ = scaled_unit(hidden)
    out[...] = regroup(unit, ROWS, part).astype(bf16)


def norm_back_kernel(part, values, own, by_x, by_y, base, *outs):
    unit, scale = scaled_unit(values[...].astype(f32))
    grad = own[...] + by_x[...].astype(f32) + by_y[...].astype(f32)
    grad = regroup(grad, grad.shape[1] // part // ROWS, part)
    mean = jnp.mean(grad * unit, axis=1, keepdims=True)
    total = base[...].astype(f32) + scale * (grad - unit * mean)
    for out in outs:
        out[...] = total.astype(out.dtype)


def on_rows(kernel, part, operands, kinds, name):
    rows, width = operands[0].shape
    step = rows // 4
    spec = pl.BlockSpec((step, width), lambda i: (i, 0))
    return pl.pallas_call(
        lambda *refs: kernel(part, *refs),
        grid=(4,),
        in_specs=[spec] * len(operands),
        out_specs=[spec] * len(kinds),
        out_shape=[jax.ShapeDtypeStruct((rows, width), kind) for kind in kinds],
        compiler_params=pltpu.CompilerParams(vmem_limit_bytes=VMEM),
        cost_estimate=lasting(4),
        name=name,
    )(*operands)


def turn(values, cosine, sine):
    return values * cosine + pltpu.roll(values, ATT_HEAD // 2, 1) * sine


def rope_kernel(where, query, key, value, cosine, sine, query_out, keyval_out):
    query_out[0, 0] = turn(query[0], cosine[0], sine[0]).astype(bf16)
    keyval_out[0, 0, :, :ATT_HEAD] = turn(key[0], cosine[0], sine[0]).astype(bf16)
    keyval_out[0, 0, :, ATT_HEAD:] = value[0].astype(bf16)


def rope_forward(where, proj, cosine, sine):
    def part(i):
        return pl.BlockSpec(
            (1, CHUNK, ATT_HEAD), lambda k, t, where: ((t ^ where[2]) * ROWS + k, 0, 4 + i)
        )

    angle = pl.BlockSpec((1, CHUNK, ATT_HEAD), lambda k, t, where: (t ^ where[2], 0, 0))
    return pl.pallas_call(
        rope_kernel,
        grid_spec=pltpu.PrefetchScalarGridSpec(
            num_scalar_prefetch=1,
            grid=(ROWS, 2),
            in_specs=[part(0), part(1), part(2), angle, angle],
            out_specs=[
                pl.BlockSpec((1, 1, CHUNK, ATT_HEAD), lambda k, t, where: (t ^ where[2], k, 0, 0)),
                pl.BlockSpec((1, 1, CHUNK, 2 * ATT_HEAD), lambda k, t, where: (k, t, 0, 0)),
            ],
        ),
        out_shape=[
            jax.ShapeDtypeStruct((2, ROWS, CHUNK, ATT_HEAD), bf16),
            jax.ShapeDtypeStruct((ROWS, 2, CHUNK, 2 * ATT_HEAD), bf16),
        ],
        compiler_params=pltpu.CompilerParams(vmem_limit_bytes=VMEM),
        cost_estimate=lasting(3),
        name="rope_forward",
    )(where, proj, proj, proj, cosine, sine)


def rope_back_kernel(where, query, keyval, cosine, sine, out):
    core, turned = cosine[0], -sine[0]
    out[0, :, :ATT_HEAD] = turn(query[0, 0], core, turned).astype(bf16)
    mine = pl.program_id(0) // 2 == where[2]
    both = jnp.where(mine, keyval[0, 0], 0.0)
    out[0, :, ATT_HEAD : 2 * ATT_HEAD] = turn(both[:, :ATT_HEAD], core, turned).astype(bf16)
    out[0, :, 2 * ATT_HEAD :] = both[:, ATT_HEAD:].astype(bf16)


def rope_back(where, query, keyval, cosine, sine):
    angle = pl.BlockSpec((1, CHUNK, ATT_HEAD), lambda k, t, where: (t ^ where[2], 0, 0))
    return pl.pallas_call(
        rope_back_kernel,
        grid_spec=pltpu.PrefetchScalarGridSpec(
            num_scalar_prefetch=1,
            grid=(ROWS, 2),
            in_specs=[
                pl.BlockSpec((1, 1, CHUNK, ATT_HEAD), lambda k, t, where: (t ^ where[2], k, 0, 0)),
                pl.BlockSpec((1, 1, CHUNK, 2 * ATT_HEAD), lambda k, t, where: (k % 2, t, 0, 0)),
                angle,
                angle,
            ],
            out_specs=pl.BlockSpec(
                (1, CHUNK, 3 * ATT_HEAD), lambda k, t, where: ((t ^ where[2]) * ROWS + k, 0, 0)
            ),
        ),
        out_shape=jax.ShapeDtypeStruct((2 * ROWS, CHUNK, 3 * ATT_HEAD), bf16),
        compiler_params=pltpu.CompilerParams(vmem_limit_bytes=VMEM),
        cost_estimate=lasting(3),
        name="rope_back",
    )(where, query, keyval, cosine, sine)


def feed_kernel(count, *refs):
    n2, g = refs[:count], refs[count : 2 * count]
    w_gu, w_down, act_out, grad_out, held_n, held_g, arrived_n, arrived_g = refs[2 * count :]
    copies_n, starts = fetch(n2, held_n, arrived_n)
    copies_g, _ = fetch(g, held_g, arrived_g)
    own = w_down.shape[0]
    for (i, at), _ in zip(by_chunk(copies_n, starts), by_chunk(copies_g, starts)):
        both = dot(held_n[at, :], w_gu[...])
        gate, up = both[:, :own], both[:, own:]
        sig = sigmoid_of(gate)
        silu = gate * sig
        act_out[at, :] = (silu * up).astype(bf16)
        grad = dot_cols(held_g[at, :], w_down[...])
        grad_out[at, :own] = (grad * up * (sig * (1.0 + gate * (1.0 - sig)))).astype(bf16)
        grad_out[at, own:] = (grad * silu).astype(bf16)


def feed(n2, g, w_gu, w_down):
    own, width = w_down.shape
    count, rows = len(n2), 8 * CHUNK
    return pl.pallas_call(
        lambda *refs: feed_kernel(count, *refs),
        in_specs=[ANY] * (2 * count) + [IN_VMEM] * 2,
        out_specs=[IN_VMEM] * 2,
        out_shape=[
            jax.ShapeDtypeStruct((rows, own), bf16),
            jax.ShapeDtypeStruct((rows, 2 * own), bf16),
        ],
        scratch_shapes=[
            pltpu.VMEM((rows, width), bf16),
            pltpu.VMEM((rows, width), bf16),
            pltpu.SemaphoreType.DMA((count,)),
            pltpu.SemaphoreType.DMA((count,)),
        ],
        compiler_params=pltpu.CompilerParams(vmem_limit_bytes=LARGE),
        cost_estimate=lasting(23),
        name="feed",
    )(*n2, *g, w_gu, w_down)


def per_device(
    tokens,
    segments,
    cotangent,
    norm_gain,
    gating_weight,
    input_weight,
    state_weight,
    step_weight,
    conv_weight,
    conv_bias,
    step_bias,
    decay_log,
    skip_gain,
    ssm_gain,
    out_weight,
    query_weight,
    keyval_weight,
    context_weight,
    mlp_gain,
    gate_weight,
    up_weight,
    down_weight,
):
    zs = lax.axis_size("z")
    b = lax.axis_index("b")
    z = lax.axis_index("z")
    c = lax.axis_index("c")
    rank = 2 * b + c
    rows = tokens.shape[1]
    width = tokens.shape[2]
    share = norm_gain.shape[0]
    ssm_width = HEADS * SSM_HEAD
    score_scale = 1.0 / math.sqrt(ATT_HEAD)

    def to_z(values):
        return (
            values.reshape(rows, ROWS, zs, 2 * share).transpose(0, 2, 1, 3).reshape(rows, width)
        )

    def from_z(values):
        return (
            values.reshape(rows, zs, ROWS, 2 * share).transpose(0, 2, 1, 3).reshape(rows, width)
        )

    def swap(values):
        return jnp.where(c == 0, values, values[::-1])

    def to_ranks(values):
        return lax.all_to_all(values, ("b", "c"), split_axis=0, concat_axis=0, tiled=True)

    def to_owner(values):
        mine = lax.psum_scatter(values, "z", scatter_dimension=0, tiled=True)[0]
        return mine.T.reshape(RANKS, share, -1)

    def along_z(values):
        return lax.all_gather(values, "z", axis=0, tiled=True)

    def owner_z(values):
        return lax.psum_scatter(values, "z", scatter_dimension=0, tiled=True)

    x = tokens[0]
    cot = cotangent[0]
    aligned = 2 * share % 128 == 0
    block = 2 * share if aligned else width
    lined = (lambda v: v) if aligned else to_z
    unlined = (lambda v: v) if aligned else from_z
    gain_col = norm_gain.astype(f32)[:, None]
    gain2_col = mlp_gain.astype(f32)[:, None]
    ssm_gain_col = ssm_gain.astype(f32)[:, None]

    (n1_own,) = on_rows(norm_in_kernel, block, [x], [bf16], "norm_in")
    scaled = lambda w, gain: (w.astype(f32) * gain).astype(bf16)
    by_rank = lambda w: w.reshape(w.shape[0], RANKS, -1).transpose(1, 0, 2)
    group_kv = KVHEADS * ATT_HEAD
    kv_heads = keyval_weight.reshape(share, 2, KVHEADS, ATT_HEAD).transpose(2, 0, 1, 3)
    kv_rank = jnp.repeat(kv_heads.reshape(KVHEADS, share, 2 * ATT_HEAD), RANKS // KVHEADS, axis=0)
    pad_cols = 128 - OWN_STATE - 8
    chan = conv_bias.shape[0]
    small = jnp.concatenate(
        [segments[0].astype(bf16), conv_weight.reshape(-1), conv_bias.reshape(-1)]
    )
    small_count = small.shape[0]
    small = jnp.pad(small, (0, share * pad_cols - small_count)).reshape(share, pad_cols)
    w_a = jnp.concatenate(
        [
            by_rank(input_weight),
            by_rank(state_weight),
            by_rank(step_weight),
            jnp.zeros((RANKS, share, 8 - OWN_HEADS), bf16),
        ],
        axis=2,
    )
    riders = jnp.broadcast_to(small[None], (RANKS, share, pad_cols))
    w_b = jnp.concatenate([by_rank(query_weight), kv_rank], axis=2)
    w_c = by_rank(gating_weight)
    cols_a, cols_b, cols_c = w_a.shape[2] + pad_cols, w_b.shape[2], w_c.shape[2]
    own_ab = to_ranks(
        jnp.concatenate([scaled(w_a, gain_col[None]), riders, scaled(w_b, gain_col[None])], axis=2)
    )
    w_ab = along_z(own_ab)
    small = w_ab[..., cols_a - pad_cols : cols_a].reshape(zs, ROWS, 2, -1)[..., :small_count]
    w_ab = w_ab.reshape(width, cols_a + cols_b)
    wa, wb = w_ab[:, :cols_a], w_ab[:, cols_a:]
    def ff_ranks(w):
        return (
            w.reshape(w.shape[0], ROWS, zs, 2, -1)
            .transpose(1, 3, 0, 2, 4)
            .reshape(RANKS, w.shape[0], -1)
        )

    w_cgu = jnp.concatenate(
        [
            scaled(w_c, gain_col[None]),
            scaled(
                jnp.concatenate([ff_ranks(gate_weight), ff_ranks(up_weight)], axis=2),
                gain2_col[None],
            ),
        ],
        axis=2,
    )
    n1, w_cgu = gather_group(lined(n1_own), w_cgu)
    own_cgu = to_ranks(w_cgu)
    own_c, w_gu = own_cgu[..., :cols_c], own_cgu[..., cols_c:]
    own_ff = w_gu.shape[2] // 2

    row_out = out_weight.shape[0]
    row_ctx = context_weight.shape[0]
    w_oc = jnp.concatenate([scaled(out_weight, ssm_gain_col), context_weight], axis=0)[None]
    segs = small[..., :rows].transpose(1, 0, 2, 3).reshape(ROWS, zs * 2 * rows).astype(f32)
    segs_all = jnp.concatenate(
        [lax.dynamic_slice_in_dim(segs, k ^ b, 1, 0) for k in range(ROWS)], axis=0
    )
    conv_all = small[..., rows:].transpose(1, 0, 2, 3).reshape(-1, CONV + 1, chan).astype(f32)
    conv_all = conv_all.transpose(1, 0, 2).reshape(CONV + 1, -1)
    conv_own = jnp.concatenate(
        [
            lax.dynamic_slice_in_dim(conv_all, rank * OWN_SSM, OWN_SSM, 1),
            lax.dynamic_slice_in_dim(conv_all, ssm_width + rank * OWN_STATE, OWN_STATE, 1),
        ],
        axis=1,
    )
    seg_pad = jnp.concatenate([jnp.zeros((ROWS, rows), f32), segs_all], axis=1)
    seg_near = lax.dynamic_slice_in_dim(seg_pad, z * 2 * rows, 3 * rows, 1)
    seg_time = seg_near[:, rows:].reshape(ROWS, 2, rows).transpose(1, 0, 2)
    seg = swap(seg_time).reshape(2 * ROWS, rows)
    seg_before = seg_near[:, : 2 * rows].reshape(ROWS, 2, rows).transpose(1, 0, 2)
    seg_before = swap(seg_before).reshape(2 * ROWS, rows)
    marks = marks_of(seg, seg_before)
    seg_rows = jnp.broadcast_to(seg[:, None, :], (2 * ROWS, 8, rows))
    seg_query = marks.reshape(2, ROWS, rows, 8)
    seg_keys = segs_all.reshape(ROWS * zs, 1, 2 * rows)
    seg_keys = jnp.broadcast_to(seg_keys, (ROWS * zs, 8, 2 * rows))
    where = jnp.stack([b, z, c]).astype(jnp.int32)
    conv_own = jnp.pad(conv_own, ((0, 3), (0, LANES_A - OWN_CONV)))
    own_slice = lambda v: lax.dynamic_slice_in_dim(v.astype(f32), rank * OWN_HEADS, OWN_HEADS, 0)
    rate = -jnp.exp(own_slice(decay_log))
    head = jnp.pad(jnp.stack([own_slice(step_bias), rate]), ((0, 6), (0, 128 - OWN_HEADS)))
    skip_wide = jnp.broadcast_to(jnp.repeat(own_slice(skip_gain), SSM_HEAD)[None], (8, OWN_SSM))

    half_head = ATT_HEAD // 2
    frequency = jnp.exp(jnp.arange(half_head, dtype=f32) * (-2.0 * math.log(ROPE_BASE) / ATT_HEAD))
    core_place = (z * 2 + (jnp.arange(2) ^ c)) * rows
    places = (core_place[:, None] + jnp.arange(rows)[None, :]).astype(f32)
    angles = (places[:, :, None] * frequency).reshape(2, rows, half_head)
    cosine, sine = jnp.cos(angles), jnp.sin(angles)
    cosine = jnp.concatenate([cosine, cosine], axis=-1)
    sine = jnp.concatenate([-sine, sine], axis=-1)

    chunks = 2 * ROWS
    proj = times(n1, after(w_ab, own_cgu))
    g_all, proj = gather_group(after(cot, own_cgu), proj)
    query, keyval = rope_forward(where, proj, cosine, sine)
    own_kv = lax.dynamic_slice_in_dim(keyval, 2 * c, 2, 0).reshape(1, 2, 2 * rows, 2 * ATT_HEAD)
    kv_own = along_z(own_kv)

    def before_chunk(own_last, moved):
        return jnp.stack(
            [jnp.where(c == 0, moved, own_last[1]), jnp.where(c == 0, own_last[0], moved)]
        )

    tails = after(proj[:, rows - 8 :, :cols_a], where)
    tails = tails.reshape(2, ROWS, 8, cols_a).astype(bf16)
    last_core = jnp.where(c == 0, tails[1], tails[0])
    moved = zshift(last_core[:, 8 - CONV + 1 :], 1)
    moved = jnp.pad(moved, ((0, 0), (8 - CONV + 1, 0), (0, 0)))
    halo = before_chunk(tails, moved).reshape(chunks, 8, cols_a).astype(f32)
    xs, bc_own, slope, meta, meta_rows = conv_forward(proj, halo, marks, conv_own, head)
    bc_own = after(bc_own, *g_all)
    mine = [bc_own] + [hop(bc_own, m) for m in range(1, ROWS)]
    mine = jnp.stack(mine)
    bc = jnp.concatenate([mine, twin(mine)], axis=0)
    wc = along_z(after(own_c, own_kv)).reshape(width, cols_c)

    passing = jnp.exp(meta[:, rows - 1, 8 : 8 + OWN_HEADS]) * marks[:, rows - 1, 1:2]
    pass_wide = swap(jnp.repeat(passing, SSM_HEAD, axis=1).reshape(2, ROWS, OWN_SSM, 1))
    p0, p1 = pass_wide[0], pass_wide[1]
    pass_both = p0 * p1
    first_local, both_local = local_states(where, xs, bc, meta, marks, p1)
    kv_other = twin(kv_own)
    state = jnp.zeros_like(both_local)
    for s in range(zs - 1):
        message = (pass_both * state + both_local).astype(bf16)
        if s == 1:
            query = after(query, message)
            context, context_low, logsum = attend(
                where, query, kv_own, kv_other, seg_query, seg_keys
            )
            gating = times(n1, after(wc, message))
        moved = lax.ppermute(message, "z", [(s, s + 1)])
        if s == 1:
            moved, context_low, gating = lax.optimization_barrier((moved, context_low, gating))
        state = state + moved.astype(f32)

    w_oc = along_z(after(w_oc, state))
    halves = w_oc.reshape(2, zs // 2, row_out + row_ctx, width)
    kept = lax.dynamic_index_in_dim(halves, c, 0, keepdims=False)
    sent = lax.dynamic_index_in_dim(halves, 1 - c, 0, keepdims=False)
    got = twin(sent)
    both = jnp.where(c == 0, jnp.stack([kept, got], 1), jnp.stack([got, kept], 1))
    w_out = both[:, :, :row_out].reshape(-1, width)
    w_ctx = both[:, :, row_out:].reshape(-1, width)
    w_gu_full = along_z(after(w_gu, state)).reshape(width, 2 * own_ff)
    w_down = along_z(after(down_weight, w_gu, state))

    ssm_out, gated_low, squares = ssm_forward(
        where, xs, bc, meta, meta_rows, marks, seg_rows, state, first_local, p0, gating, skip_wide
    )
    squares = sum_group(squares[:, 0].reshape(2, ROWS, rows))
    scale_ssm = lax.rsqrt(squares * (1.0 / ssm_width) + EPSILON).reshape(chunks, rows, 1)

    flat = lambda v: v.reshape(-1, v.shape[-1])
    norms = jnp.broadcast_to(scale_ssm.reshape(-1, 1), (chunks * rows, 8))
    mixed = scatter_product([flat(gated_low), flat(context_low)], [w_out, w_ctx], norm=norms)
    hidden, n2_own = on_rows(norm_two_kernel, block, [x, *mixed], [f32, bf16], "norm_two")

    n2 = gather_group(lined(n2_own))
    activation, grad_gu = feed(n2, g_all, w_gu_full, w_down)

    e2, grad_down_terms, _, folded = scatter_product(
        [grad_gu],
        [w_gu_full],
        turned=True,
        give=True,
        meanwhile=lambda own: weight_grad(after(activation, own).T, g_all),
    )
    grad_down = owner_z(grad_down_terms)
    grad_gu_terms = weight_grad(after(grad_gu, folded).T, n2, zs)
    e2 = (after(e2[0], grad_gu_terms),) + e2[1:]
    grad_gu_w = to_owner(grad_gu_terms)
    grad_hidden, grad_mix_own = on_rows(
        norm_back_kernel, block, [hidden, *map(unlined, e2), cot], [f32, bf16], "norm_back"
    )
    grad_mix = gather_group(grad_mix_own)
    (late_own, late_x, late_y), _, _, late_folded = scatter_product(
        [after(activation, grad_mix_own)], [w_down], give=True
    )
    es, grad_context, es_sum = mixer_back(
        grad_mix, after(w_out, late_own), w_ctx, ssm_out, gating
    )
    es_sum = es_sum[:, 0] * scale_ssm[..., 0]
    es_mean = sum_group(es_sum.reshape(2, ROWS, rows)) * (1.0 / ssm_width)
    scales = jnp.pad(
        jnp.stack([scale_ssm[..., 0], es_mean.reshape(chunks, rows)], axis=-1),
        ((0, 0), (0, 0), (0, 6)),
    )
    gy, grad_gating, unit_low, later_grad, both_grad = gate_back(
        where, es, scales, gating, ssm_out, bc, meta, marks, p0
    )

    def out_grads(unit_low):
        mixer_in = jnp.concatenate([flat(unit_low), flat(context_low)], axis=-1)
        grad_oc_w = weight_grad(mixer_in.T, grad_mix)
        grad_out_rows = grad_oc_w[:OWN_SSM].reshape(zs // 2, 2, row_out, width)
        grad_ctx_rows = grad_oc_w[OWN_SSM:].reshape(zs // 2, 2, row_ctx, width)
        grad_oc = jnp.concatenate([grad_out_rows, grad_ctx_rows], axis=2)
        oc_kept = lax.dynamic_index_in_dim(grad_oc, c, 1, keepdims=False)
        oc_got = twin(lax.dynamic_index_in_dim(grad_oc, 1 - c, 1, keepdims=False))
        return jnp.where(
            c == 0,
            jnp.concatenate([oc_kept, oc_got], axis=0),
            jnp.concatenate([oc_got, oc_kept], axis=0),
        )

    flowing = jnp.zeros_like(both_grad)
    grad_c_low = flat(grad_gating)
    for s in range(zs - 1, 0, -1):
        message = (pass_both * flowing + both_grad).astype(bf16)
        if s == 1:
            grad_context = after(grad_context, message).reshape(2, ROWS, rows, ATT_HEAD)
            grad_query, grad_kv = attend_back(
                where, query, kv_own, kv_other, seg_query, seg_keys, grad_context, context, logsum
            )
            grad_wc_terms = weight_grad(after(grad_c_low, message).T, n1, zs)
            kv_kept = lax.dynamic_slice_in_dim(grad_kv, 2 * c, 2, 1).astype(f32)
            kv_got = twin(lax.dynamic_slice_in_dim(grad_kv, 2 - 2 * c, 2, 1)).astype(f32)
            kv_terms = (kv_kept + kv_got).astype(bf16)
        moved = lax.ppermute(message, "z", [(s, s - 1)])
        if s == zs - 1:
            oc_all = out_grads(after(unit_low, message))
            moved, oc_all, late_folded = lax.optimization_barrier((moved, oc_all, late_folded))
        if s == zs - 2:
            got_gu = to_ranks(after(grad_gu_w, message, grad_down))
            moved, got_gu, late_x, late_y = lax.optimization_barrier(
                (moved, got_gu, late_x, late_y)
            )
            grad_oc_own = owner_z(after(oc_all, got_gu))
        if s == 1:
            moved, grad_query, kv_terms, grad_wc_terms, grad_oc_own = lax.optimization_barrier(
                (moved, grad_query, kv_terms, grad_wc_terms, grad_oc_own)
            )
        flowing = flowing + moved.astype(f32)
    grad_wc = to_owner(grad_wc_terms)

    kv_grad = owner_z(kv_terms)
    kv_grad = kv_grad[0].astype(f32)
    grad_b_low = rope_back(
        where, grad_query, kv_grad.reshape(2, 2, rows, 2 * ATT_HEAD), cosine, sine
    )
    grad_b_low = flat(grad_b_low)
    grad_wb_terms = weight_grad(grad_b_low.T, n1, zs)
    grad_wb = to_owner(grad_wb_terms)

    got_gu = got_gu.astype(f32)
    grad_xs, *bc_terms, grad_step, head_sums = ssm_back(
        where, xs, gy, bc, meta, meta_rows, marks, seg_rows, state, first_local, flowing, later_grad,
        p0, p1, skip_wide, head,
    )
    got = twin(jnp.stack(bc_terms[ROWS:])).astype(f32)
    bc_sums = [bc_terms[k].astype(f32) + got[k] for k in range(ROWS)]
    grad_bc = bc_sums[0]
    for k in range(1, ROWS):
        grad_bc = grad_bc + hop(bc_sums[k].astype(bf16), k).astype(f32)

    near = CONV - 1
    bc_near = grad_bc[:, :near].reshape(ROWS, near, 2, PIECE).transpose(2, 0, 1, 3)
    grad_near = jnp.concatenate(
        [grad_xs[:, :near], bc_near.reshape(chunks, near, PIECE)], axis=-1
    )
    grad_near = grad_near * slope[:, :near, :OWN_CONV]
    give = jnp.zeros((chunks, near, OWN_CONV), f32)
    for o in range(near):
        masked = grad_near[:, : near - o] * marks[:, : near - o, 3 + o : 4 + o]
        give = give + jnp.pad(masked * conv_own[o, :OWN_CONV], ((0, 0), (o, 0), (0, 0)))
    give = give.reshape(2, ROWS, near, OWN_CONV)
    moved = zshift(jnp.where(c == 0, give[0], give[1]).astype(bf16), -1).astype(f32)
    given = jnp.stack(
        [jnp.where(c == 0, give[1], moved), jnp.where(c == 0, moved, give[0])]
    ).reshape(chunks, near, OWN_CONV)
    given = after(given, grad_wb_terms)
    given = jnp.pad(given, ((0, 0), (8 - near, 0), (0, LANES_A - OWN_CONV)))
    grad_a_low, conv_sums = conv_backward(
        grad_xs, grad_bc, grad_step, slope, proj, halo, marks, given, conv_own
    )
    grad_a_low = flat(grad_a_low)
    conv_sums = jnp.sum(conv_sums, axis=0)[: CONV + 1, :OWN_CONV]
    head_sums = jnp.sum(head_sums, axis=0)[:3, :OWN_HEADS] * jnp.stack(
        [jnp.ones_like(rate), rate, jnp.ones_like(rate)]
    )
    head_sums = jnp.pad(head_sums.reshape(1, -1), ((0, 0), (0, OWN_CONV - 3 * OWN_HEADS)))

    def all_sums(sums):
        total = sums
        for flip in range(1, zs):
            total = total + zhop(sums, flip)
        table = jnp.stack([total, twin(total)])
        return jnp.concatenate([table] + [hop(table, flip) for flip in range(1, ROWS)], axis=0)

    grad_wa_terms = weight_grad(grad_a_low.T, n1, zs)
    grad_a_low = after(grad_a_low, grad_wa_terms)
    e1, _, _, e1_folded = scatter_product(
        [grad_c_low, grad_b_low, grad_a_low], [wc, wb, wa], turned=True, give=True
    )
    grad_wa = to_owner(grad_wa_terms)
    late_own = after(late_own, e1_folded)
    result = (hidden + late_own + late_x.astype(f32) + late_y.astype(f32)).astype(bf16)
    grad_oc_own = grad_oc_own[0].astype(f32)
    sums = jnp.concatenate([conv_sums, head_sums], axis=0)
    got_bc = to_ranks(after(jnp.concatenate([grad_wb, grad_wc], axis=2), e1_folded))
    got_a = to_ranks(grad_wa)
    table = all_sums(sums)
    e1 = (after(e1[0], got_bc, table),) + e1[1:]
    (grad_x,) = on_rows(
        norm_back_kernel, block, [x, *map(unlined, e1), grad_hidden], [bf16], "norm_back_in"
    )

    def unrank(values):
        return values.transpose(1, 0, 2).reshape(share, -1)

    got_a, got_bc = got_a.astype(f32), got_bc.astype(f32)
    got_b, got_c = got_bc[..., :cols_b], got_bc[..., cols_b:]
    d_input = unrank(got_a[..., :OWN_SSM])
    d_state = unrank(got_a[..., OWN_SSM:OWN_CONV])
    d_step = unrank(got_a[..., OWN_CONV : OWN_CONV + OWN_HEADS])
    d_query = unrank(got_b[..., :ATT_HEAD])
    d_kv = got_b[..., ATT_HEAD:].reshape(KVHEADS, RANKS // KVHEADS, share, 2, ATT_HEAD).sum(1)
    d_kv = d_kv.transpose(1, 2, 0, 3).reshape(share, 2 * group_kv)
    d_gating = unrank(got_c)

    def ff_unrank(values):
        return (
            values.reshape(ROWS, 2, share, zs, own_ff // zs)
            .transpose(2, 0, 3, 1, 4)
            .reshape(share, -1)
        )

    d_gate, d_up = ff_unrank(got_gu[..., :own_ff]), ff_unrank(got_gu[..., own_ff:])

    def gain_grad(pairs):
        return sum(jnp.sum(w.astype(f32) * d, axis=1) for w, d in pairs)

    d_norm_gain = gain_grad(
        (
            (gating_weight, d_gating),
            (input_weight, d_input),
            (state_weight, d_state),
            (step_weight, d_step),
            (query_weight, d_query),
            (keyval_weight, d_kv),
        )
    )
    d_mlp_gain = gain_grad(((gate_weight, d_gate), (up_weight, d_up)))
    d_out = grad_oc_own[:row_out]
    d_ctx = grad_oc_own[row_out:]
    d_ssm_gain = gain_grad(((out_weight, d_out),))

    place = jnp.arange(RANKS)
    chosen = ((place ^ rank)[:, None] == place[None, :]).astype(f32)
    table = jnp.einsum("rs,sof->rof", chosen, table, precision=HIGH)
    conv_ssm = table[:, : CONV + 1, :OWN_SSM].transpose(1, 0, 2).reshape(CONV + 1, -1)
    conv_state = table[:, : CONV + 1, OWN_SSM:].transpose(1, 0, 2).reshape(CONV + 1, -1)
    conv_full = jnp.concatenate([conv_ssm, conv_state], axis=1)
    conv_mine = lax.dynamic_slice_in_dim(conv_full, (rank // 2 * zs * 2 + z * 2 + c) * chan, chan, 1)
    heads = table[:, CONV + 1, : 3 * OWN_HEADS].reshape(RANKS, 3, OWN_HEADS)
    heads = heads.transpose(1, 0, 2).reshape(3, HEADS)

    return (
        result[None],
        grad_x[None],
        d_norm_gain,
        d_gating * gain_col,
        d_input * gain_col,
        d_state * gain_col,
        d_step * gain_col,
        conv_mine[:CONV],
        conv_mine[CONV],
        heads[0],
        heads[1],
        heads[2],
        d_ssm_gain,
        d_out * ssm_gain_col,
        d_query * gain_col,
        d_kv * gain_col,
        d_ctx,
        d_mlp_gain,
        d_gate * gain2_col,
        d_up * gain2_col,
        grad_down.astype(f32),
    )


def solution(mesh):
    places = mesh.devices.reshape(ROWS, mesh.shape["seq"] // 2, 2)
    split = Mesh(places, ("b", "z", "c"))
    everywhere = ("b", "z", "c")
    row = P(everywhere, None)
    vector = P(everywhere)
    token = P("b", ("z", "c"), None)
    return jax.shard_map(
        per_device,
        mesh=split,
        in_specs=(
            token,
            P("b", ("z", "c")),
            token,
            vector,
            row,
            row,
            row,
            row,
            P(None, everywhere),
            vector,
            P(),
            P(),
            P(),
            vector,
            row,
            row,
            row,
            row,
            vector,
            row,
            row,
            row,
        ),
        out_specs=(
            token,
            token,
            vector,
            row,
            row,
            row,
            row,
            P(None, everywhere),
            vector,
            P(),
            P(),
            P(),
            vector,
            row,
            row,
            row,
            row,
            vector,
            row,
            row,
            row,
        ),
        check_vma=False,
    )
```

time: 1290 us -> 1060 us (0.82)
  Pallas kernels: 0 us -> 392 us
  matrix products: 272 us -> 0.23 us
  local copies, waits for them, and re-layouts: 318 us -> 116 us
  other arithmetic: 185 us -> 59.5 us
  waiting for transfers between devices: 300 us -> 359 us
  starting transfers between devices: 142 us -> 90.2 us
  blocking collectives: 41.7 us -> 19.2 us
    pallas_call x0 -> x37, Pallas kernels: none -> 392 us  [the longest x8 66.3 us: group_terms(): pl.pallas_call(lambda *refs: terms_kernel(len(lefts), turned, len(got), n...]
    dot_general x40 -> x0, matrix products: 272 us -> none  [the longest x20 176 us: dot(): lax.dot_general(left, right, (dims, ((), ())), preferred_element_type=f32)]
    unnamed x515 -> x179, local copies, waits for them, and re-layouts: 128 us -> 21.7 us
    another operation x13 -> x8, local copies, waits for them, and re-layouts: 45.7 us -> 0.5 us  [the longest x3 0.38 us: per_device(): jnp.stack([scale_ssm[..., 0], es_mean.reshape(chunks, rows)], axis=-1)]
    all_gather x6, waiting for transfers between devices: 0.05 us -> 34.2 us  [along_z(): return lax.all_gather(values, 'z', axis=0, tiled=True)]
    reduce_sum x15 -> x2, other arithmetic: 33.6 us -> 0.03 us  [the longest x1 0.01 us: per_device(): jnp.sum(head_sums, axis=0)[:3, :OWN_HEADS]]
    ppermute x10 -> x3, starting transfers between devices: 37.9 us -> 4.45 us  [zhop(): lax.ppermute(values, 'z', [(i, i ^ flip) for i in range(lax.axis_size('z'...]
    all_to_all x4, waiting for transfers between devices: 13.4 us -> 41.2 us  [to_ranks(): lax.all_to_all(values, ('b', 'c'), split_axis=0, concat_axis=0, tiled=True)]
  transfers between devices with their start and end apart: 130 -> 120, of which waited for: 44 -> 58; matrix products, arithmetic and copies ran while one was open for 54% -> 13% of each run, Pallas kernels for 0% -> 31%
where the time goes in v2:
time: 1060 us; the launch traced here: 1050 us
  Pallas kernels  392 us (37%)
  waiting for transfers between devices  359 us (34%)
  local copies, waits for them, and re-layouts  116 us (11%)
  starting transfers between devices  90.2 us (9%)
  other arithmetic  59.5 us (6%)
  blocking collectives  19.2 us (2%)
  between operations  16.2 us (2%)
    ppermute x47, waiting for transfers between devices, hop(): return lax.ppermute(values, 'b', [(i, i ^ flip) for i in range(ROWS)])  229 us
    pallas_call x8, Pallas kernels, group_terms(): pl.pallas_call(lambda *refs: terms_kernel(len(lefts), turned, len(got), n...  66.3 us
    pallas_call x6, Pallas kernels, weight_grad(): pl.pallas_call(weight_grad_kernel, grid=(parts,), in_specs=[pl.BlockSpec(...  62.7 us
    ppermute x47, starting transfers between devices, hop(): return lax.ppermute(values, 'b', [(i, i ^ flip) for i in range(ROWS)])  50.1 us
    all_to_all x4, waiting for transfers between devices, to_ranks(): lax.all_to_all(values, ('b', 'c'), split_axis=0, concat_axis=0, tiled=True)  41.2 us
    pallas_call x1, Pallas kernels, ssm_back(): pl.pallas_call(ssm_back_kernel, grid_spec=pltpu.PrefetchScalarGridSpec(nu...  39.4 us
    all_gather x6, waiting for transfers between devices, along_z(): return lax.all_gather(values, 'z', axis=0, tiled=True)  34.2 us
    pallas_call x2, Pallas kernels, times(): pl.pallas_call(lambda *refs: times_kernel(count, *refs), in_specs=[ANY] *...  26.5 us
  transfers between devices with their start and end apart: 120, of which 58 were waited for; matrix products, arithmetic and copies ran while one was open for 13% of the time, Pallas kernels for 31%

profile of v2, /device:TPU:0, one launch (start us, length us, event | category | flops | bytes accessed | tf_op | source)
XLA Modules:
  0.0 1052.6 jit_solution(13766079763802376315)
XLA Ops:
  15.2 19.2 %all_to_all.25 = bf16[8,64,896]{2,1,0:T(8,128)(2,1)} all-to-all(bf16[8,64,896]{2,1,0:T(8,128)(2,1)S(1)} %copy.265), channel_id=1, replica_groups=mesh['b'=4,'z'=4,'c'=2] {'b','c'}, dimensions={0} | all-to-all | bytes 1835008 | tf_op jit(solution)/shard_map/all_to_all | solution.py:1224
  42.7 20.2 %collective-permute-done.refs_1_.refs_2_ = bf16[256,2048]{1,0:T(8,128)(2,1)S(1)} collective-permute-done((bf16[256,2048]{1,0:T(8,128)(2,1)}, bf16[256,2048]{1,0:T(8,128)(2,1)S(1)}, u32[]{:S(2)}, u32[]{:S(2)}) %collective-permute-start) | collective-permute-done | bytes 1048608 | tf_op jit(solution)/shard_map/ppermute | solution.py:62
  74.6 13.3 %all-to-all-done = bf16[8,64,1408]{2,1,0:T(8,128)(2,1)} async-done(((bf16[8,64,1408]{2,1,0:T(8,128)(2,1)}), bf16[8,64,1408]{2,1,0:T(8,128)(2,1)}, u32[]{:S(2)}, u32[]{:S(2)}) %all-to-all-start) | async-done | bytes 1441824 | tf_op jit(solution)/shard_map/all_to_all | solution.py:1224
  107.6 16.4 %times.2.proj.query.key.value = f32[8,256,896]{2,1,0:T(8,128)} custom-call(bf16[256,2048]{1,0:T(8,128)(2,1)} %norm_in.1.refs_0_.refs_1_, bf16[256,2048]{1,0:T(8,128)(2,1)} %copy-done.2, bf16[256,2048]{1,0:T(8,128)(2,1)} %collective-permute-done.1.refs_2_.refs_3_, bf16[128,2048]{1,0:T(8,128)(2,1)} %copy-done.7, bf16[128,2048]{1,0:T(8,128)(2,1)} %copy-done.8, ...), custom_call_target="tpu_custom_call" | custom-call | bytes 17820000 | tf_op jit(solution)/shard_map/times/pallas_call | solution.py:843
  164.8 11.9 %conv_forward.1 = (bf16[8,256,384]{2,1,0:T(8,128)(2,1)}, bf16[4,256,128]{2,1,0:T(8,128)(2,1)}, f32[8,256,512]{2,1,0:T(8,128)}, f32[8,256,32]{2,1,0:T(8,128)}, f32[8,16,256]{2,1,0:T(8,128)}) custom-call(f32[8,256,896]{2,1,0:T(8,128)} %times.2.proj.query.key.value, f32[8,8,512]{2,1,0:T(8,128)} %bitcast_convert_fusion.halo, f32[8,256,8]{2,1,0:T(8,128)} %marks.1, ...), custom_call_target="tpu_custom_call" | custom-call | bytes 8800000 | tf_op jit(solution)/shard_map/conv_forward/pallas_call | solution.py:241
  202.2 11.4 %local_states.1 = (f32[4,384,256]{2,1,0:T(8,128)}, f32[4,384,256]{2,1,0:T(8,128)}) custom-call(s32[3]{0:T(128)} %pad_add_fusion.1.where, bf16[8,256,384]{2,1,0:T(8,128)(2,1)} %get-tuple-element.164.xs, bf16[8,4,256,128]{3,2,1,0:T(8,128)(2,1)} %copy-done, bf16[8,4,256,128]{3,2,1,0:T(8,128)(2,1)} %copy-done, bf16[8,4,256,128]{3,2,1,0:T(8,128)(2,1)} %copy-done, ...), custom_call_target="tpu_custom_call" | custom-call | bytes 8800000 | tf_op jit(solution)/shard_map/local_states/pallas_call | solution.py:340
  219.8 17.0 %collective-permute-done.23 = bf16[4,384,256]{2,1,0:T(8,128)(2,1)S(1)} collective-permute-done((bf16[4,384,256]{2,1,0:T(8,128)(2,1)S(1)}, bf16[4,384,256]{2,1,0:T(8,128)(2,1)S(1)}, u32[]{:S(2)}, u32[]{:S(2)}) %collective-permute-start.23) | collective-permute-done | bytes 786464 | tf_op jit(solution)/shard_map/ppermute | solution.py:1384
  238.7 10.1 times.3.gating.refs_13_
  249.5 15.8 %attend.1 = (f32[2,4,256,128]{3,2,1,0:T(8,128)}, bf16[2,4,256,128]{3,2,1,0:T(8,128)(2,1)}, f32[4,512,8]{2,1,0:T(8,128)}) custom-call(s32[3]{0:T(128)} %pad_add_fusion.1.where, bf16[2,4,256,128]{3,2,1,0:T(8,128)(2,1)} %get-tuple-element.173.query, bf16[4,2,512,256]{3,2,1,0:T(8,128)(2,1)} %all-gather.9.cloned.1.call-done.kv_own, ...), custom_call_target="tpu_custom_call" | custom-call | bytes 11000000 | tf_op jit(solution)/shard_map/attend/pallas_call | solution.py:480
  274.8 19.8 %ssm_forward.1 = (f32[8,256,384]{2,1,0:T(8,128)}, bf16[8,256,384]{2,1,0:T(8,128)(2,1)}, f32[8,8,256]{2,1,0:T(8,128)}) custom-call(s32[3]{0:T(128)} %pad_add_fusion.1.where, bf16[8,256,384]{2,1,0:T(8,128)(2,1)} %get-tuple-element.164.xs, bf16[8,4,256,128]{3,2,1,0:T(8,128)(2,1)} %copy-done, bf16[8,4,256,128]{3,2,1,0:T(8,128)(2,1)} %copy-done, ...), custom_call_target="tpu_custom_call" | custom-call | bytes 17600000 | tf_op jit(solution)/shard_map/ssm_forward/pallas_call | solution.py:390
  295.7 29.0 %all-gather.13.cloned.1.call-done = bf16[4,128,2048]{2,1,0:T(8,128)(2,1)} async-done(((bf16[1,128,2048]{2,1,0:T(8,128)(2,1)}), bf16[4,128,2048]{2,1,0:T(8,128)(2,1)}) %all-gather.13.cloned.1.call-update) | async-done | bytes 2097168 | tf_op jit(solution)/shard_map/all_gather | solution.py:1231
  362.1 13.1 %collective-permute-done.36.to_x = bf16[128,2048]{1,0:T(8,128)(2,1)S(1)} collective-permute-done((bf16[128,2048]{1,0:T(8,128)(2,1)}, bf16[128,2048]{1,0:T(8,128)(2,1)S(1)}, u32[]{:S(2)}, u32[]{:S(2)}) %collective-permute-start.36) | collective-permute-done | bytes 524320 | tf_op jit(solution)/shard_map/ppermute | solution.py:62
  382.8 22.7 %collective-permute-done.38.refs_2_ = bf16[256,2048]{1,0:T(8,128)(2,1)S(1)} collective-permute-done((bf16[256,2048]{1,0:T(8,128)(2,1)}, bf16[256,2048]{1,0:T(8,128)(2,1)S(1)}, u32[]{:S(2)}, u32[]{:S(2)}) %collective-permute-start.38) | collective-permute-done | bytes 1048608 | tf_op jit(solution)/shard_map/ppermute | solution.py:62
  414.5 20.9 %collective-permute-done.40.refs_1_.refs_2_ = bf16[256,2048]{1,0:T(8,128)(2,1)S(1)} collective-permute-done((bf16[256,2048]{1,0:T(8,128)(2,1)}, bf16[256,2048]{1,0:T(8,128)(2,1)S(1)}, u32[]{:S(2)}, u32[]{:S(2)}) %collective-permute-start.40) | collective-permute-done | bytes 1048608 | tf_op jit(solution)/shard_map/ppermute | solution.py:62
  453.6 22.5 %feed.1 = (bf16[2048,512]{1,0:T(8,128)(2,1)}, bf16[2048,1024]{1,0:T(8,128)(2,1)}) custom-call(bf16[256,2048]{1,0:T(8,128)(2,1)} %get-tuple-element.197.refs_0_.refs_1_, bf16[256,2048]{1,0:T(8,128)(2,1)} %copy-done.16, bf16[256,2048]{1,0:T(8,128)(2,1)} %copy-done.17, bf16[128,2048]{1,0:T(8,128)(2,1)} %collective-permute-done.42.refs_3_.refs_4_, ...), custom_call_target="tpu_custom_call" | custom-call | bytes 25300000 | tf_op jit(solution)/shard_map/feed/pallas_call | solution.py:1155
  505.1 9.9 weight_grad.6
  527.4 15.8 %weight_grad.7 = bf16[4,1024,512]{2,1,0:T(8,128)(2,1)} custom-call(bf16[1024,2048]{1,0:T(8,128)(2,1)} %bitcast.249, bf16[256,2048]{1,0:T(8,128)(2,1)} %get-tuple-element.197.refs_0_.refs_1_, bf16[256,2048]{1,0:T(8,128)(2,1)} %copy-done.16, bf16[256,2048]{1,0:T(8,128)(2,1)} %copy-done.17, bf16[128,2048]{1,0:T(8,128)(2,1)} %collective-permute-done.42.refs_3_.refs_4_, ...), custom_call_target="tpu_custom_call" | custom-call | bytes 15664000 | tf_op jit(solution)/shard_map/weight_grad/pallas_call | solution.py:904
  545.3 22.5 %collective-permute-done.55.refs_2_ = bf16[256,2048]{1,0:T(8,128)(2,1)S(1)} collective-permute-done((bf16[256,2048]{1,0:T(8,128)(2,1)}, bf16[256,2048]{1,0:T(8,128)(2,1)S(1)}, u32[]{:S(2)}, u32[]{:S(2)}) %collective-permute-start.55) | collective-permute-done | bytes 1048608 | tf_op jit(solution)/shard_map/ppermute | solution.py:62
  583.4 15.6 %collective-permute-done.61.refs_1_.refs_2_ = bf16[256,2048]{1,0:T(8,128)(2,1)S(1)} collective-permute-done((bf16[256,2048]{1,0:T(8,128)(2,1)}, bf16[256,2048]{1,0:T(8,128)(2,1)S(1)}, u32[]{:S(2)}, u32[]{:S(2)}) %collective-permute-start.61) | collective-permute-done | bytes 1048608 | tf_op jit(solution)/shard_map/ppermute | solution.py:62
  625.5 16.7 %mixer_back.1 = (f32[8,256,384]{2,1,0:T(8,128)}, bf16[8,256,128]{2,1,0:T(8,128)(2,1)}, f32[8,8,256]{2,1,0:T(8,128)}) custom-call(bf16[256,2048]{1,0:T(8,128)(2,1)} %get-tuple-element.218.refs_0_.refs_1_, bf16[256,2048]{1,0:T(8,128)(2,1)} %copy-done.14, bf16[256,2048]{1,0:T(8,128)(2,1)} %copy-done.15, ...), custom_call_target="tpu_custom_call" | custom-call | bytes 14300000 | tf_op jit(solution)/shard_map/mixer_back/pallas_call | solution.py:868
  653.1 14.4 %gate_back.1 = (bf16[8,256,384]{2,1,0:T(8,128)(2,1)}, bf16[8,256,384]{2,1,0:T(8,128)(2,1)}, bf16[8,256,384]{2,1,0:T(8,128)(2,1)}, f32[4,384,256]{2,1,0:T(8,128)}, f32[4,384,256]{2,1,0:T(8,128)}) custom-call(s32[3]{0:T(128)} %pad_add_fusion.1.where, f32[8,256,384]{2,1,0:T(8,128)} %get-tuple-element.227.es, f32[8,256,8]{2,1,0:T(8,128)} %pad.41.scale, ...), custom_call_target="tpu_custom_call" | custom-call | bytes 12100000 | tf_op jit(solution)/shard_map/gate_back/pallas_call | solution.py:605
  673.5 9.8 weight_grad.8
  688.3 11.2 %collective-permute-done.76.to_x = bf16[128,2048]{1,0:T(8,128)(2,1)} collective-permute-done((bf16[128,2048]{1,0:T(8,128)(2,1)S(1)}, bf16[128,2048]{1,0:T(8,128)(2,1)}, u32[]{:S(2)}, u32[]{:S(2)}) %collective-permute-start.76) | collective-permute-done | bytes 524320 | tf_op jit(solution)/shard_map/ppermute | solution.py:62
  719.8 11.2 %collective-permute-done.79 = bf16[256,2048]{1,0:T(8,128)(2,1)} collective-permute-done((bf16[256,2048]{1,0:T(8,128)(2,1)}, bf16[256,2048]{1,0:T(8,128)(2,1)}, u32[]{:S(2)}, u32[]{:S(2)}) %collective-permute-start.79) | collective-permute-done | bytes 1048608 | tf_op jit(solution)/shard_map/ppermute | solution.py:62
  742.6 18.4 %attend_back.1 = (f32[2,4,256,128]{3,2,1,0:T(8,128)}, bf16[4,4,512,256]{3,2,1,0:T(8,128)(2,1)}) custom-call(s32[3]{0:T(128)} %pad_add_fusion.1.where, bf16[2,4,256,128]{3,2,1,0:T(8,128)(2,1)} %get-tuple-element.173.query, bf16[4,2,512,256]{3,2,1,0:T(8,128)(2,1)} %all-gather.9.cloned.1.call-done.kv_own, ...), custom_call_target="tpu_custom_call" | custom-call | bytes 15400000 | tf_op jit(solution)/shard_map/attend_back/pallas_call | solution.py:545
  779.9 16.7 %collective-permute-done.81 = bf16[4,384,256]{2,1,0:T(8,128)(2,1)} collective-permute-done((bf16[4,384,256]{2,1,0:T(8,128)(2,1)}, bf16[4,384,256]{2,1,0:T(8,128)(2,1)}, u32[]{:S(2)}, u32[]{:S(2)}) %collective-permute-start.81) | collective-permute-done | bytes 786464 | tf_op jit(solution)/shard_map/ppermute | solution.py:1472
  800.3 39.4 %ssm_back.1 = (f32[8,256,384]{2,1,0:T(8,128)}, bf16[4,256,128]{2,1,0:T(8,128)(2,1)}, bf16[4,256,128]{2,1,0:T(8,128)(2,1)}, bf16[4,256,128]{2,1,0:T(8,128)(2,1)},...) custom-call(s32[3]{0:T(128)} %pad_add_fusion.1.where, ...), custom_call_target="tpu_custom_call" | custom-call | bytes 33000000 | tf_op jit(solution)/shard_map/ssm_back/pallas_call | solution.py:719
  889.3 11.4 %conv_backward.1 = (bf16[8,256,512]{2,1,0:T(8,128)(2,1)}, f32[8,8,512]{2,1,0:T(8,128)}) custom-call(f32[8,256,384]{2,1,0:T(8,128)} %get-tuple-element.258.grad_xs, f32[4,256,128]{2,1,0:T(8,128)} %copy-done.23, f32[8,256,8]{2,1,0:T(8,128)} %get-tuple-element.267.step, f32[8,256,512]{2,1,0:T(8,128)} %get-tuple-element.268.slope, ...), custom_call_target="tpu_custom_call" | custom-call | bytes 6600000 | tf_op jit(solution)/shard_map/conv_backward/pallas_call | solution.py:787
  904.8 9.9 weight_grad.11
  940.4 10.4 group_terms.14
  963.0 11.3 %group_terms.15 = (f32[256,2048]{1,0:T(8,128)}, f32[256,2048]{1,0:T(8,128)}, f32[256,2048]{1,0:T(8,128)}, bf16[128,2048]{1,0:T(8,128)(2,1)}, bf16[128,2048]{1,0:T(8,128)(2,1)}) custom-call(bf16[2048,384]{1,0:T(8,128)(2,1)} %bitcast.254, bf16[2048,384]{1,0:T(8,128)(2,1)} %bitcast.242, bf16[2048,512]{1,0:T(8,128)(2,1)} %bitcast.245, ...), custom_call_target="tpu_custom_call" | custom-call | bytes 12222222 | tf_op jit(solution)/shard_map/group_terms/pallas_call | solution.py:962
  1007.0 18.0 %all-to-all-done.3 = bf16[8,64,768]{2,1,0:T(8,128)(2,1)S(1)} async-done(((bf16[8,64,768]{2,1,0:T(8,128)(2,1)}), bf16[8,64,768]{2,1,0:T(8,128)(2,1)S(1)}, u32[]{:S(2)}, u32[]{:S(2)}) %all-to-all-start.3) | async-done | bytes 786464 | tf_op jit(solution)/shard_map/all_to_all | solution.py:1224
  (678 shorter events, 510.3 us)
Async XLA Ops:
  7.2 98.8 %all-gather.7.cloned.1.call-start = ((), (), s32[]{:S(2)}) async-start(), calls=%async_computation.12 | async-start | bytes 4587520 | tf_op jit(solution)/shard_map/all_gather | solution.py:1231
  67.7 145.9 %all-gather.9.cloned.1.call-start = ((), (), s32[]{:S(2)}) async-start(), calls=%async_computation.13 | async-start | bytes 2621440 | tf_op jit(solution)/shard_map/all_gather | solution.py:1231
  68.3 29.7 %collective-permute-start.7 = (bf16[256,2048]{1,0:T(8,128)(2,1)S(1)}, bf16[256,2048]{1,0:T(8,128)(2,1)}, u32[]{:S(2)}, u32[]{:S(2)}) collective-permute-start(bf16[256,2048]{1,0:T(8,128)(2,1)S(1)} %collective-permute-done.refs_1_.refs_2_), channel_id=1, source_target_pairs={{0,1},{1,0},{2,3},{3,2},{4,5},{5,4},{6,7},{7,6},{8,9},{9,8},{10,11... | collective-permute-start | bytes 3145736 | tf_op jit(solution)/shard_map/ppermute | solution.py:66
  69.3 28.2 %collective-permute-start.4 = (bf16[128,2048]{1,0:T(8,128)(2,1)}, bf16[128,2048]{1,0:T(8,128)(2,1)S(1)}, u32[]{:S(2)}, u32[]{:S(2)}) collective-permute-start(bf16[128,2048]{1,0:T(8,128)(2,1)} %slice.298), channel_id=1, source_target_pairs={{0,16},{8,24},{16,0},{24,8},{1,17},{9,25},{17,1},{25,9},{2,18},{10... | collective-permute-start | bytes 1572872 | tf_op jit(solution)/shard_map/ppermute | solution.py:62
  74.6 31.4 %collective-permute-start.8 = (bf16[256,2048]{1,0:T(8,128)(2,1)}, bf16[256,2048]{1,0:T(8,128)(2,1)}, u32[]{:S(2)}, u32[]{:S(2)}) collective-permute-start(bf16[256,2048]{1,0:T(8,128)(2,1)} %collective-permute-done.1.refs_2_.refs_3_), channel_id=1, source_target_pairs={{0,1},{1,0},{2,3},{3,2},{4,5},{5,4},{6,7},{7,6},{8,9},{9,8},{10,11... | collective-permute-start | bytes 3145736 | tf_op jit(solution)/shard_map/ppermute | solution.py:66
  87.9 36.2 %collective-permute-start.2 = (bf16[256,2048]{1,0:T(8,128)(2,1)}, bf16[256,2048]{1,0:T(8,128)(2,1)}, u32[]{:S(2)}, u32[]{:S(2)}) collective-permute-start(bf16[256,2048]{1,0:T(8,128)(2,1)} %bitcast.256), channel_id=1, source_target_pairs={{0,8},{8,0},{16,24},{24,16},{1,9},{9,1},{17,25},{25,17},{2,10},{10... | collective-permute-start | bytes 3145736 | tf_op jit(solution)/shard_map/ppermute | solution.py:62
  97.5 26.5 %collective-permute-start.3 = (bf16[256,2048]{1,0:T(8,128)(2,1)}, bf16[256,2048]{1,0:T(8,128)(2,1)}, u32[]{:S(2)}, u32[]{:S(2)}) collective-permute-start(bf16[256,2048]{1,0:T(8,128)(2,1)} %bitcast.257), channel_id=1, source_target_pairs={{0,16},{8,24},{16,0},{24,8},{1,17},{9,25},{17,1},{25,9},{2,18},{10... | collective-permute-start | bytes 3145736 | tf_op jit(solution)/shard_map/ppermute | solution.py:62
  133.4 105.3 %all-gather.11.cloned.1.call-start = ((), (), s32[]{:S(2)}) async-start(), calls=%async_computation.14 | async-start | bytes 1966080 | tf_op jit(solution)/shard_map/all_gather | solution.py:1231
  134.2 43.6 %collective-permute-start.14 = (bf16[256,2048]{1,0:T(8,128)(2,1)S(1)}, bf16[256,2048]{1,0:T(8,128)(2,1)S(1)}, u32[]{:S(2)}, u32[]{:S(2)}) collective-permute-start(bf16[256,2048]{1,0:T(8,128)(2,1)S(1)} %bitcast.261), channel_id=1, source_target_pairs={{0,1},{1,0},{2,3},{3,2},{4,5},{5,4},{6,7},{7,6},{8,9},{9,8},{10,11... | collective-permute-start | bytes 3145736 | tf_op jit(solution)/shard_map/ppermute | solution.py:66
  138.8 39.0 %collective-permute-start.15 = (bf16[256,2048]{1,0:T(8,128)(2,1)}, bf16[256,2048]{1,0:T(8,128)(2,1)S(1)}, u32[]{:S(2)}, u32[]{:S(2)}) collective-permute-start(bf16[256,2048]{1,0:T(8,128)(2,1)} %collective-permute-done.2.refs_11_.refs_2_), channel_id=1, source_target_pairs={{0,1},{1,0},{2,3},{3,2},{4,5},{5,4},{6,7},{7,6},{8,9},{9,8},{10,11... | collective-permute-start | bytes 3145736 | tf_op jit(solution)/shard_map/ppermute | solution.py:66
  155.7 169.0 %all-gather.13.cloned.1.call-start = ((), (), s32[]{:S(2)}) async-start(), calls=%async_computation.15 | async-start | bytes 2621440 | tf_op jit(solution)/shard_map/all_gather | solution.py:1231
  213.6 35.1 %collective-permute-start.25 = (bf16[4,2,512,256]{3,2,1,0:T(8,128)(2,1)}, bf16[4,2,512,256]{3,2,1,0:T(8,128)(2,1)}, u32[]{:S(2)}, u32[]{:S(2)}) collective-permute-start(bf16[4,2,512,256]{3,2,1,0:T(8,128)(2,1)} %all-gather.9.cloned.1.call-done.kv_own), channel_id=1, source_target_pairs={{0,1},{1,0},{2,3},{3,2},{4,5},{5,4},{6,7},{7,6},{8,9},{9,8},{10,11... | collective-permute-start | bytes 6291464 | tf_op jit(solution)/shard_map/ppermute | solution.py:66
  237.9 27.4 %collective-permute-start.24 = (bf16[4,384,256]{2,1,0:T(8,128)(2,1)}, bf16[4,384,256]{2,1,0:T(8,128)(2,1)S(1)}, u32[]{:S(2)}, u32[]{:S(2)}) collective-permute-start(bf16[4,384,256]{2,1,0:T(8,128)(2,1)} %fusion.1), channel_id=1, source_target_pairs={{2,4},{3,5},{10,12},{11,13},{18,20},{19,21},{26,28},{27,29}} | collective-permute-start | bytes 2359304 | tf_op jit(solution)/shard_map/ppermute | solution.py:1384
  269.7 181.6 %all-gather.17.cloned.1.call-start = ((), (), s32[]{:S(2)}) async-start(), calls=%async_computation.17 | async-start | bytes 2621440 | tf_op jit(solution)/shard_map/all_gather | solution.py:1231
  272.1 179.6 %all-gather.15.cloned.1.call-start = ((), (), s32[]{:S(2)}) async-start(), calls=%async_computation.16 | async-start | bytes 5242880 | tf_op jit(solution)/shard_map/all_gather | solution.py:1231
  295.5 30.9 %collective-permute-start.28 = (f32[2,4,256]{2,1,0:T(4,128)S(1)}, f32[2,4,256]{2,1,0:T(4,128)S(1)}, u32[]{:S(2)}, u32[]{:S(2)}) collective-permute-start(f32[2,4,256]{2,1,0:T(4,128)S(1)} %reshape_squeeze.6), channel_id=1, source_target_pairs={{0,1},{1,0},{2,3},{3,2},{4,5},{5,4},{6,7},{7,6},{8,9},{9,8},{10,11... | collective-permute-start | bytes 24584 | tf_op jit(solution)/shard_map/ppermute | solution.py:66
  295.6 416.7 %reduce-scatter.8.cloned.1.call-start = ((), (), s32[]{:S(2)}) async-start(), calls=%async_computation.18 | async-start | bytes 5242880 | tf_op jit(solution)/shard_map/reduce_scatter | solution.py:1227
  414.5 37.3 %collective-permute-start.44 = (bf16[256,2048]{1,0:T(8,128)(2,1)}, bf16[256,2048]{1,0:T(8,128)(2,1)S(1)}, u32[]{:S(2)}, u32[]{:S(2)}) collective-permute-start(bf16[256,2048]{1,0:T(8,128)(2,1)} %get-tuple-element.197.refs_0_.refs_1_), channel_id=1, source_target_pairs={{0,1},{1,0},{2,3},{3,2},{4,5},{5,4},{6,7},{7,6},{8,9},{9,8},{10,11... | collective-permute-start | bytes 3145736 | tf_op jit(solution)/shard_map/ppermute | solution.py:66
  543.3 171.3 %reduce-scatter.10.cloned.1.call-start = ((), (), s32[]{:S(2)}) async-start(), calls=%async_computation.19 | async-start | bytes 2621440 | tf_op jit(solution)/shard_map/reduce_scatter | solution.py:1234
  599.9 25.6 %collective-permute-start.65 = (bf16[256,2048]{1,0:T(8,128)(2,1)S(1)}, bf16[256,2048]{1,0:T(8,128)(2,1)}, u32[]{:S(2)}, u32[]{:S(2)}) collective-permute-start(bf16[256,2048]{1,0:T(8,128)(2,1)S(1)} %copy-done.21), channel_id=1, source_target_pairs={{0,1},{1,0},{2,3},{3,2},{4,5},{5,4},{6,7},{7,6},{8,9},{9,8},{10,11... | collective-permute-start | bytes 3145736 | tf_op jit(solution)/shard_map/ppermute | solution.py:66
  704.5 26.4 %collective-permute-start.79 = (bf16[256,2048]{1,0:T(8,128)(2,1)}, bf16[256,2048]{1,0:T(8,128)(2,1)}, u32[]{:S(2)}, u32[]{:S(2)}) collective-permute-start(bf16[256,2048]{1,0:T(8,128)(2,1)} %get-tuple-element.237), channel_id=1, source_target_pairs={{0,8},{8,0},{16,24},{24,16},{1,9},{9,1},{17,25},{25,17},{2,10},{10... | collective-permute-start | bytes 3145736 | tf_op jit(solution)/shard_map/ppermute | solution.py:62
  705.4 27.8 %collective-permute-start.80 = (bf16[256,2048]{1,0:T(8,128)(2,1)}, bf16[256,2048]{1,0:T(8,128)(2,1)}, u32[]{:S(2)}, u32[]{:S(2)}) collective-permute-start(bf16[256,2048]{1,0:T(8,128)(2,1)} %get-tuple-element.241), channel_id=1, source_target_pairs={{0,16},{8,24},{16,0},{24,8},{1,17},{9,25},{17,1},{25,9},{2,18},{10... | collective-permute-start | bytes 3145736 | tf_op jit(solution)/shard_map/ppermute | solution.py:62
  714.6 25.6 %all-to-all-start.2 = ((bf16[8,64,1024]{2,1,0:T(8,128)(2,1)}), bf16[8,64,1024]{2,1,0:T(8,128)(2,1)S(1)}, u32[]{:S(2)}, u32[]{:S(2)}) async-start(bf16[8,64,1024]{2,1,0:T(8,128)(2,1)} %bitcast.276), calls=%async_computation.4 | async-start | bytes 2097152 | tf_op jit(solution)/shard_map/all_to_all | solution.py:1224
  718.2 78.5 %reduce-scatter.12.cloned.1.call-start = ((), (), s32[]{:S(2)}) async-start(), calls=%async_computation.20 | async-start | bytes 2621440 | tf_op jit(solution)/shard_map/reduce_scatter | solution.py:1234
  740.2 101.8 %reduce-scatter.14.cloned.1.call-start = ((), (), s32[]{:S(2)}) async-start(), calls=%async_computation.21 | async-start | bytes 2621440 | tf_op jit(solution)/shard_map/reduce_scatter | solution.py:1234
  764.2 32.5 %collective-permute-start.81 = (bf16[4,384,256]{2,1,0:T(8,128)(2,1)}, bf16[4,384,256]{2,1,0:T(8,128)(2,1)}, u32[]{:S(2)}, u32[]{:S(2)}) collective-permute-start(bf16[4,384,256]{2,1,0:T(8,128)(2,1)} %add_convert_fusion.2), channel_id=1, source_target_pairs={{2,0},{3,1},{10,8},{11,9},{18,16},{19,17},{26,24},{27,25}} | collective-permute-start | bytes 2359304 | tf_op jit(solution)/shard_map/ppermute | solution.py:1472
  796.7 162.1 %reduce-scatter.18.cloned.1.call-start = ((), (), s32[]{:S(2)}) async-start(), calls=%async_computation.23 | async-start | bytes 1966080 | tf_op jit(solution)/shard_map/reduce_scatter | solution.py:1227
  797.5 197.6 %reduce-scatter.16.cloned.1.call-start = ((), (), s32[]{:S(2)}) async-start(), calls=%async_computation.22 | async-start | bytes 1966080 | tf_op jit(solution)/shard_map/reduce_scatter | solution.py:1227
  862.7 163.3 %reduce-scatter.20.cloned.1.call-start = ((), (), s32[]{:S(2)}) async-start(), calls=%async_computation.24 | async-start | bytes 2621440 | tf_op jit(solution)/shard_map/reduce_scatter | solution.py:1227
  992.7 39.0 %collective-permute-start.101 = (bf16[256,2048]{1,0:T(8,128)(2,1)}, bf16[256,2048]{1,0:T(8,128)(2,1)}, u32[]{:S(2)}, u32[]{:S(2)}) collective-permute-start(bf16[256,2048]{1,0:T(8,128)(2,1)} %get-tuple-element.280), channel_id=1, source_target_pairs={{0,8},{8,0},{16,24},{24,16},{1,9},{9,1},{17,25},{25,17},{2,10},{10... | collective-permute-start | bytes 3145736 | tf_op jit(solution)/shard_map/ppermute | solution.py:62
  994.2 37.5 %collective-permute-start.102 = (bf16[256,2048]{1,0:T(8,128)(2,1)}, bf16[256,2048]{1,0:T(8,128)(2,1)}, u32[]{:S(2)}, u32[]{:S(2)}) collective-permute-start(bf16[256,2048]{1,0:T(8,128)(2,1)} %get-tuple-element.290), channel_id=1, source_target_pairs={{0,16},{8,24},{16,0},{24,8},{1,17},{9,25},{17,1},{25,9},{2,18},{10... | collective-permute-start | bytes 3145736 | tf_op jit(solution)/shard_map/ppermute | solution.py:62
  997.3 27.8 %all-to-all-start.3 = ((bf16[8,64,768]{2,1,0:T(8,128)(2,1)}), bf16[8,64,768]{2,1,0:T(8,128)(2,1)S(1)}, u32[]{:S(2)}, u32[]{:S(2)}) async-start(bf16[8,64,768]{2,1,0:T(8,128)(2,1)} %pad_maximum_fusion.4), calls=%async_computation.9 | async-start | bytes 1572864 | tf_op jit(solution)/shard_map/all_to_all | solution.py:1224
  (174 other events, 1671.0 us)
Sparse Core Ops, SparseCore 0:
  34.5 71.4 all-gather.6
  133.5 45.1 all-gather.8
  180.3 36.1 all-gather.10
  269.8 54.7 all-gather.12
  326.1 44.6 all-gather.16
  372.2 79.4 all-gather.14
  543.4 74.1 reduce-scatter.7
  620.0 44.3 reduce-scatter.9
  740.4 45.0 reduce-scatter.11
  796.8 41.9 reduce-scatter.13
  841.2 34.5 reduce-scatter.17
  877.9 34.2 reduce-scatter.15
  914.8 42.4 reduce-scatter.19

commit v3 on v2

--- a/solution.py
+++ b/solution.py
@@ -81,13 +81,16 @@
     return lax.optimization_barrier((values,) + earlier)[0]
 
 
-def gather_group(own, meanwhile=None):
+def gather_group(own, meanwhile=None, then=None):
     half = own.shape[0] // 2
     by_x = hop(own, 1)
     by_y = hop(own, 2)
     if meanwhile is not None:
         by_x, by_y, meanwhile = lax.optimization_barrier((by_x, by_y, meanwhile))
-    mine = [own, by_x, by_y, hop(by_x[:half], 2), hop(by_y[half:], 1)]
+    far = hop(by_x[:half], 2), hop(by_y[half:], 1)
+    if then is not None:
+        *far, meanwhile = lax.optimization_barrier((*far, then(meanwhile)))
+    mine = [own, by_x, by_y, *far]
     pieces = mine + [twin(part) for part in mine]
     return pieces if meanwhile is None else (pieces, meanwhile)
 
@@ -571,7 +574,7 @@
 
 def gate_back_kernel(
     where, es, scale, gating, ssm_out, c0, c1, c2, c3, meta, marks, p0,
-    gy_out, gating_out, unit_out, later_out, both_out,
+    gy_out, gating_out, later_out, both_out,
 ):
     gate = gating[0]
     sig = sigmoid_of(gate)
@@ -579,7 +582,6 @@
     out = ssm_out[0]
     norm = scale[0, :, 0:1]
     unit = out * act * norm
-    unit_out[0] = unit.astype(bf16)
     grad = norm * (es[0] - unit * scale[0, :, 1:2])
     gy = (grad * act).astype(bf16)
     gy_out[0] = gy
@@ -614,9 +616,9 @@
                 time_spec((CHUNK, 8), True),
                 slot_spec((OWN_SSM, 1)),
             ],
-            out_specs=[wide, wide, wide, slot_spec((OWN_SSM, STATE)), slot_spec((OWN_SSM, STATE))],
+            out_specs=[wide, wide, slot_spec((OWN_SSM, STATE)), slot_spec((OWN_SSM, STATE))],
         ),
-        out_shape=[token, token, token, state, state],
+        out_shape=[token, token, state, state],
         compiler_params=pltpu.CompilerParams(vmem_limit_bytes=VMEM),
         cost_estimate=lasting(11),
         name="gate_back",
@@ -823,18 +825,18 @@
     return copies, starts
 
 
-def by_chunk(copies, starts):
-    for i in range(8):
+def by_pair(copies, starts):
+    for i in range(0, 8, 2):
         for j, copy in enumerate(copies):
-            if i * CHUNK < starts[j + 1] <= (i + 1) * CHUNK:
+            if i * CHUNK < starts[j + 1] <= (i + 2) * CHUNK:
                 copy.wait()
-        yield i, slice(i * CHUNK, (i + 1) * CHUNK)
+        yield i, slice(i * CHUNK, (i + 2) * CHUNK)
 
 
 def times_kernel(count, *refs):
     pieces, (weight, out, held, arrived) = refs[:count], refs[count:]
-    for i, at in by_chunk(*fetch(pieces, held, arrived)):
-        out[i] = dot(held[at, :], weight[...])
+    for i, at in by_pair(*fetch(pieces, held, arrived)):
+        out[i : i + 2] = dot(held[at, :], weight[...]).reshape(2, CHUNK, -1)
 
 
 def times(pieces, weight):
@@ -855,12 +857,14 @@
 def mixer_back_kernel(count, *refs):
     pieces = refs[:count]
     w_out, w_ctx, ssm_out, gating, es_out, context_out, sum_out, held, arrived = refs[count:]
-    for i, at in by_chunk(*fetch(pieces, held, arrived)):
-        es = dot_cols(held[at, :], w_out[...])
-        es_out[i] = es
-        context_out[i] = dot_cols(held[at, :], w_ctx[...]).astype(bf16)
-        gate = gating[i]
-        sum_out[i] = row_sums(es * ssm_out[i] * gate * sigmoid_of(gate))
+    for i, at in by_pair(*fetch(pieces, held, arrived)):
+        es = dot_cols(held[at, :], w_out[...]).reshape(2, CHUNK, OWN_SSM)
+        es_out[i : i + 2] = es
+        context = dot_cols(held[at, :], w_ctx[...]).astype(bf16)
+        context_out[i : i + 2] = context.reshape(2, CHUNK, ATT_HEAD)
+        for j in range(2):
+            gate = gating[i + j]
+            sum_out[i + j] = row_sums(es[j] * ssm_out[i + j] * gate * sigmoid_of(gate))
 
 
 def mixer_back(pieces, w_out, w_ctx, ssm_out, gating):
@@ -914,15 +918,15 @@
     )(left, *pieces)
 
 
-def terms_kernel(count, turned, adds, scaled_by, *refs):
+def terms_kernel(count, turned, adds, scaled_by, far, *refs):
     lefts, weights = refs[:count], refs[count : 2 * count]
     rest = refs[2 * count :]
     norm = rest[0] if scaled_by else None
     got = rest[int(scaled_by) : int(scaled_by) + adds]
     outs = rest[int(scaled_by) + adds :]
-    rows = outs[0].shape[0]
-    half = rows // 2
-    for k in range(ROWS):
+    half = outs[0].shape[0]
+    rows = 2 * half if far and adds else half
+    for k in range(1 if far else ROWS - 1):
         at = slice(k * rows, (k + 1) * rows)
         total = None
         for i in range(count):
@@ -932,20 +936,22 @@
             total = product if total is None else total + product
         if adds:
             total = total + got[k][...].astype(f32)
-        if adds and k == 3:
-            outs[3][...] = total[:half].astype(bf16)
-            outs[4][...] = total[half:].astype(bf16)
+        if adds and far:
+            outs[0][...] = total[:half].astype(bf16)
+            outs[1][...] = total[half:].astype(bf16)
         else:
             outs[k][...] = total.astype(outs[k].dtype)
 
 
-def group_terms(lefts, weights, turned, core, got=(), norm=None):
+def group_terms(lefts, weights, turned, core, far, got=(), norm=None):
     width = weights[0].shape[0 if turned else 1]
     rows = lefts[0].shape[0] // 8
     block = min(width, 512)
-    in_specs = [
-        pl.BlockSpec((ROWS * rows, left.shape[1]), lambda i, core=core: (core, 0)) for left in lefts
-    ]
+    if far:
+        row_spec = lambda cols: pl.BlockSpec((rows, cols), lambda i: (core * ROWS + ROWS - 1, 0))
+    else:
+        row_spec = lambda cols: pl.BlockSpec((ROWS * rows, cols), lambda i: (core, 0))
+    in_specs = [row_spec(left.shape[1]) for left in lefts]
     for weight in weights:
         if turned:
             in_specs.append(pl.BlockSpec((block, weight.shape[1]), lambda i: (i, 0)))
@@ -953,14 +959,17 @@
             in_specs.append(pl.BlockSpec((weight.shape[0], block), lambda i: (0, i)))
     operands = list(lefts) + list(weights)
     if norm is not None:
-        in_specs.append(pl.BlockSpec((ROWS * rows, 8), lambda i, core=core: (core, 0)))
+        in_specs.append(row_spec(8))
         operands.append(norm)
     piece = pl.BlockSpec((rows, block), lambda i: (0, i))
     in_specs += [piece] * len(got)
-    kinds = [(rows, f32)] * 3 + [(rows // 2, bf16)] * 2 if got else [(rows, bf16)] * 4
+    if got:
+        kinds = [(rows // 2, bf16)] * 2 if far else [(rows, f32)] * 3
+    else:
+        kinds = [(rows, bf16)] * (1 if far else 3)
     depth = sum(left.shape[1] for left in lefts)
     return pl.pallas_call(
-        lambda *refs: terms_kernel(len(lefts), turned, len(got), norm is not None, *refs),
+        lambda *refs: terms_kernel(len(lefts), turned, len(got), norm is not None, far, *refs),
         grid=(width // block,),
         in_specs=in_specs,
         out_specs=[pl.BlockSpec((n, block), lambda i: (0, i)) for n, _ in kinds],
@@ -971,10 +980,18 @@
     )(*operands, *got)
 
 
-def scatter_product(lefts, weights, turned=False, norm=None, give=False, meanwhile=None):
-    other = group_terms(lefts, weights, turned, 1, norm=norm)
-    got = [twin(part) for part in other]
-    own, for_x, for_y, far_a, far_b = group_terms(lefts, weights, turned, 0, got=got, norm=norm)
+def spread(for_x, for_y, to_x, to_y):
+    by_x, by_y = fold(for_x, for_y, to_x, to_y)
+    return by_x, hop(by_x, 1), hop(by_y, 2)
+
+
+def scatter_product(lefts, weights, turned=False, norm=None, give=False, meanwhile=None, beside=None):
+    far_got = [twin(part) for part in group_terms(lefts, weights, turned, 1, True, norm=norm)]
+    near_got = [twin(part) for part in group_terms(lefts, weights, turned, 1, False, norm=norm)]
+    if beside is not None:
+        near_got, beside = lax.optimization_barrier((near_got, beside))
+    far_a, far_b = group_terms(lefts, weights, turned, 0, True, got=far_got, norm=norm)
+    own, for_x, for_y = group_terms(lefts, weights, turned, 0, False, got=near_got, norm=norm)
     to_x, to_y = hop(far_a, 2), hop(far_b, 1)
     done = None
     if meanwhile is not None:
@@ -982,7 +999,7 @@
         to_x, to_y, done = lax.optimization_barrier((to_x, to_y, done))
     by_x, by_y = fold(for_x, for_y, to_x, to_y)
     sums = own, hop(by_x, 1), hop(by_y, 2)
-    return (sums, done, own, by_x) if give else sums
+    return (sums, done, beside, by_x) if give else sums
 
 
 def fold_kernel(for_x, for_y, to_x, to_y, by_x, by_y):
@@ -995,7 +1012,7 @@
 
 def fold(for_x, for_y, to_x, to_y):
     rows, width = for_x.shape
-    block = min(width, 512)
+    block = min(width, 1024)
     spec = lambda n: pl.BlockSpec((n, block), lambda i: (0, i))
     return pl.pallas_call(
         fold_kernel,
@@ -1047,11 +1064,11 @@
 
 def on_rows(kernel, part, operands, kinds, name):
     rows, width = operands[0].shape
-    step = rows // 4
+    step = rows // 2
     spec = pl.BlockSpec((step, width), lambda i: (i, 0))
     return pl.pallas_call(
         lambda *refs: kernel(part, *refs),
-        grid=(4,),
+        grid=(2,),
         in_specs=[spec] * len(operands),
         out_specs=[spec] * len(kinds),
         out_shape=[jax.ShapeDtypeStruct((rows, width), kind) for kind in kinds],
@@ -1138,7 +1155,7 @@
     copies_n, starts = fetch(n2, held_n, arrived_n)
     copies_g, _ = fetch(g, held_g, arrived_g)
     own = w_down.shape[0]
-    for (i, at), _ in zip(by_chunk(copies_n, starts), by_chunk(copies_g, starts)):
+    for (i, at), _ in zip(by_pair(copies_n, starts), by_pair(copies_g, starts)):
         both = dot(held_n[at, :], w_gu[...])
         gate, up = both[:, :own], both[:, own:]
         sig = sigmoid_of(gate)
@@ -1360,7 +1377,6 @@
     moved = jnp.pad(moved, ((0, 0), (8 - CONV + 1, 0), (0, 0)))
     halo = before_chunk(tails, moved).reshape(chunks, 8, cols_a).astype(f32)
     xs, bc_own, slope, meta, meta_rows = conv_forward(proj, halo, marks, conv_own, head)
-    bc_own = after(bc_own, *g_all)
     mine = [bc_own] + [hop(bc_own, m) for m in range(1, ROWS)]
     mine = jnp.stack(mine)
     bc = jnp.concatenate([mine, twin(mine)], axis=0)
@@ -1381,12 +1397,15 @@
                 where, query, kv_own, kv_other, seg_query, seg_keys
             )
             gating = times(n1, after(wc, message))
+        if s == zs - 2:
+            w_oc = along_z(after(w_oc, message))
         moved = lax.ppermute(message, "z", [(s, s + 1)])
+        if s == 0:
+            moved, *g_all = lax.optimization_barrier((moved, *g_all))
         if s == 1:
             moved, context_low, gating = lax.optimization_barrier((moved, context_low, gating))
         state = state + moved.astype(f32)
 
-    w_oc = along_z(after(w_oc, state))
     halves = w_oc.reshape(2, zs // 2, row_out + row_ctx, width)
     kept = lax.dynamic_index_in_dim(halves, c, 0, keepdims=False)
     sent = lax.dynamic_index_in_dim(halves, 1 - c, 0, keepdims=False)
@@ -1420,31 +1439,45 @@
     )
     grad_down = owner_z(grad_down_terms)
     grad_gu_terms = weight_grad(after(grad_gu, folded).T, n2, zs)
-    e2 = (after(e2[0], grad_gu_terms),) + e2[1:]
+    *e2, grad_gu_terms = lax.optimization_barrier((*e2, grad_gu_terms))
     grad_gu_w = to_owner(grad_gu_terms)
     grad_hidden, grad_mix_own = on_rows(
         norm_back_kernel, block, [hidden, *map(unlined, e2), cot], [f32, bf16], "norm_back"
     )
-    grad_mix = gather_group(grad_mix_own)
-    (late_own, late_x, late_y), _, _, late_folded = scatter_product(
-        [after(activation, grad_mix_own)], [w_down], give=True
-    )
+    unit_low = (gated_low.astype(f32) * scale_ssm).astype(bf16)
+    mixer_left = jnp.concatenate([flat(unit_low), flat(context_low)], axis=-1).T
+    late = after(activation, grad_mix_own)
+    late_other = [group_terms([late], [w_down], False, 1, far) for far in (True, False)]
+
+    def late_sums(meanwhile):
+        other, left = meanwhile
+        far_got, near_got = [[twin(part) for part in parts] for parts in other]
+        return (
+            group_terms([late], [w_down], False, 0, True, got=far_got),
+            group_terms([late], [w_down], False, 0, False, got=near_got),
+            left,
+        )
+
+    grad_mix, ((far_a, far_b), (late_own, for_x, for_y), mixer_left) = gather_group(
+        grad_mix_own, (late_other, mixer_left), late_sums
+    )
+    to_x, to_y = hop(far_a, 2), hop(far_b, 1)
     es, grad_context, es_sum = mixer_back(
-        grad_mix, after(w_out, late_own), w_ctx, ssm_out, gating
-    )
+        grad_mix, after(w_out, late_own, far_a, mixer_left), w_ctx, ssm_out, gating
+    )
+    grad_oc_w = weight_grad(after(mixer_left, es_sum), grad_mix)
     es_sum = es_sum[:, 0] * scale_ssm[..., 0]
     es_mean = sum_group(es_sum.reshape(2, ROWS, rows)) * (1.0 / ssm_width)
     scales = jnp.pad(
         jnp.stack([scale_ssm[..., 0], es_mean.reshape(chunks, rows)], axis=-1),
         ((0, 0), (0, 0), (0, 6)),
     )
-    gy, grad_gating, unit_low, later_grad, both_grad = gate_back(
+    scales, to_x, to_y, grad_oc_w = lax.optimization_barrier((scales, to_x, to_y, grad_oc_w))
+    gy, grad_gating, later_grad, both_grad = gate_back(
         where, es, scales, gating, ssm_out, bc, meta, marks, p0
     )
 
-    def out_grads(unit_low):
-        mixer_in = jnp.concatenate([flat(unit_low), flat(context_low)], axis=-1)
-        grad_oc_w = weight_grad(mixer_in.T, grad_mix)
+    def out_grads(grad_oc_w):
         grad_out_rows = grad_oc_w[:OWN_SSM].reshape(zs // 2, 2, row_out, width)
         grad_ctx_rows = grad_oc_w[OWN_SSM:].reshape(zs // 2, 2, row_ctx, width)
         grad_oc = jnp.concatenate([grad_out_rows, grad_ctx_rows], axis=2)
@@ -1466,26 +1499,24 @@
                 where, query, kv_own, kv_other, seg_query, seg_keys, grad_context, context, logsum
             )
             grad_wc_terms = weight_grad(after(grad_c_low, message).T, n1, zs)
-            kv_kept = lax.dynamic_slice_in_dim(grad_kv, 2 * c, 2, 1).astype(f32)
-            kv_got = twin(lax.dynamic_slice_in_dim(grad_kv, 2 - 2 * c, 2, 1)).astype(f32)
-            kv_terms = (kv_kept + kv_got).astype(bf16)
         moved = lax.ppermute(message, "z", [(s, s - 1)])
         if s == zs - 1:
-            oc_all = out_grads(after(unit_low, message))
-            moved, oc_all, late_folded = lax.optimization_barrier((moved, oc_all, late_folded))
+            late_folded, late_x, late_y = spread(for_x, for_y, to_x, to_y)
+            moved, late_folded = lax.optimization_barrier((moved, late_folded))
         if s == zs - 2:
             got_gu = to_ranks(after(grad_gu_w, message, grad_down))
-            moved, got_gu, late_x, late_y = lax.optimization_barrier(
-                (moved, got_gu, late_x, late_y)
-            )
-            grad_oc_own = owner_z(after(oc_all, got_gu))
+            oc_all = out_grads(after(grad_oc_w, message))
+            moved, got_gu, oc_all = lax.optimization_barrier((moved, got_gu, oc_all))
         if s == 1:
-            moved, grad_query, kv_terms, grad_wc_terms, grad_oc_own = lax.optimization_barrier(
-                (moved, grad_query, kv_terms, grad_wc_terms, grad_oc_own)
+            moved, grad_query, grad_kv, grad_wc_terms, late_x, late_y = lax.optimization_barrier(
+                (moved, grad_query, grad_kv, grad_wc_terms, late_x, late_y)
             )
         flowing = flowing + moved.astype(f32)
     grad_wc = to_owner(grad_wc_terms)
 
+    kv_kept = lax.dynamic_slice_in_dim(grad_kv, 2 * c, 2, 1).astype(f32)
+    kv_got = twin(lax.dynamic_slice_in_dim(grad_kv, 2 - 2 * c, 2, 1)).astype(f32)
+    kv_terms = (kv_kept + kv_got).astype(bf16)
     kv_grad = owner_z(kv_terms)
     kv_grad = kv_grad[0].astype(f32)
     grad_b_low = rope_back(
@@ -1542,34 +1573,22 @@
 
     grad_wa_terms = weight_grad(grad_a_low.T, n1, zs)
     grad_a_low = after(grad_a_low, grad_wa_terms)
-    e1, _, _, e1_folded = scatter_product(
-        [grad_c_low, grad_b_low, grad_a_low], [wc, wb, wa], turned=True, give=True
+    sums = jnp.concatenate([conv_sums, head_sums], axis=0)
+    e1, table, _, e1_folded = scatter_product(
+        [grad_c_low, grad_b_low, grad_a_low],
+        [wc, wb, wa],
+        turned=True,
+        give=True,
+        meanwhile=lambda own: all_sums(sums),
     )
     grad_wa = to_owner(grad_wa_terms)
     late_own = after(late_own, e1_folded)
     result = (hidden + late_own + late_x.astype(f32) + late_y.astype(f32)).astype(bf16)
-    grad_oc_own = grad_oc_own[0].astype(f32)
-    sums = jnp.concatenate([conv_sums, head_sums], axis=0)
-    got_bc = to_ranks(after(jnp.concatenate([grad_wb, grad_wc], axis=2), e1_folded))
-    got_a = to_ranks(grad_wa)
-    table = all_sums(sums)
-    e1 = (after(e1[0], got_bc, table),) + e1[1:]
-    (grad_x,) = on_rows(
-        norm_back_kernel, block, [x, *map(unlined, e1), grad_hidden], [bf16], "norm_back_in"
-    )
+    grad_oc_own = owner_z(after(oc_all, grad_wa_terms))[0].astype(f32)
+    got = to_ranks(after(jnp.concatenate([grad_wa, grad_wb, grad_wc], axis=2), e1_folded))
 
     def unrank(values):
         return values.transpose(1, 0, 2).reshape(share, -1)
-
-    got_a, got_bc = got_a.astype(f32), got_bc.astype(f32)
-    got_b, got_c = got_bc[..., :cols_b], got_bc[..., cols_b:]
-    d_input = unrank(got_a[..., :OWN_SSM])
-    d_state = unrank(got_a[..., OWN_SSM:OWN_CONV])
-    d_step = unrank(got_a[..., OWN_CONV : OWN_CONV + OWN_HEADS])
-    d_query = unrank(got_b[..., :ATT_HEAD])
-    d_kv = got_b[..., ATT_HEAD:].reshape(KVHEADS, RANKS // KVHEADS, share, 2, ATT_HEAD).sum(1)
-    d_kv = d_kv.transpose(1, 2, 0, 3).reshape(share, 2 * group_kv)
-    d_gating = unrank(got_c)
 
     def ff_unrank(values):
         return (
@@ -1578,25 +1597,44 @@
             .reshape(share, -1)
         )
 
-    d_gate, d_up = ff_unrank(got_gu[..., :own_ff]), ff_unrank(got_gu[..., own_ff:])
-
     def gain_grad(pairs):
         return sum(jnp.sum(w.astype(f32) * d, axis=1) for w, d in pairs)
 
-    d_norm_gain = gain_grad(
-        (
-            (gating_weight, d_gating),
-            (input_weight, d_input),
-            (state_weight, d_state),
-            (step_weight, d_step),
-            (query_weight, d_query),
-            (keyval_weight, d_kv),
-        )
-    )
-    d_mlp_gain = gain_grad(((gate_weight, d_gate), (up_weight, d_up)))
-    d_out = grad_oc_own[:row_out]
-    d_ctx = grad_oc_own[row_out:]
+    d_gate, d_up = ff_unrank(got_gu[..., :own_ff]), ff_unrank(got_gu[..., own_ff:])
+    d_out, d_ctx = grad_oc_own[:row_out], grad_oc_own[row_out:]
+    ready = (
+        gain_grad(((gate_weight, d_gate), (up_weight, d_up))),
+        d_gate * gain2_col,
+        d_up * gain2_col,
+        grad_down.astype(f32),
+        result,
+    )
+    *e1, got, ready = lax.optimization_barrier((*e1, got, ready))
+    got_a, got_bc = got[..., :cols_a], got[..., cols_a:]
+    d_mlp_gain, d_gate, d_up, d_down, result = ready
     d_ssm_gain = gain_grad(((out_weight, d_out),))
+    (grad_x,) = on_rows(
+        norm_back_kernel, block, [x, *map(unlined, e1), grad_hidden], [bf16], "norm_back_in"
+    )
+
+    got_bc = got_bc.astype(f32)
+    got_b, got_c = got_bc[..., :cols_b], got_bc[..., cols_b:]
+    d_query = unrank(got_b[..., :ATT_HEAD])
+    d_kv = got_b[..., ATT_HEAD:].reshape(KVHEADS, RANKS // KVHEADS, share, 2, ATT_HEAD).sum(1)
+    d_kv = d_kv.transpose(1, 2, 0, 3).reshape(share, 2 * group_kv)
+    d_gating = unrank(got_c)
+    gain_part = gain_grad(
+        ((gating_weight, d_gating), (query_weight, d_query), (keyval_weight, d_kv))
+    )
+    ready = (gain_part, d_query * gain_col, d_kv * gain_col, d_gating * gain_col)
+    gain_part, d_query, d_kv, d_gating = ready
+    got_a = got_a.astype(f32)
+    d_input = unrank(got_a[..., :OWN_SSM])
+    d_state = unrank(got_a[..., OWN_SSM:OWN_CONV])
+    d_step = unrank(got_a[..., OWN_CONV : OWN_CONV + OWN_HEADS])
+    d_norm_gain = gain_part + gain_grad(
+        ((input_weight, d_input), (state_weight, d_state), (step_weight, d_step))
+    )
 
     place = jnp.arange(RANKS)
     chosen = ((place ^ rank)[:, None] == place[None, :]).astype(f32)
@@ -1612,7 +1650,7 @@
         result[None],
         grad_x[None],
         d_norm_gain,
-        d_gating * gain_col,
+        d_gating,
         d_input * gain_col,
         d_state * gain_col,
         d_step * gain_col,
@@ -1623,13 +1661,13 @@
         heads[2],
         d_ssm_gain,
         d_out * ssm_gain_col,
-        d_query * gain_col,
-        d_kv * gain_col,
+        d_query,
+        d_kv,
         d_ctx,
         d_mlp_gain,
-        d_gate * gain2_col,
-        d_up * gain2_col,
-        grad_down.astype(f32),
+        d_gate,
+        d_up,
+        d_down,
     )
 
 

time: 1060 us -> 996 us (0.940)
  waiting for transfers between devices: 359 us -> 264 us
  Pallas kernels: 392 us -> 414 us
    ppermute x47, waiting for transfers between devices: 229 us -> 125 us  [hop(): return lax.ppermute(values, 'b', [(i, i ^ flip) for i in range(ROWS)])]
    pallas_call x8 -> x16, Pallas kernels: 66.3 us -> 98.8 us  [group_terms(): pl.pallas_call(lambda *refs: terms_kernel(len(lefts), turned, len(got), n...]
    reduce_scatter x3, waiting for transfers between devices: 0.01 us -> 26.1 us  [owner_z(): return lax.psum_scatter(values, 'z', scatter_dimension=0, tiled=True)]
    all_to_all x4 -> x3, waiting for transfers between devices: 41.2 us -> 31.3 us  [to_ranks(): lax.all_to_all(values, ('b', 'c'), split_axis=0, concat_axis=0, tiled=True)]
    unnamed x179 -> x171, local copies, waits for them, and re-layouts: 21.7 us -> 18.3 us
  transfers between devices with their start and end apart: 120 -> 119, of which waited for: 58 -> 49; matrix products, arithmetic and copies ran while one was open for 13% -> 15% of each run, Pallas kernels for 31% -> 38%
where the time goes in v3:
time: 996 us; the launch traced here: 987 us
  Pallas kernels  414 us (42%)
  waiting for transfers between devices  264 us (27%)
  local copies, waits for them, and re-layouts  123 us (12%)
  starting transfers between devices  89.8 us (9%)
  other arithmetic  59.7 us (6%)
  blocking collectives  19.2 us (2%)
  between operations  16.3 us (2%)
    ppermute x47, waiting for transfers between devices, hop(): return lax.ppermute(values, 'b', [(i, i ^ flip) for i in range(ROWS)])  125 us
    pallas_call x16, Pallas kernels, group_terms(): pl.pallas_call(lambda *refs: terms_kernel(len(lefts), turned, len(got), n...  98.8 us
    pallas_call x6, Pallas kernels, weight_grad(): pl.pallas_call(weight_grad_kernel, grid=(parts,), in_specs=[pl.BlockSpec(...  62.8 us
    ppermute x47, starting transfers between devices, hop(): return lax.ppermute(values, 'b', [(i, i ^ flip) for i in range(ROWS)])  49.9 us
    pallas_call x1, Pallas kernels, ssm_back(): pl.pallas_call(ssm_back_kernel, grid_spec=pltpu.PrefetchScalarGridSpec(nu...  39.5 us
    all_gather x6, waiting for transfers between devices, along_z(): return lax.all_gather(values, 'z', axis=0, tiled=True)  35.9 us
    all_to_all x3, waiting for transfers between devices, to_ranks(): lax.all_to_all(values, ('b', 'c'), split_axis=0, concat_axis=0, tiled=True)  31.3 us
    reduce_scatter x3, waiting for transfers between devices, owner_z(): return lax.psum_scatter(values, 'z', scatter_dimension=0, tiled=True)  26.1 us
  transfers between devices with their start and end apart: 119, of which 49 were waited for; matrix products, arithmetic and copies ran while one was open for 15% of the time, Pallas kernels for 38%

profile of v3, /device:TPU:0, one launch (start us, length us, event | category | flops | bytes accessed | tf_op | source)
XLA Modules:
  0.0 986.8 jit_solution(16124151528676475324)
XLA Ops:
  15.2 19.2 %all_to_all.20 = bf16[8,64,896]{2,1,0:T(8,128)(2,1)} all-to-all(bf16[8,64,896]{2,1,0:T(8,128)(2,1)S(1)} %copy.275), channel_id=1, replica_groups=mesh['b'=4,'z'=4,'c'=2] {'b','c'}, dimensions={0} | all-to-all | bytes 1835008 | tf_op jit(solution)/shard_map/all_to_all | solution.py:1241
  48.6 12.9 %collective-permute-done.refs_1_.refs_2_ = bf16[256,2048]{1,0:T(8,128)(2,1)S(1)} collective-permute-done((bf16[256,2048]{1,0:T(8,128)(2,1)}, bf16[256,2048]{1,0:T(8,128)(2,1)S(1)}, u32[]{:S(2)}, u32[]{:S(2)}) %collective-permute-start) | collective-permute-done | bytes 1048608 | tf_op jit(solution)/shard_map/ppermute | solution.py:62
  72.1 14.3 %all-to-all-done = bf16[8,64,1408]{2,1,0:T(8,128)(2,1)} async-done(((bf16[8,64,1408]{2,1,0:T(8,128)(2,1)}), bf16[8,64,1408]{2,1,0:T(8,128)(2,1)}, u32[]{:S(2)}, u32[]{:S(2)}) %all-to-all-start) | async-done | bytes 1441824 | tf_op jit(solution)/shard_map/all_to_all | solution.py:1241
  86.4 9.7 collective-permute-done.4.refs_3_.refs_4_
  107.6 16.0 %times.2.proj.query.key.value = f32[8,256,896]{2,1,0:T(8,128)} custom-call(bf16[256,2048]{1,0:T(8,128)(2,1)} %norm_in.1.refs_0_.refs_1_, bf16[256,2048]{1,0:T(8,128)(2,1)} %copy-done.5, bf16[256,2048]{1,0:T(8,128)(2,1)} %copy-done.6, bf16[128,2048]{1,0:T(8,128)(2,1)} %collective-permute-done.4.refs_3_.refs_4_, ...), custom_call_target="tpu_custom_call" | custom-call | bytes 17820000 | tf_op jit(solution)/shard_map/times/pallas_call | solution.py:845
  151.8 11.9 %conv_forward.1 = (bf16[8,256,384]{2,1,0:T(8,128)(2,1)}, bf16[4,256,128]{2,1,0:T(8,128)(2,1)}, f32[8,256,512]{2,1,0:T(8,128)}, f32[8,256,32]{2,1,0:T(8,128)}, f32[8,16,256]{2,1,0:T(8,128)}) custom-call(f32[8,256,896]{2,1,0:T(8,128)} %times.2.proj.query.key.value, f32[8,8,512]{2,1,0:T(8,128)} %bitcast_convert_fusion.halo, f32[8,256,8]{2,1,0:T(8,128)} %marks.1, ...), custom_call_target="tpu_custom_call" | custom-call | bytes 8800000 | tf_op jit(solution)/shard_map/conv_forward/pallas_call | solution.py:244
  190.0 11.4 %local_states.1 = (f32[4,384,256]{2,1,0:T(8,128)}, f32[4,384,256]{2,1,0:T(8,128)}) custom-call(s32[3]{0:T(128)} %pad_add_fusion.1.where, bf16[8,256,384]{2,1,0:T(8,128)(2,1)} %get-tuple-element.202.xs, bf16[8,4,256,128]{3,2,1,0:T(8,128)(2,1)} %copy-done, bf16[8,4,256,128]{3,2,1,0:T(8,128)(2,1)} %copy-done, bf16[8,4,256,128]{3,2,1,0:T(8,128)(2,1)} %copy-done, ...), custom_call_target="tpu_custom_call" | custom-call | bytes 8800000 | tf_op jit(solution)/shard_map/local_states/pallas_call | solution.py:343
  210.6 18.1 %collective-permute-done.16 = bf16[4,384,256]{2,1,0:T(8,128)(2,1)S(1)} collective-permute-done((bf16[4,384,256]{2,1,0:T(8,128)(2,1)S(1)}, bf16[4,384,256]{2,1,0:T(8,128)(2,1)S(1)}, u32[]{:S(2)}, u32[]{:S(2)}) %collective-permute-start.16) | collective-permute-done | bytes 786464 | tf_op jit(solution)/shard_map/ppermute | solution.py:1402
  231.6 9.7 times.3.gating.refs_13_
  242.1 15.8 %attend.1 = (f32[2,4,256,128]{3,2,1,0:T(8,128)}, bf16[2,4,256,128]{3,2,1,0:T(8,128)(2,1)}, f32[4,512,8]{2,1,0:T(8,128)}) custom-call(s32[3]{0:T(128)} %pad_add_fusion.1.where, bf16[2,4,256,128]{3,2,1,0:T(8,128)(2,1)} %get-tuple-element.211.query, bf16[4,2,512,256]{3,2,1,0:T(8,128)(2,1)} %all-gather.9.cloned.1.call-done.kv_own, ...), custom_call_target="tpu_custom_call" | custom-call | bytes 11000000 | tf_op jit(solution)/shard_map/attend/pallas_call | solution.py:483
  266.4 19.8 %ssm_forward.1 = (f32[8,256,384]{2,1,0:T(8,128)}, bf16[8,256,384]{2,1,0:T(8,128)(2,1)}, f32[8,8,256]{2,1,0:T(8,128)}) custom-call(s32[3]{0:T(128)} %pad_add_fusion.1.where, bf16[8,256,384]{2,1,0:T(8,128)(2,1)} %get-tuple-element.202.xs, bf16[8,4,256,128]{3,2,1,0:T(8,128)(2,1)} %copy-done, bf16[8,4,256,128]{3,2,1,0:T(8,128)(2,1)} %copy-done, ...), custom_call_target="tpu_custom_call" | custom-call | bytes 17600000 | tf_op jit(solution)/shard_map/ssm_forward/pallas_call | solution.py:393
  287.4 21.1 %all-gather.13.cloned.1.call-done = bf16[4,128,2048]{2,1,0:T(8,128)(2,1)} async-done(((bf16[1,128,2048]{2,1,0:T(8,128)(2,1)}), bf16[4,128,2048]{2,1,0:T(8,128)(2,1)}) %all-gather.13.cloned.1.call-update) | async-done | bytes 2097168 | tf_op jit(solution)/shard_map/all_gather | solution.py:1248
  359.5 22.5 %collective-permute-done.38.refs_2_ = bf16[256,2048]{1,0:T(8,128)(2,1)S(1)} collective-permute-done((bf16[256,2048]{1,0:T(8,128)(2,1)}, bf16[256,2048]{1,0:T(8,128)(2,1)S(1)}, u32[]{:S(2)}, u32[]{:S(2)}) %collective-permute-start.38) | collective-permute-done | bytes 1048608 | tf_op jit(solution)/shard_map/ppermute | solution.py:62
  389.9 21.0 %collective-permute-done.40.refs_1_.refs_2_ = bf16[256,2048]{1,0:T(8,128)(2,1)S(1)} collective-permute-done((bf16[256,2048]{1,0:T(8,128)(2,1)}, bf16[256,2048]{1,0:T(8,128)(2,1)S(1)}, u32[]{:S(2)}, u32[]{:S(2)}) %collective-permute-start.40) | collective-permute-done | bytes 1048608 | tf_op jit(solution)/shard_map/ppermute | solution.py:62
  413.9 9.2 collective-permute-done.42.refs_3_.refs_4_
  426.9 8.6 all-gather.15.cloned.1.call-done
  436.5 21.2 %feed.1 = (bf16[2048,512]{1,0:T(8,128)(2,1)}, bf16[2048,1024]{1,0:T(8,128)(2,1)}) custom-call(bf16[256,2048]{1,0:T(8,128)(2,1)} %get-tuple-element.234.refs_0_.refs_1_, bf16[256,2048]{1,0:T(8,128)(2,1)} %copy-done.16, bf16[256,2048]{1,0:T(8,128)(2,1)} %copy-done.17, bf16[128,2048]{1,0:T(8,128)(2,1)} %collective-permute-done.42.refs_3_.refs_4_, ...), custom_call_target="tpu_custom_call" | custom-call | bytes 25300000 | tf_op jit(solution)/shard_map/feed/pallas_call | solution.py:1172
  492.0 9.9 weight_grad.6
  513.1 15.9 %weight_grad.7 = bf16[4,1024,512]{2,1,0:T(8,128)(2,1)} custom-call(bf16[1024,2048]{1,0:T(8,128)(2,1)} %bitcast.275, bf16[256,2048]{1,0:T(8,128)(2,1)} %get-tuple-element.234.refs_0_.refs_1_, bf16[256,2048]{1,0:T(8,128)(2,1)} %copy-done.16, bf16[256,2048]{1,0:T(8,128)(2,1)} %copy-done.17, bf16[128,2048]{1,0:T(8,128)(2,1)} %collective-permute-done.42.refs_3_.refs_4_, ...), custom_call_target="tpu_custom_call" | custom-call | bytes 15664000 | tf_op jit(solution)/shard_map/weight_grad/pallas_call | solution.py:908
  583.5 15.6 %mixer_back.1 = (f32[8,256,384]{2,1,0:T(8,128)}, bf16[8,256,128]{2,1,0:T(8,128)(2,1)}, f32[8,8,256]{2,1,0:T(8,128)}) custom-call(bf16[256,2048]{1,0:T(8,128)(2,1)} %get-tuple-element.266.refs_0_.refs_1_, bf16[256,2048]{1,0:T(8,128)(2,1)} %copy-done.18, bf16[256,2048]{1,0:T(8,128)(2,1)} %collective-permute-done.58.refs_2_.refs_3_, ...), custom_call_target="tpu_custom_call" | custom-call | bytes 14300000 | tf_op jit(solution)/shard_map/mixer_back/pallas_call | solution.py:872
  604.2 9.9 %weight_grad.8 = bf16[512,2048]{1,0:T(8,128)(2,1)} custom-call(bf16[512,2048]{1,0:T(8,128)(2,1)} %maximum_bitcast_fusion.refs_0_, bf16[256,2048]{1,0:T(8,128)(2,1)} %get-tuple-element.266.refs_0_.refs_1_, bf16[256,2048]{1,0:T(8,128)(2,1)} %copy-done.18, bf16[256,2048]{1,0:T(8,128)(2,1)} %collective-permute-done.58.refs_2_.refs_3_, ...), custom_call_target="tpu_custom_call" | custom-call | bytes 10032000 | tf_op jit(solution)/shard_map/weight_grad/pallas_call | solution.py:908
  621.4 14.3 %gate_back.1 = (bf16[8,256,384]{2,1,0:T(8,128)(2,1)}, bf16[8,256,384]{2,1,0:T(8,128)(2,1)}, f32[4,384,256]{2,1,0:T(8,128)}, f32[4,384,256]{2,1,0:T(8,128)}) custom-call(s32[3]{0:T(128)} %pad_add_fusion.1.where, f32[8,256,384]{2,1,0:T(8,128)} %get-tuple-element.290.es, f32[8,256,8]{2,1,0:T(8,128)} %pad.41.scale, f32[8,256,384]{2,1,0:T(8,128)} %times.3.gating.refs_13_, ...), custom_call_target="tpu_custom_call" | custom-call | bytes 12100000 | tf_op jit(solution)/shard_map/gate_back/pallas_call | solution.py:607
  648.0 13.1 %reduce-scatter.10.cloned.1.call-done = bf16[128,2048]{1,0:T(8,128)(2,1)} async-done(((bf16[512,2048]{1,0:T(8,128)(2,1)}), bf16[128,2048]{1,0:T(8,128)(2,1)}) %reduce-scatter.10.cloned.1.call-update) | async-done | bytes 524304 | tf_op jit(solution)/shard_map/reduce_scatter | solution.py:1251
  696.2 18.0 %attend_back.1 = (f32[2,4,256,128]{3,2,1,0:T(8,128)}, bf16[4,4,512,256]{3,2,1,0:T(8,128)(2,1)}) custom-call(s32[3]{0:T(128)} %pad_add_fusion.1.where, bf16[2,4,256,128]{3,2,1,0:T(8,128)(2,1)} %get-tuple-element.211.query, bf16[4,2,512,256]{3,2,1,0:T(8,128)(2,1)} %all-gather.9.cloned.1.call-done.kv_own, ...), custom_call_target="tpu_custom_call" | custom-call | bytes 15400000 | tf_op jit(solution)/shard_map/attend_back/pallas_call | solution.py:548
  733.2 39.5 %ssm_back.1 = (f32[8,256,384]{2,1,0:T(8,128)}, bf16[4,256,128]{2,1,0:T(8,128)(2,1)}, bf16[4,256,128]{2,1,0:T(8,128)(2,1)}, bf16[4,256,128]{2,1,0:T(8,128)(2,1)},...) custom-call(s32[3]{0:T(128)} %pad_add_fusion.1.where, ...), custom_call_target="tpu_custom_call" | custom-call | bytes 33000000 | tf_op jit(solution)/shard_map/ssm_back/pallas_call | solution.py:721
  774.3 10.7 %reduce-scatter.12.cloned.1.call-done = bf16[1,2,512,256]{3,2,1,0:T(8,128)(2,1)} async-done(((bf16[4,2,512,256]{3,2,1,0:T(8,128)(2,1)}), bf16[1,2,512,256]{3,2,1,0:T(8,128)(2,1)}) %reduce-scatter.12.cloned.1.call-update) | async-done | bytes 524304 | tf_op jit(solution)/shard_map/reduce_scatter | solution.py:1251
  797.0 8.7 weight_grad.10
  832.7 11.2 %conv_backward.1 = (bf16[8,256,512]{2,1,0:T(8,128)(2,1)}, f32[8,8,512]{2,1,0:T(8,128)}) custom-call(f32[8,256,384]{2,1,0:T(8,128)} %get-tuple-element.322.grad_xs, f32[4,256,128]{2,1,0:T(8,128)} %copy-done.23, f32[8,256,8]{2,1,0:T(8,128)} %get-tuple-element.331.step, f32[8,256,512]{2,1,0:T(8,128)} %get-tuple-element.332.slope, ...), custom_call_target="tpu_custom_call" | custom-call | bytes 6600000 | tf_op jit(solution)/shard_map/conv_backward/pallas_call | solution.py:789
  847.9 9.9 %weight_grad.11 = bf16[4,512,512]{2,1,0:T(8,128)(2,1)} custom-call(bf16[512,2048]{1,0:T(8,128)(2,1)} %copy.304.refs_0_, bf16[256,2048]{1,0:T(8,128)(2,1)} %norm_in.1.refs_0_.refs_1_, bf16[256,2048]{1,0:T(8,128)(2,1)} %copy-done.5, bf16[256,2048]{1,0:T(8,128)(2,1)} %copy-done.6, bf16[128,2048]{1,0:T(8,128)(2,1)} %collective-permute-done.4.refs_3_.refs_4_, ...), custom_call_target="tpu_custom_call" | custom-call | bytes 10032000 | tf_op jit(solution)/shard_map/weight_grad/pallas_call | solution.py:908
  875.0 8.8 group_terms.28
  915.4 9.5 group_terms.29
  957.6 9.3 all-to-all-done.3
  (678 shorter events, 503.9 us)
Async XLA Ops:
  7.2 98.8 %all-gather.7.cloned.1.call-start = ((), (), s32[]{:S(2)}) async-start(), calls=%async_computation.11 | async-start | bytes 4587520 | tf_op jit(solution)/shard_map/all_gather | solution.py:1248
  66.2 135.2 %all-gather.9.cloned.1.call-start = ((), (), s32[]{:S(2)}) async-start(), calls=%async_computation.12 | async-start | bytes 2621440 | tf_op jit(solution)/shard_map/all_gather | solution.py:1248
  66.9 29.8 %collective-permute-start.7 = (bf16[256,2048]{1,0:T(8,128)(2,1)S(1)}, bf16[256,2048]{1,0:T(8,128)(2,1)}, u32[]{:S(2)}, u32[]{:S(2)}) collective-permute-start(bf16[256,2048]{1,0:T(8,128)(2,1)S(1)} %collective-permute-done.refs_1_.refs_2_), channel_id=1, source_target_pairs={{0,1},{1,0},{2,3},{3,2},{4,5},{5,4},{6,7},{7,6},{8,9},{9,8},{10,11... | collective-permute-start | bytes 3145736 | tf_op jit(solution)/shard_map/ppermute | solution.py:66
  67.9 28.2 %collective-permute-start.4 = (bf16[128,2048]{1,0:T(8,128)(2,1)}, bf16[128,2048]{1,0:T(8,128)(2,1)}, u32[]{:S(2)}, u32[]{:S(2)}) collective-permute-start(bf16[128,2048]{1,0:T(8,128)(2,1)} %slice.304), channel_id=1, source_target_pairs={{0,16},{8,24},{16,0},{24,8},{1,17},{9,25},{17,1},{25,9},{2,18},{10... | collective-permute-start | bytes 1572872 | tf_op jit(solution)/shard_map/ppermute | solution.py:62
  72.1 33.9 %collective-permute-start.8 = (bf16[256,2048]{1,0:T(8,128)(2,1)S(1)}, bf16[256,2048]{1,0:T(8,128)(2,1)}, u32[]{:S(2)}, u32[]{:S(2)}) collective-permute-start(bf16[256,2048]{1,0:T(8,128)(2,1)S(1)} %collective-permute-done.1.refs_2_.refs_3_), channel_id=1, source_target_pairs={{0,1},{1,0},{2,3},{3,2},{4,5},{5,4},{6,7},{7,6},{8,9},{9,8},{10,11... | collective-permute-start | bytes 3145736 | tf_op jit(solution)/shard_map/ppermute | solution.py:66
  86.4 37.2 %collective-permute-start.2 = (bf16[256,2048]{1,0:T(8,128)(2,1)}, bf16[256,2048]{1,0:T(8,128)(2,1)}, u32[]{:S(2)}, u32[]{:S(2)}) collective-permute-start(bf16[256,2048]{1,0:T(8,128)(2,1)} %bitcast.281), channel_id=1, source_target_pairs={{0,8},{8,0},{16,24},{24,16},{1,9},{9,1},{17,25},{25,17},{2,10},{10... | collective-permute-start | bytes 3145736 | tf_op jit(solution)/shard_map/ppermute | solution.py:62
  96.1 27.5 %collective-permute-start.3 = (bf16[256,2048]{1,0:T(8,128)(2,1)}, bf16[256,2048]{1,0:T(8,128)(2,1)}, u32[]{:S(2)}, u32[]{:S(2)}) collective-permute-start(bf16[256,2048]{1,0:T(8,128)(2,1)} %bitcast.282), channel_id=1, source_target_pairs={{0,16},{8,24},{16,0},{24,8},{1,17},{9,25},{17,1},{25,9},{2,18},{10... | collective-permute-start | bytes 3145736 | tf_op jit(solution)/shard_map/ppermute | solution.py:62
  133.0 98.6 %all-gather.11.cloned.1.call-start = ((), (), s32[]{:S(2)}) async-start(), calls=%async_computation.13 | async-start | bytes 1966080 | tf_op jit(solution)/shard_map/all_gather | solution.py:1248
  134.4 67.0 %collective-permute-start.19 = (bf16[256,2048]{1,0:T(8,128)(2,1)S(1)}, bf16[256,2048]{1,0:T(8,128)(2,1)}, u32[]{:S(2)}, u32[]{:S(2)}) collective-permute-start(bf16[256,2048]{1,0:T(8,128)(2,1)S(1)} %bitcast.286), channel_id=1, source_target_pairs={{0,1},{1,0},{2,3},{3,2},{4,5},{5,4},{6,7},{7,6},{8,9},{9,8},{10,11... | collective-permute-start | bytes 3145736 | tf_op jit(solution)/shard_map/ppermute | solution.py:66
  139.0 68.7 %collective-permute-start.20 = (bf16[256,2048]{1,0:T(8,128)(2,1)}, bf16[256,2048]{1,0:T(8,128)(2,1)}, u32[]{:S(2)}, u32[]{:S(2)}) collective-permute-start(bf16[256,2048]{1,0:T(8,128)(2,1)} %collective-permute-done.2.refs_11_.refs_2_), channel_id=1, source_target_pairs={{0,1},{1,0},{2,3},{3,2},{4,5},{5,4},{6,7},{7,6},{8,9},{9,8},{10,11... | collective-permute-start | bytes 3145736 | tf_op jit(solution)/shard_map/ppermute | solution.py:66
  150.6 157.9 %all-gather.13.cloned.1.call-start = ((), (), s32[]{:S(2)}) async-start(), calls=%async_computation.14 | async-start | bytes 2621440 | tf_op jit(solution)/shard_map/all_gather | solution.py:1248
  173.1 35.1 %collective-permute-start.21 = (bf16[256,2048]{1,0:T(8,128)(2,1)}, bf16[256,2048]{1,0:T(8,128)(2,1)}, u32[]{:S(2)}, u32[]{:S(2)}) collective-permute-start(bf16[256,2048]{1,0:T(8,128)(2,1)} %collective-permute-done.3.refs_12_.refs_3_), channel_id=1, source_target_pairs={{0,1},{1,0},{2,3},{3,2},{4,5},{5,4},{6,7},{7,6},{8,9},{9,8},{10,11... | collective-permute-start | bytes 3145736 | tf_op jit(solution)/shard_map/ppermute | solution.py:66
  201.4 39.9 %collective-permute-start.25 = (bf16[4,2,512,256]{3,2,1,0:T(8,128)(2,1)}, bf16[4,2,512,256]{3,2,1,0:T(8,128)(2,1)}, u32[]{:S(2)}, u32[]{:S(2)}) collective-permute-start(bf16[4,2,512,256]{3,2,1,0:T(8,128)(2,1)} %all-gather.9.cloned.1.call-done.kv_own), channel_id=1, source_target_pairs={{0,1},{1,0},{2,3},{3,2},{4,5},{5,4},{6,7},{7,6},{8,9},{9,8},{10,11... | collective-permute-start | bytes 6291464 | tf_op jit(solution)/shard_map/ppermute | solution.py:66
  229.9 28.1 %collective-permute-start.24 = (bf16[4,384,256]{2,1,0:T(8,128)(2,1)}, bf16[4,384,256]{2,1,0:T(8,128)(2,1)S(1)}, u32[]{:S(2)}, u32[]{:S(2)}) collective-permute-start(bf16[4,384,256]{2,1,0:T(8,128)(2,1)} %fusion.1), channel_id=1, source_target_pairs={{2,4},{3,5},{10,12},{11,13},{18,20},{19,21},{26,28},{27,29}} | collective-permute-start | bytes 2359304 | tf_op jit(solution)/shard_map/ppermute | solution.py:1402
  259.1 167.7 %all-gather.17.cloned.1.call-start = ((), (), s32[]{:S(2)}) async-start(), calls=%async_computation.16 | async-start | bytes 2621440 | tf_op jit(solution)/shard_map/all_gather | solution.py:1248
  263.6 171.8 %all-gather.15.cloned.1.call-start = ((), (), s32[]{:S(2)}) async-start(), calls=%async_computation.15 | async-start | bytes 5242880 | tf_op jit(solution)/shard_map/all_gather | solution.py:1248
  287.1 358.6 %reduce-scatter.8.cloned.1.call-start = ((), (), s32[]{:S(2)}) async-start(), calls=%async_computation.17 | async-start | bytes 5242880 | tf_op jit(solution)/shard_map/reduce_scatter | solution.py:1244
  389.9 45.6 %collective-permute-start.44 = (bf16[256,2048]{1,0:T(8,128)(2,1)}, bf16[256,2048]{1,0:T(8,128)(2,1)S(1)}, u32[]{:S(2)}, u32[]{:S(2)}) collective-permute-start(bf16[256,2048]{1,0:T(8,128)(2,1)} %get-tuple-element.234.refs_0_.refs_1_), channel_id=1, source_target_pairs={{0,1},{1,0},{2,3},{3,2},{4,5},{5,4},{6,7},{7,6},{8,9},{9,8},{10,11... | collective-permute-start | bytes 3145736 | tf_op jit(solution)/shard_map/ppermute | solution.py:66
  531.6 129.4 %reduce-scatter.10.cloned.1.call-start = ((), (), s32[]{:S(2)}) async-start(), calls=%async_computation.18 | async-start | bytes 2621440 | tf_op jit(solution)/shard_map/reduce_scatter | solution.py:1251
  666.1 118.9 %reduce-scatter.12.cloned.1.call-start = ((), (), s32[]{:S(2)}) async-start(), calls=%async_computation.19 | async-start | bytes 2621440 | tf_op jit(solution)/shard_map/reduce_scatter | solution.py:1251
  667.7 46.5 %collective-permute-start.80 = (bf16[256,2048]{1,0:T(8,128)(2,1)}, bf16[256,2048]{1,0:T(8,128)(2,1)}, u32[]{:S(2)}, u32[]{:S(2)}) collective-permute-start(bf16[256,2048]{1,0:T(8,128)(2,1)} %get-tuple-element.301), channel_id=1, source_target_pairs={{0,8},{8,0},{16,24},{24,16},{1,9},{9,1},{17,25},{25,17},{2,10},{10... | collective-permute-start | bytes 3145736 | tf_op jit(solution)/shard_map/ppermute | solution.py:62
  669.7 44.6 %collective-permute-start.81 = (bf16[256,2048]{1,0:T(8,128)(2,1)}, bf16[256,2048]{1,0:T(8,128)(2,1)}, u32[]{:S(2)}, u32[]{:S(2)}) collective-permute-start(bf16[256,2048]{1,0:T(8,128)(2,1)} %get-tuple-element.316), channel_id=1, source_target_pairs={{0,16},{8,24},{16,0},{24,8},{1,17},{9,25},{17,1},{25,9},{2,18},{10... | collective-permute-start | bytes 3145736 | tf_op jit(solution)/shard_map/ppermute | solution.py:62
  684.7 36.9 %collective-permute-start.79 = (bf16[4,384,256]{2,1,0:T(8,128)(2,1)}, bf16[4,384,256]{2,1,0:T(8,128)(2,1)S(1)}, u32[]{:S(2)}, u32[]{:S(2)}) collective-permute-start(bf16[4,384,256]{2,1,0:T(8,128)(2,1)} %add_convert_fusion.2), channel_id=1, source_target_pairs={{2,0},{3,1},{10,8},{11,9},{18,16},{19,17},{26,24},{27,25}} | collective-permute-start | bytes 2359304 | tf_op jit(solution)/shard_map/ppermute | solution.py:1502
  729.6 183.9 %reduce-scatter.18.cloned.1.call-start = ((), (), s32[]{:S(2)}) async-start(), calls=%async_computation.22 | async-start | bytes 1966080 | tf_op jit(solution)/shard_map/reduce_scatter | solution.py:1244
  730.2 207.5 %reduce-scatter.16.cloned.1.call-start = ((), (), s32[]{:S(2)}) async-start(), calls=%async_computation.21 | async-start | bytes 1966080 | tf_op jit(solution)/shard_map/reduce_scatter | solution.py:1244
  774.1 31.7 %collective-permute-start.83 = (bf16[4,4,256,128]{3,2,1,0:T(8,128)(2,1)S(1)}, bf16[4,4,256,128]{3,2,1,0:T(8,128)(2,1)S(1)}, u32[]{:S(2)}, u32[]{:S(2)}) collective-permute-start(bf16[4,4,256,128]{3,2,1,0:T(8,128)(2,1)S(1)} %pad_maximum_fusion.3), channel_id=1, source_target_pairs={{0,1},{1,0},{2,3},{3,2},{4,5},{5,4},{6,7},{7,6},{8,9},{9,8},{10,11... | collective-permute-start | bytes 3145736 | tf_op jit(solution)/shard_map/ppermute | solution.py:66
  805.7 133.1 %reduce-scatter.14.cloned.1.call-start = ((), (), s32[]{:S(2)}) async-start(), calls=%async_computation.20 | async-start | bytes 2621440 | tf_op jit(solution)/shard_map/reduce_scatter | solution.py:1244
  857.8 93.0 %reduce-scatter.20.cloned.1.call-start = ((), (), s32[]{:S(2)}) async-start(), calls=%async_computation.23 | async-start | bytes 2621440 | tf_op jit(solution)/shard_map/reduce_scatter | solution.py:1251
  883.8 31.6 %collective-permute-start.88 = (bf16[256,2048]{1,0:T(8,128)(2,1)}, bf16[256,2048]{1,0:T(8,128)(2,1)}, u32[]{:S(2)}, u32[]{:S(2)}) collective-permute-start(bf16[256,2048]{1,0:T(8,128)(2,1)} %get-tuple-element.336), channel_id=1, source_target_pairs={{0,1},{1,0},{2,3},{3,2},{4,5},{5,4},{6,7},{7,6},{8,9},{9,8},{10,11... | collective-permute-start | bytes 3145736 | tf_op jit(solution)/shard_map/ppermute | solution.py:66
  883.8 31.6 %collective-permute-start.89 = (bf16[256,2048]{1,0:T(8,128)(2,1)}, bf16[256,2048]{1,0:T(8,128)(2,1)}, u32[]{:S(2)}, u32[]{:S(2)}) collective-permute-start(bf16[256,2048]{1,0:T(8,128)(2,1)} %get-tuple-element.337), channel_id=1, source_target_pairs={{0,1},{1,0},{2,3},{3,2},{4,5},{5,4},{6,7},{7,6},{8,9},{9,8},{10,11... | collective-permute-start | bytes 3145736 | tf_op jit(solution)/shard_map/ppermute | solution.py:66
  884.3 31.1 %collective-permute-start.90 = (bf16[256,2048]{1,0:T(8,128)(2,1)}, bf16[256,2048]{1,0:T(8,128)(2,1)}, u32[]{:S(2)}, u32[]{:S(2)}) collective-permute-start(bf16[256,2048]{1,0:T(8,128)(2,1)} %get-tuple-element.338), channel_id=1, source_target_pairs={{0,1},{1,0},{2,3},{3,2},{4,5},{5,4},{6,7},{7,6},{8,9},{9,8},{10,11... | collective-permute-start | bytes 3145736 | tf_op jit(solution)/shard_map/ppermute | solution.py:66
  929.5 28.2 %collective-permute-start.102 = (bf16[256,2048]{1,0:T(8,128)(2,1)}, bf16[256,2048]{1,0:T(8,128)(2,1)}, u32[]{:S(2)}, u32[]{:S(2)}) collective-permute-start(bf16[256,2048]{1,0:T(8,128)(2,1)} %get-tuple-element.349), channel_id=1, source_target_pairs={{0,16},{8,24},{16,0},{24,8},{1,17},{9,25},{17,1},{25,9},{2,18},{10... | collective-permute-start | bytes 3145736 | tf_op jit(solution)/shard_map/ppermute | solution.py:62
  (169 other events, 1836.0 us)
Sparse Core Ops, SparseCore 0:
  34.5 71.4 all-gather.6
  133.1 44.5 all-gather.8
  179.3 36.4 all-gather.10
  259.2 49.1 all-gather.12
  309.9 44.6 all-gather.16
  356.0 79.4 all-gather.14
  530.7 74.3 reduce-scatter.7
  607.4 53.5 reduce-scatter.9
  729.7 55.2 reduce-scatter.11
  787.2 34.5 reduce-scatter.17
  824.3 34.4 reduce-scatter.15
  861.0 44.2 reduce-scatter.13
  907.6 43.1 reduce-scatter.19

commit v4 on v3

--- a/solution.py
+++ b/solution.py
@@ -1498,18 +1498,19 @@
             grad_query, grad_kv = attend_back(
                 where, query, kv_own, kv_other, seg_query, seg_keys, grad_context, context, logsum
             )
-            grad_wc_terms = weight_grad(after(grad_c_low, message).T, n1, zs)
         moved = lax.ppermute(message, "z", [(s, s - 1)])
         if s == zs - 1:
             late_folded, late_x, late_y = spread(for_x, for_y, to_x, to_y)
             moved, late_folded = lax.optimization_barrier((moved, late_folded))
         if s == zs - 2:
-            got_gu = to_ranks(after(grad_gu_w, message, grad_down))
             oc_all = out_grads(after(grad_oc_w, message))
-            moved, got_gu, oc_all = lax.optimization_barrier((moved, got_gu, oc_all))
+            grad_wc_terms = weight_grad(after(grad_c_low, message).T, n1, zs)
+            moved, grad_gu_w, grad_down, oc_all, grad_wc_terms = lax.optimization_barrier(
+                (moved, grad_gu_w, grad_down, oc_all, grad_wc_terms)
+            )
         if s == 1:
-            moved, grad_query, grad_kv, grad_wc_terms, late_x, late_y = lax.optimization_barrier(
-                (moved, grad_query, grad_kv, grad_wc_terms, late_x, late_y)
+            moved, grad_query, grad_kv, late_x, late_y = lax.optimization_barrier(
+                (moved, grad_query, grad_kv, late_x, late_y)
             )
         flowing = flowing + moved.astype(f32)
     grad_wc = to_owner(grad_wc_terms)
@@ -1526,7 +1527,6 @@
     grad_wb_terms = weight_grad(grad_b_low.T, n1, zs)
     grad_wb = to_owner(grad_wb_terms)
 
-    got_gu = got_gu.astype(f32)
     grad_xs, *bc_terms, grad_step, head_sums = ssm_back(
         where, xs, gy, bc, meta, meta_rows, marks, seg_rows, state, first_local, flowing, later_grad,
         p0, p1, skip_wide, head,
@@ -1552,7 +1552,8 @@
     given = jnp.stack(
         [jnp.where(c == 0, give[1], moved), jnp.where(c == 0, moved, give[0])]
     ).reshape(chunks, near, OWN_CONV)
-    given = after(given, grad_wb_terms)
+    got_gu = to_ranks(after(grad_gu_w, grad_xs))
+    given, got_gu = lax.optimization_barrier((after(given, grad_wb_terms), got_gu))
     given = jnp.pad(given, ((0, 0), (8 - near, 0), (0, LANES_A - OWN_CONV)))
     grad_a_low, conv_sums = conv_backward(
         grad_xs, grad_bc, grad_step, slope, proj, halo, marks, given, conv_own
@@ -1600,6 +1601,7 @@
     def gain_grad(pairs):
         return sum(jnp.sum(w.astype(f32) * d, axis=1) for w, d in pairs)
 
+    got_gu = got_gu.astype(f32)
     d_gate, d_up = ff_unrank(got_gu[..., :own_ff]), ff_unrank(got_gu[..., own_ff:])
     d_out, d_ctx = grad_oc_own[:row_out], grad_oc_own[row_out:]
     ready = (

time: 996 us -> 981 us (0.985)
  waiting for transfers between devices: 264 us -> 251 us
    reduce_scatter x3, waiting for transfers between devices: 26.1 us -> 2.23 us  [owner_z(): return lax.psum_scatter(values, 'z', scatter_dimension=0, tiled=True)]
    ppermute x3, waiting for transfers between devices: 7.33 us -> 27.4 us  [per_device(): moved = lax.ppermute(message, 'z', [(s, s - 1)])]
    unnamed x171 -> x199, local copies, waits for them, and re-layouts: 18.3 us -> 20.6 us
where the time goes in v4:
time: 981 us; the launch traced here: 972 us
  Pallas kernels  415 us (42%)
  waiting for transfers between devices  251 us (26%)
  local copies, waits for them, and re-layouts  124 us (13%)
  starting transfers between devices  86.2 us (9%)
  other arithmetic  59.5 us (6%)
  blocking collectives  19.2 us (2%)
  between operations  16.4 us (2%)
    ppermute x47, waiting for transfers between devices, hop(): return lax.ppermute(values, 'b', [(i, i ^ flip) for i in range(ROWS)])  125 us
    pallas_call x16, Pallas kernels, group_terms(): pl.pallas_call(lambda *refs: terms_kernel(len(lefts), turned, len(got), n...  99.4 us
    pallas_call x6, Pallas kernels, weight_grad(): pl.pallas_call(weight_grad_kernel, grid=(parts,), in_specs=[pl.BlockSpec(...  62.9 us
    ppermute x47, starting transfers between devices, hop(): return lax.ppermute(values, 'b', [(i, i ^ flip) for i in range(ROWS)])  46.4 us
    pallas_call x1, Pallas kernels, ssm_back(): pl.pallas_call(ssm_back_kernel, grid_spec=pltpu.PrefetchScalarGridSpec(nu...  39.5 us
    all_gather x6, waiting for transfers between devices, along_z(): return lax.all_gather(values, 'z', axis=0, tiled=True)  35.9 us
    ppermute x3, waiting for transfers between devices, per_device(): moved = lax.ppermute(message, 'z', [(s, s - 1)])  27.4 us
    pallas_call x2, Pallas kernels, times(): pl.pallas_call(lambda *refs: times_kernel(count, *refs), in_specs=[ANY] *...  25.7 us
  transfers between devices with their start and end apart: 119, of which 49 were waited for; matrix products, arithmetic and copies ran while one was open for 15% of the time, Pallas kernels for 38%

profile of v4, /device:TPU:0, one launch (start us, length us, event | category | flops | bytes accessed | tf_op | source)
XLA Modules:
  0.0 971.8 jit_solution(13991897101668214027)
XLA Ops:
  15.2 19.2 %all_to_all.20 = bf16[8,64,896]{2,1,0:T(8,128)(2,1)} all-to-all(bf16[8,64,896]{2,1,0:T(8,128)(2,1)S(1)} %copy.275), channel_id=1, replica_groups=mesh['b'=4,'z'=4,'c'=2] {'b','c'}, dimensions={0} | all-to-all | bytes 1835008 | tf_op jit(solution)/shard_map/all_to_all | solution.py:1241
  48.6 12.9 %collective-permute-done.refs_1_.refs_2_ = bf16[256,2048]{1,0:T(8,128)(2,1)S(1)} collective-permute-done((bf16[256,2048]{1,0:T(8,128)(2,1)}, bf16[256,2048]{1,0:T(8,128)(2,1)S(1)}, u32[]{:S(2)}, u32[]{:S(2)}) %collective-permute-start) | collective-permute-done | bytes 1048608 | tf_op jit(solution)/shard_map/ppermute | solution.py:62
  72.1 14.3 %all-to-all-done = bf16[8,64,1408]{2,1,0:T(8,128)(2,1)} async-done(((bf16[8,64,1408]{2,1,0:T(8,128)(2,1)}), bf16[8,64,1408]{2,1,0:T(8,128)(2,1)}, u32[]{:S(2)}, u32[]{:S(2)}) %all-to-all-start) | async-done | bytes 1441824 | tf_op jit(solution)/shard_map/all_to_all | solution.py:1241
  86.4 9.7 %collective-permute-done.4.refs_3_.refs_4_ = bf16[128,2048]{1,0:T(8,128)(2,1)} collective-permute-done((bf16[128,2048]{1,0:T(8,128)(2,1)}, bf16[128,2048]{1,0:T(8,128)(2,1)}, u32[]{:S(2)}, u32[]{:S(2)}) %collective-permute-start.4) | collective-permute-done | bytes 524320 | tf_op jit(solution)/shard_map/ppermute | solution.py:62
  107.6 16.0 %times.2.proj.query.key.value = f32[8,256,896]{2,1,0:T(8,128)} custom-call(bf16[256,2048]{1,0:T(8,128)(2,1)} %norm_in.1.refs_0_.refs_1_, bf16[256,2048]{1,0:T(8,128)(2,1)} %copy-done.5, bf16[256,2048]{1,0:T(8,128)(2,1)} %copy-done.6, bf16[128,2048]{1,0:T(8,128)(2,1)} %collective-permute-done.4.refs_3_.refs_4_, ...), custom_call_target="tpu_custom_call" | custom-call | bytes 17820000 | tf_op jit(solution)/shard_map/times/pallas_call | solution.py:845
  151.8 11.9 %conv_forward.1 = (bf16[8,256,384]{2,1,0:T(8,128)(2,1)}, bf16[4,256,128]{2,1,0:T(8,128)(2,1)}, f32[8,256,512]{2,1,0:T(8,128)}, f32[8,256,32]{2,1,0:T(8,128)}, f32[8,16,256]{2,1,0:T(8,128)}) custom-call(f32[8,256,896]{2,1,0:T(8,128)} %times.2.proj.query.key.value, f32[8,8,512]{2,1,0:T(8,128)} %bitcast_convert_fusion.halo, f32[8,256,8]{2,1,0:T(8,128)} %marks.1, ...), custom_call_target="tpu_custom_call" | custom-call | bytes 8800000 | tf_op jit(solution)/shard_map/conv_forward/pallas_call | solution.py:244
  190.0 11.4 %local_states.1 = (f32[4,384,256]{2,1,0:T(8,128)}, f32[4,384,256]{2,1,0:T(8,128)}) custom-call(s32[3]{0:T(128)} %pad_add_fusion.1.where, bf16[8,256,384]{2,1,0:T(8,128)(2,1)} %get-tuple-element.205.xs, bf16[8,4,256,128]{3,2,1,0:T(8,128)(2,1)} %copy-done, bf16[8,4,256,128]{3,2,1,0:T(8,128)(2,1)} %copy-done, bf16[8,4,256,128]{3,2,1,0:T(8,128)(2,1)} %copy-done, ...), custom_call_target="tpu_custom_call" | custom-call | bytes 8800000 | tf_op jit(solution)/shard_map/local_states/pallas_call | solution.py:343
  210.6 18.1 %collective-permute-done.16 = bf16[4,384,256]{2,1,0:T(8,128)(2,1)S(1)} collective-permute-done((bf16[4,384,256]{2,1,0:T(8,128)(2,1)S(1)}, bf16[4,384,256]{2,1,0:T(8,128)(2,1)S(1)}, u32[]{:S(2)}, u32[]{:S(2)}) %collective-permute-start.16) | collective-permute-done | bytes 786464 | tf_op jit(solution)/shard_map/ppermute | solution.py:1402
  231.6 9.7 times.3.gating.refs_13_
  242.1 15.8 %attend.1 = (f32[2,4,256,128]{3,2,1,0:T(8,128)}, bf16[2,4,256,128]{3,2,1,0:T(8,128)(2,1)}, f32[4,512,8]{2,1,0:T(8,128)}) custom-call(s32[3]{0:T(128)} %pad_add_fusion.1.where, bf16[2,4,256,128]{3,2,1,0:T(8,128)(2,1)} %get-tuple-element.214.query, bf16[4,2,512,256]{3,2,1,0:T(8,128)(2,1)} %all-gather.9.cloned.1.call-done.kv_own, ...), custom_call_target="tpu_custom_call" | custom-call | bytes 11000000 | tf_op jit(solution)/shard_map/attend/pallas_call | solution.py:483
  266.3 19.8 %ssm_forward.1 = (f32[8,256,384]{2,1,0:T(8,128)}, bf16[8,256,384]{2,1,0:T(8,128)(2,1)}, f32[8,8,256]{2,1,0:T(8,128)}) custom-call(s32[3]{0:T(128)} %pad_add_fusion.1.where, bf16[8,256,384]{2,1,0:T(8,128)(2,1)} %get-tuple-element.205.xs, bf16[8,4,256,128]{3,2,1,0:T(8,128)(2,1)} %copy-done, bf16[8,4,256,128]{3,2,1,0:T(8,128)(2,1)} %copy-done, ...), custom_call_target="tpu_custom_call" | custom-call | bytes 17600000 | tf_op jit(solution)/shard_map/ssm_forward/pallas_call | solution.py:393
  287.3 21.1 %all-gather.13.cloned.1.call-done = bf16[4,128,2048]{2,1,0:T(8,128)(2,1)} async-done(((bf16[1,128,2048]{2,1,0:T(8,128)(2,1)}), bf16[4,128,2048]{2,1,0:T(8,128)(2,1)}) %all-gather.13.cloned.1.call-update) | async-done | bytes 2097168 | tf_op jit(solution)/shard_map/all_gather | solution.py:1248
  359.6 22.4 %collective-permute-done.38.refs_2_ = bf16[256,2048]{1,0:T(8,128)(2,1)S(1)} collective-permute-done((bf16[256,2048]{1,0:T(8,128)(2,1)}, bf16[256,2048]{1,0:T(8,128)(2,1)S(1)}, u32[]{:S(2)}, u32[]{:S(2)}) %collective-permute-start.38) | collective-permute-done | bytes 1048608 | tf_op jit(solution)/shard_map/ppermute | solution.py:62
  390.0 21.0 %collective-permute-done.40.refs_1_.refs_2_ = bf16[256,2048]{1,0:T(8,128)(2,1)S(1)} collective-permute-done((bf16[256,2048]{1,0:T(8,128)(2,1)}, bf16[256,2048]{1,0:T(8,128)(2,1)S(1)}, u32[]{:S(2)}, u32[]{:S(2)}) %collective-permute-start.40) | collective-permute-done | bytes 1048608 | tf_op jit(solution)/shard_map/ppermute | solution.py:62
  414.0 9.2 collective-permute-done.42.refs_3_.refs_4_
  426.9 8.5 all-gather.15.cloned.1.call-done
  436.4 21.2 %feed.1 = (bf16[2048,512]{1,0:T(8,128)(2,1)}, bf16[2048,1024]{1,0:T(8,128)(2,1)}) custom-call(bf16[256,2048]{1,0:T(8,128)(2,1)} %get-tuple-element.237.refs_0_.refs_1_, bf16[256,2048]{1,0:T(8,128)(2,1)} %copy-done.16, bf16[256,2048]{1,0:T(8,128)(2,1)} %copy-done.18, bf16[128,2048]{1,0:T(8,128)(2,1)} %collective-permute-done.42.refs_3_.refs_4_, ...), custom_call_target="tpu_custom_call" | custom-call | bytes 25300000 | tf_op jit(solution)/shard_map/feed/pallas_call | solution.py:1172
  492.1 9.9 %weight_grad.6 = bf16[512,2048]{1,0:T(8,128)(2,1)} custom-call(bf16[512,2048]{1,0:T(8,128)(2,1)} %bitcast.292, bf16[256,2048]{1,0:T(8,128)(2,1)} %bitcast.284, bf16[256,2048]{1,0:T(8,128)(2,1)} %collective-permute-done.2.refs_11_.refs_2_, bf16[256,2048]{1,0:T(8,128)(2,1)} %collective-permute-done.3.refs_12_.refs_3_, ...), custom_call_target="tpu_custom_call" | custom-call | bytes 10032000 | tf_op jit(solution)/shard_map/weight_grad/pallas_call | solution.py:908
  513.3 15.8 %weight_grad.7 = bf16[4,1024,512]{2,1,0:T(8,128)(2,1)} custom-call(bf16[1024,2048]{1,0:T(8,128)(2,1)} %bitcast.275, bf16[256,2048]{1,0:T(8,128)(2,1)} %get-tuple-element.237.refs_0_.refs_1_, bf16[256,2048]{1,0:T(8,128)(2,1)} %copy-done.16, bf16[256,2048]{1,0:T(8,128)(2,1)} %copy-done.18, bf16[128,2048]{1,0:T(8,128)(2,1)} %collective-permute-done.42.refs_3_.refs_4_, ...), custom_call_target="tpu_custom_call" | custom-call | bytes 15664000 | tf_op jit(solution)/shard_map/weight_grad/pallas_call | solution.py:908
  584.4 15.6 %mixer_back.1 = (f32[8,256,384]{2,1,0:T(8,128)}, bf16[8,256,128]{2,1,0:T(8,128)(2,1)}, f32[8,8,256]{2,1,0:T(8,128)}) custom-call(bf16[256,2048]{1,0:T(8,128)(2,1)} %get-tuple-element.269.refs_0_.refs_1_, bf16[256,2048]{1,0:T(8,128)(2,1)} %copy-done.17, bf16[256,2048]{1,0:T(8,128)(2,1)} %collective-permute-done.58.refs_2_.refs_3_, ...), custom_call_target="tpu_custom_call" | custom-call | bytes 14300000 | tf_op jit(solution)/shard_map/mixer_back/pallas_call | solution.py:872
  605.2 10.0 %weight_grad.8 = bf16[512,2048]{1,0:T(8,128)(2,1)} custom-call(bf16[512,2048]{1,0:T(8,128)(2,1)} %maximum_bitcast_fusion.refs_0_, bf16[256,2048]{1,0:T(8,128)(2,1)} %get-tuple-element.269.refs_0_.refs_1_, bf16[256,2048]{1,0:T(8,128)(2,1)} %copy-done.17, bf16[256,2048]{1,0:T(8,128)(2,1)} %collective-permute-done.58.refs_2_.refs_3_, ...), custom_call_target="tpu_custom_call" | custom-call | bytes 10032000 | tf_op jit(solution)/shard_map/weight_grad/pallas_call | solution.py:908
  622.4 14.1 %gate_back.1 = (bf16[8,256,384]{2,1,0:T(8,128)(2,1)}, bf16[8,256,384]{2,1,0:T(8,128)(2,1)}, f32[4,384,256]{2,1,0:T(8,128)}, f32[4,384,256]{2,1,0:T(8,128)}) custom-call(s32[3]{0:T(128)} %pad_add_fusion.1.where, f32[8,256,384]{2,1,0:T(8,128)} %get-tuple-element.293.es, f32[8,256,8]{2,1,0:T(8,128)} %pad.41.scale, f32[8,256,384]{2,1,0:T(8,128)} %times.3.gating.refs_13_, ...), custom_call_target="tpu_custom_call" | custom-call | bytes 12100000 | tf_op jit(solution)/shard_map/gate_back/pallas_call | solution.py:607
  651.8 8.6 weight_grad.9
  668.8 18.0 %attend_back.1 = (f32[2,4,256,128]{3,2,1,0:T(8,128)}, bf16[4,4,512,256]{3,2,1,0:T(8,128)(2,1)}) custom-call(s32[3]{0:T(128)} %pad_add_fusion.1.where, bf16[2,4,256,128]{3,2,1,0:T(8,128)(2,1)} %get-tuple-element.214.query, bf16[4,2,512,256]{3,2,1,0:T(8,128)(2,1)} %all-gather.9.cloned.1.call-done.kv_own, ...), custom_call_target="tpu_custom_call" | custom-call | bytes 15400000 | tf_op jit(solution)/shard_map/attend_back/pallas_call | solution.py:548
  686.9 27.4 %collective-permute-done.79 = bf16[4,384,256]{2,1,0:T(8,128)(2,1)S(1)} collective-permute-done((bf16[4,384,256]{2,1,0:T(8,128)(2,1)S(1)}, bf16[4,384,256]{2,1,0:T(8,128)(2,1)S(1)}, u32[]{:S(2)}, u32[]{:S(2)}) %collective-permute-start.79) | collective-permute-done | bytes 786464 | tf_op jit(solution)/shard_map/ppermute | solution.py:1501
  725.5 39.5 %ssm_back.1 = (f32[8,256,384]{2,1,0:T(8,128)}, bf16[4,256,128]{2,1,0:T(8,128)(2,1)}, bf16[4,256,128]{2,1,0:T(8,128)(2,1)}, bf16[4,256,128]{2,1,0:T(8,128)(2,1)},...) custom-call(s32[3]{0:T(128)} %pad_add_fusion.1.where, ...), custom_call_target="tpu_custom_call" | custom-call | bytes 33000000 | tf_op jit(solution)/shard_map/ssm_back/pallas_call | solution.py:721
  779.5 8.7 weight_grad.10
  817.0 11.2 %conv_backward.1 = (bf16[8,256,512]{2,1,0:T(8,128)(2,1)}, f32[8,8,512]{2,1,0:T(8,128)}) custom-call(f32[8,256,384]{2,1,0:T(8,128)} %get-tuple-element.324.grad_xs, f32[4,256,128]{2,1,0:T(8,128)} %copy-done.24, f32[8,256,8]{2,1,0:T(8,128)} %get-tuple-element.333.step, f32[8,256,512]{2,1,0:T(8,128)} %get-tuple-element.334.slope, ...), custom_call_target="tpu_custom_call" | custom-call | bytes 6600000 | tf_op jit(solution)/shard_map/conv_backward/pallas_call | solution.py:789
  832.2 9.8 %weight_grad.11 = bf16[4,512,512]{2,1,0:T(8,128)(2,1)} custom-call(bf16[512,2048]{1,0:T(8,128)(2,1)} %copy.304.refs_0_, bf16[256,2048]{1,0:T(8,128)(2,1)} %norm_in.1.refs_0_.refs_1_, bf16[256,2048]{1,0:T(8,128)(2,1)} %copy-done.5, bf16[256,2048]{1,0:T(8,128)(2,1)} %copy-done.6, bf16[128,2048]{1,0:T(8,128)(2,1)} %collective-permute-done.4.refs_3_.refs_4_, ...), custom_call_target="tpu_custom_call" | custom-call | bytes 10032000 | tf_op jit(solution)/shard_map/weight_grad/pallas_call | solution.py:908
  860.6 8.7 group_terms.28
  899.9 9.5 group_terms.29
  943.1 8.9 all-to-all-done.3
  (706 shorter events, 477.1 us)
Async XLA Ops:
  7.2 98.8 %all-gather.7.cloned.1.call-start = ((), (), s32[]{:S(2)}) async-start(), calls=%async_computation.11 | async-start | bytes 4587520 | tf_op jit(solution)/shard_map/all_gather | solution.py:1248
  66.2 135.2 %all-gather.9.cloned.1.call-start = ((), (), s32[]{:S(2)}) async-start(), calls=%async_computation.12 | async-start | bytes 2621440 | tf_op jit(solution)/shard_map/all_gather | solution.py:1248
  66.9 29.8 %collective-permute-start.7 = (bf16[256,2048]{1,0:T(8,128)(2,1)S(1)}, bf16[256,2048]{1,0:T(8,128)(2,1)}, u32[]{:S(2)}, u32[]{:S(2)}) collective-permute-start(bf16[256,2048]{1,0:T(8,128)(2,1)S(1)} %collective-permute-done.refs_1_.refs_2_), channel_id=1, source_target_pairs={{0,1},{1,0},{2,3},{3,2},{4,5},{5,4},{6,7},{7,6},{8,9},{9,8},{10,11... | collective-permute-start | bytes 3145736 | tf_op jit(solution)/shard_map/ppermute | solution.py:66
  67.9 28.2 %collective-permute-start.4 = (bf16[128,2048]{1,0:T(8,128)(2,1)}, bf16[128,2048]{1,0:T(8,128)(2,1)}, u32[]{:S(2)}, u32[]{:S(2)}) collective-permute-start(bf16[128,2048]{1,0:T(8,128)(2,1)} %slice.304), channel_id=1, source_target_pairs={{0,16},{8,24},{16,0},{24,8},{1,17},{9,25},{17,1},{25,9},{2,18},{10... | collective-permute-start | bytes 1572872 | tf_op jit(solution)/shard_map/ppermute | solution.py:62
  72.1 33.9 %collective-permute-start.8 = (bf16[256,2048]{1,0:T(8,128)(2,1)S(1)}, bf16[256,2048]{1,0:T(8,128)(2,1)}, u32[]{:S(2)}, u32[]{:S(2)}) collective-permute-start(bf16[256,2048]{1,0:T(8,128)(2,1)S(1)} %collective-permute-done.1.refs_2_.refs_3_), channel_id=1, source_target_pairs={{0,1},{1,0},{2,3},{3,2},{4,5},{5,4},{6,7},{7,6},{8,9},{9,8},{10,11... | collective-permute-start | bytes 3145736 | tf_op jit(solution)/shard_map/ppermute | solution.py:66
  86.4 37.2 %collective-permute-start.2 = (bf16[256,2048]{1,0:T(8,128)(2,1)}, bf16[256,2048]{1,0:T(8,128)(2,1)}, u32[]{:S(2)}, u32[]{:S(2)}) collective-permute-start(bf16[256,2048]{1,0:T(8,128)(2,1)} %bitcast.281), channel_id=1, source_target_pairs={{0,8},{8,0},{16,24},{24,16},{1,9},{9,1},{17,25},{25,17},{2,10},{10... | collective-permute-start | bytes 3145736 | tf_op jit(solution)/shard_map/ppermute | solution.py:62
  96.1 27.5 %collective-permute-start.3 = (bf16[256,2048]{1,0:T(8,128)(2,1)}, bf16[256,2048]{1,0:T(8,128)(2,1)}, u32[]{:S(2)}, u32[]{:S(2)}) collective-permute-start(bf16[256,2048]{1,0:T(8,128)(2,1)} %bitcast.282), channel_id=1, source_target_pairs={{0,16},{8,24},{16,0},{24,8},{1,17},{9,25},{17,1},{25,9},{2,18},{10... | collective-permute-start | bytes 3145736 | tf_op jit(solution)/shard_map/ppermute | solution.py:62
  133.0 98.6 %all-gather.11.cloned.1.call-start = ((), (), s32[]{:S(2)}) async-start(), calls=%async_computation.13 | async-start | bytes 1966080 | tf_op jit(solution)/shard_map/all_gather | solution.py:1248
  134.3 67.0 %collective-permute-start.19 = (bf16[256,2048]{1,0:T(8,128)(2,1)S(1)}, bf16[256,2048]{1,0:T(8,128)(2,1)}, u32[]{:S(2)}, u32[]{:S(2)}) collective-permute-start(bf16[256,2048]{1,0:T(8,128)(2,1)S(1)} %bitcast.286), channel_id=1, source_target_pairs={{0,1},{1,0},{2,3},{3,2},{4,5},{5,4},{6,7},{7,6},{8,9},{9,8},{10,11... | collective-permute-start | bytes 3145736 | tf_op jit(solution)/shard_map/ppermute | solution.py:66
  138.9 68.8 %collective-permute-start.20 = (bf16[256,2048]{1,0:T(8,128)(2,1)}, bf16[256,2048]{1,0:T(8,128)(2,1)}, u32[]{:S(2)}, u32[]{:S(2)}) collective-permute-start(bf16[256,2048]{1,0:T(8,128)(2,1)} %collective-permute-done.2.refs_11_.refs_2_), channel_id=1, source_target_pairs={{0,1},{1,0},{2,3},{3,2},{4,5},{5,4},{6,7},{7,6},{8,9},{9,8},{10,11... | collective-permute-start | bytes 3145736 | tf_op jit(solution)/shard_map/ppermute | solution.py:66
  150.5 157.9 %all-gather.13.cloned.1.call-start = ((), (), s32[]{:S(2)}) async-start(), calls=%async_computation.14 | async-start | bytes 2621440 | tf_op jit(solution)/shard_map/all_gather | solution.py:1248
  173.1 35.1 %collective-permute-start.21 = (bf16[256,2048]{1,0:T(8,128)(2,1)}, bf16[256,2048]{1,0:T(8,128)(2,1)}, u32[]{:S(2)}, u32[]{:S(2)}) collective-permute-start(bf16[256,2048]{1,0:T(8,128)(2,1)} %collective-permute-done.3.refs_12_.refs_3_), channel_id=1, source_target_pairs={{0,1},{1,0},{2,3},{3,2},{4,5},{5,4},{6,7},{7,6},{8,9},{9,8},{10,11... | collective-permute-start | bytes 3145736 | tf_op jit(solution)/shard_map/ppermute | solution.py:66
  201.4 39.9 %collective-permute-start.25 = (bf16[4,2,512,256]{3,2,1,0:T(8,128)(2,1)}, bf16[4,2,512,256]{3,2,1,0:T(8,128)(2,1)}, u32[]{:S(2)}, u32[]{:S(2)}) collective-permute-start(bf16[4,2,512,256]{3,2,1,0:T(8,128)(2,1)} %all-gather.9.cloned.1.call-done.kv_own), channel_id=1, source_target_pairs={{0,1},{1,0},{2,3},{3,2},{4,5},{5,4},{6,7},{7,6},{8,9},{9,8},{10,11... | collective-permute-start | bytes 6291464 | tf_op jit(solution)/shard_map/ppermute | solution.py:66
  229.8 28.1 %collective-permute-start.24 = (bf16[4,384,256]{2,1,0:T(8,128)(2,1)}, bf16[4,384,256]{2,1,0:T(8,128)(2,1)S(1)}, u32[]{:S(2)}, u32[]{:S(2)}) collective-permute-start(bf16[4,384,256]{2,1,0:T(8,128)(2,1)} %fusion.1), channel_id=1, source_target_pairs={{2,4},{3,5},{10,12},{11,13},{18,20},{19,21},{26,28},{27,29}} | collective-permute-start | bytes 2359304 | tf_op jit(solution)/shard_map/ppermute | solution.py:1402
  259.1 167.8 %all-gather.17.cloned.1.call-start = ((), (), s32[]{:S(2)}) async-start(), calls=%async_computation.16 | async-start | bytes 2621440 | tf_op jit(solution)/shard_map/all_gather | solution.py:1248
  263.6 171.9 %all-gather.15.cloned.1.call-start = ((), (), s32[]{:S(2)}) async-start(), calls=%async_computation.15 | async-start | bytes 5242880 | tf_op jit(solution)/shard_map/all_gather | solution.py:1248
  287.1 376.7 %reduce-scatter.8.cloned.1.call-start = ((), (), s32[]{:S(2)}) async-start(), calls=%async_computation.17 | async-start | bytes 5242880 | tf_op jit(solution)/shard_map/reduce_scatter | solution.py:1244
  390.0 45.4 %collective-permute-start.44 = (bf16[256,2048]{1,0:T(8,128)(2,1)}, bf16[256,2048]{1,0:T(8,128)(2,1)S(1)}, u32[]{:S(2)}, u32[]{:S(2)}) collective-permute-start(bf16[256,2048]{1,0:T(8,128)(2,1)} %get-tuple-element.237.refs_0_.refs_1_), channel_id=1, source_target_pairs={{0,1},{1,0},{2,3},{3,2},{4,5},{5,4},{6,7},{7,6},{8,9},{9,8},{10,11... | collective-permute-start | bytes 3145736 | tf_op jit(solution)/shard_map/ppermute | solution.py:66
  531.8 134.3 %reduce-scatter.10.cloned.1.call-start = ((), (), s32[]{:S(2)}) async-start(), calls=%async_computation.18 | async-start | bytes 2621440 | tf_op jit(solution)/shard_map/reduce_scatter | solution.py:1251
  601.4 166.1 %reduce-scatter.12.cloned.1.call-start = ((), (), s32[]{:S(2)}) async-start(), calls=%async_computation.19 | async-start | bytes 2621440 | tf_op jit(solution)/shard_map/reduce_scatter | solution.py:1251
  648.5 38.4 %collective-permute-start.80 = (bf16[256,2048]{1,0:T(8,128)(2,1)}, bf16[256,2048]{1,0:T(8,128)(2,1)}, u32[]{:S(2)}, u32[]{:S(2)}) collective-permute-start(bf16[256,2048]{1,0:T(8,128)(2,1)} %get-tuple-element.304), channel_id=1, source_target_pairs={{0,8},{8,0},{16,24},{24,16},{1,9},{9,1},{17,25},{25,17},{2,10},{10... | collective-permute-start | bytes 3145736 | tf_op jit(solution)/shard_map/ppermute | solution.py:62
  649.5 37.4 %collective-permute-start.81 = (bf16[256,2048]{1,0:T(8,128)(2,1)}, bf16[256,2048]{1,0:T(8,128)(2,1)}, u32[]{:S(2)}, u32[]{:S(2)}) collective-permute-start(bf16[256,2048]{1,0:T(8,128)(2,1)} %get-tuple-element.318), channel_id=1, source_target_pairs={{0,16},{8,24},{16,0},{24,8},{1,17},{9,25},{17,1},{25,9},{2,18},{10... | collective-permute-start | bytes 3145736 | tf_op jit(solution)/shard_map/ppermute | solution.py:62
  667.5 46.8 %collective-permute-start.79 = (bf16[4,384,256]{2,1,0:T(8,128)(2,1)S(1)}, bf16[4,384,256]{2,1,0:T(8,128)(2,1)S(1)}, u32[]{:S(2)}, u32[]{:S(2)}) collective-permute-start(bf16[4,384,256]{2,1,0:T(8,128)(2,1)S(1)} %add_convert_fusion.2), channel_id=1, source_target_pairs={{2,0},{3,1},{10,8},{11,9},{18,16},{19,17},{26,24},{27,25}} | collective-permute-start | bytes 2359304 | tf_op jit(solution)/shard_map/ppermute | solution.py:1501
  722.3 157.6 %reduce-scatter.18.cloned.1.call-start = ((), (), s32[]{:S(2)}) async-start(), calls=%async_computation.22 | async-start | bytes 1966080 | tf_op jit(solution)/shard_map/reduce_scatter | solution.py:1244
  722.9 199.1 %reduce-scatter.16.cloned.1.call-start = ((), (), s32[]{:S(2)}) async-start(), calls=%async_computation.21 | async-start | bytes 1966080 | tf_op jit(solution)/shard_map/reduce_scatter | solution.py:1244
  800.4 122.7 %reduce-scatter.14.cloned.1.call-start = ((), (), s32[]{:S(2)}) async-start(), calls=%async_computation.20 | async-start | bytes 2621440 | tf_op jit(solution)/shard_map/reduce_scatter | solution.py:1244
  842.0 91.9 %reduce-scatter.20.cloned.1.call-start = ((), (), s32[]{:S(2)}) async-start(), calls=%async_computation.23 | async-start | bytes 2621440 | tf_op jit(solution)/shard_map/reduce_scatter | solution.py:1251
  869.3 30.6 %collective-permute-start.88 = (bf16[256,2048]{1,0:T(8,128)(2,1)}, bf16[256,2048]{1,0:T(8,128)(2,1)}, u32[]{:S(2)}, u32[]{:S(2)}) collective-permute-start(bf16[256,2048]{1,0:T(8,128)(2,1)} %get-tuple-element.341), channel_id=1, source_target_pairs={{0,1},{1,0},{2,3},{3,2},{4,5},{5,4},{6,7},{7,6},{8,9},{9,8},{10,11... | collective-permute-start | bytes 3145736 | tf_op jit(solution)/shard_map/ppermute | solution.py:66
  869.3 30.6 %collective-permute-start.89 = (bf16[256,2048]{1,0:T(8,128)(2,1)}, bf16[256,2048]{1,0:T(8,128)(2,1)}, u32[]{:S(2)}, u32[]{:S(2)}) collective-permute-start(bf16[256,2048]{1,0:T(8,128)(2,1)} %get-tuple-element.342), channel_id=1, source_target_pairs={{0,1},{1,0},{2,3},{3,2},{4,5},{5,4},{6,7},{7,6},{8,9},{9,8},{10,11... | collective-permute-start | bytes 3145736 | tf_op jit(solution)/shard_map/ppermute | solution.py:66
  869.8 30.1 %collective-permute-start.90 = (bf16[256,2048]{1,0:T(8,128)(2,1)}, bf16[256,2048]{1,0:T(8,128)(2,1)}, u32[]{:S(2)}, u32[]{:S(2)}) collective-permute-start(bf16[256,2048]{1,0:T(8,128)(2,1)} %get-tuple-element.343), channel_id=1, source_target_pairs={{0,1},{1,0},{2,3},{3,2},{4,5},{5,4},{6,7},{7,6},{8,9},{9,8},{10,11... | collective-permute-start | bytes 3145736 | tf_op jit(solution)/shard_map/ppermute | solution.py:66
  913.3 26.3 %collective-permute-start.101 = (bf16[256,2048]{1,0:T(8,128)(2,1)}, bf16[256,2048]{1,0:T(8,128)(2,1)S(1)}, u32[]{:S(2)}, u32[]{:S(2)}) collective-permute-start(bf16[256,2048]{1,0:T(8,128)(2,1)} %get-tuple-element.353), channel_id=1, source_target_pairs={{0,8},{8,0},{16,24},{24,16},{1,9},{9,1},{17,25},{25,17},{2,10},{10... | collective-permute-start | bytes 3145736 | tf_op jit(solution)/shard_map/ppermute | solution.py:62
  914.9 28.2 %collective-permute-start.102 = (bf16[256,2048]{1,0:T(8,128)(2,1)}, bf16[256,2048]{1,0:T(8,128)(2,1)}, u32[]{:S(2)}, u32[]{:S(2)}) collective-permute-start(bf16[256,2048]{1,0:T(8,128)(2,1)} %get-tuple-element.354), channel_id=1, source_target_pairs={{0,16},{8,24},{16,0},{24,8},{1,17},{9,25},{17,1},{25,9},{2,18},{10... | collective-permute-start | bytes 3145736 | tf_op jit(solution)/shard_map/ppermute | solution.py:62
  (183 other events, 1871.3 us)
Sparse Core Ops, SparseCore 0:
  34.5 71.4 all-gather.6
  133.1 44.5 all-gather.8
  179.3 36.4 all-gather.10
  259.2 49.1 all-gather.12
  309.8 44.6 all-gather.16
  356.0 79.4 all-gather.14
  530.8 74.3 reduce-scatter.7
  607.6 52.6 reduce-scatter.9
  722.4 45.0 reduce-scatter.11
  769.8 34.5 reduce-scatter.17
  806.8 34.5 reduce-scatter.15
  843.7 44.7 reduce-scatter.13
  890.8 43.0 reduce-scatter.19
